TPU v7x, 128 devices: a whole 4x4x4 slice. The times are simulated.
128 devices in a mesh: ctx: 16 (over z_lo, x, core), fsdp: 8 (over z_hi, y).
Axes of the slice: x: 4, y: 4, z: 4 (z_hi: 2, z_lo: 2; z = z_hi * 2 + z_lo), core: 2. Of those that a mesh axis runs over, the one named last changes fastest.
Arguments:
- tokens: bfloat16 [8, 2048, 2048], P('fsdp', 'ctx'), may hold values from -6 to 6
- cotangent: bfloat16 [8, 2048, 2048], P('fsdp', 'ctx'), may hold values from -6 to 6
- attn_gain: float32 [2048], replicated, may hold values from 0.5 to 1.5
- q_weight: bfloat16 [2048, 2048], P(None, 'fsdp'), may hold values from -0.125 to 0.125
- k_weight: bfloat16 [2048, 1024], P(None, 'fsdp'), may hold values from -0.125 to 0.125
- v_weight: bfloat16 [2048, 1024], P(None, 'fsdp'), may hold values from -0.125 to 0.125
- q_gain: float32 [128], replicated, may hold values from 0.5 to 1.5
- k_gain: float32 [128], replicated, may hold values from 0.5 to 1.5
- o_weight: bfloat16 [2048, 2048], P('fsdp'), may hold values from -2 to 2
- mlp_gain: float32 [2048], replicated, may hold values from 0.5 to 1.5
- gate_weight: bfloat16 [2048, 6144], P(None, 'fsdp'), may hold values from -0.125 to 0.125
- up_weight: bfloat16 [2048, 6144], P(None, 'fsdp'), may hold values from -0.125 to 0.125
- down_weight: bfloat16 [6144, 2048], P('fsdp'), may hold values from -0.078125 to 0.078125
- doc_lengths: int32 [8, 4], replicated, may hold values from 1 to 1984, 2048 in all within a row
- block_place: int32 [32], replicated, may hold values from 0 to 31, as said below
Outputs:
- out_rows: bfloat16 [8, 2048, 2048], P('fsdp', 'ctx')
- tokens_grad: bfloat16 [8, 2048, 2048], P('fsdp', 'ctx')
- attn_gain_grad: float32 [2048], replicated
- q_weight_grad: float32 [2048, 2048], P('ctx', 'fsdp')
- k_weight_grad: float32 [2048, 1024], P('ctx', 'fsdp')
- v_weight_grad: float32 [2048, 1024], P('ctx', 'fsdp')
- q_gain_grad: float32 [128], replicated
- k_gain_grad: float32 [128], replicated
- o_weight_grad: float32 [2048, 2048], P('fsdp', 'ctx')
- mlp_gain_grad: float32 [2048], replicated
- gate_weight_grad: float32 [2048, 6144], P('ctx', 'fsdp')
- up_weight_grad: float32 [2048, 6144], P('ctx', 'fsdp')
- down_weight_grad: float32 [6144, 2048], P('fsdp', 'ctx')
Inputs may be any that keep to these rules, and one draw needn't show every extreme that they name: `block_place`: stored blocks 2 j and 2 j + 1 hold blocks b and 31 - b of the sequence, in either order; each block is held once. `doc_lengths`: each row sums to 2048; one document of each row has exactly 1984 tokens.
All inputs are finite; a program needn't handle non-finite values.
Results may differ from a plain program's by a relative error of at most 0.028.
Values may be sent and summed in bfloat16 or wider, within the bound.
A program may use at most 192 MiB of HBM per device.

v0:
```python
import jax
import jax.numpy as jnp
from jax import lax
from jax.sharding import PartitionSpec as P

EPSILON = 1e-06
ROPE_BASE = 1000000.0
MASKED_SCORE = -1e30


def rms_scale(values, gain_vec):
    inverse = lax.rsqrt(jnp.mean(values * values, axis=-1, keepdims=True) + EPSILON)
    return values * inverse * gain_vec


def head_prep(values, gain_vec, cos_table, sin_table):
    scaled = rms_scale(values, gain_vec)
    midway = scaled.shape[-1] // 2
    turned = jnp.concatenate([-scaled[..., midway:], scaled[..., :midway]], axis=-1)
    return scaled * cos_table + turned * sin_table


def tables(positions, head_dim):
    exponent_steps = jnp.arange(head_dim // 2, dtype=jnp.int32).astype(jnp.float32) * (
        2.0 / head_dim
    )
    frequency = ROPE_BASE ** (-exponent_steps)
    phases = positions.astype(jnp.float32)[:, None] * frequency[None, :]
    phases = jnp.concatenate([phases, phases], axis=-1)
    return (jnp.cos(phases), jnp.sin(phases))


def stored_positions(block_place, block_width):
    return (
        block_place[:, None] * block_width + jnp.arange(block_width, dtype=jnp.int32)[None, :]
    ).reshape(-1)


def document_ids(positions, doc_lengths):
    ends = jnp.cumsum(doc_lengths, axis=-1, dtype=jnp.int32)
    return jnp.sum(
        (positions[None, :, None] >= ends[:, None, :]).astype(jnp.int32), axis=-1, dtype=jnp.int32
    )


def per_device(
    tokens,
    cotangent,
    attn_gain,
    q_weight,
    k_weight,
    v_weight,
    q_gain,
    k_gain,
    o_weight,
    mlp_gain,
    gate_weight,
    up_weight,
    down_weight,
    doc_lengths,
    block_place,
):
    ctx_place = lax.axis_index("ctx")
    local_rows = tokens.shape[1]
    block_width = local_rows // 2
    head_dim = q_gain.shape[0]
    heads_local = q_weight.shape[1] // head_dim
    groups_local = k_weight.shape[1] // head_dim
    per_group = heads_local // groups_local
    score_scale = head_dim ** (-0.5)
    positions = stored_positions(block_place, block_width)
    documents = document_ids(positions, doc_lengths)
    own_positions = lax.dynamic_slice_in_dim(positions, ctx_place * local_rows, local_rows)
    own_documents = lax.dynamic_slice_in_dim(documents, ctx_place * local_rows, local_rows, 1)
    allowed = (positions[None, None, :] <= own_positions[None, :, None]) & (
        documents[:, None, :] == own_documents[:, :, None]
    )
    allowed = allowed[:, None, None, :, :]
    cos_rows, sin_rows = tables(own_positions, head_dim)
    cos_rows = cos_rows[None, :, None, :]
    sin_rows = sin_rows[None, :, None, :]
    residual = tokens[0].astype(jnp.float32)
    normed = rms_scale(residual, attn_gain).astype(jnp.bfloat16)
    normed_all = lax.all_gather(normed[None], "fsdp", axis=0, tiled=True)
    seq_count = normed_all.shape[0]
    q_raw = jnp.einsum(
        "srd,dc->src", normed_all, q_weight, preferred_element_type=jnp.float32
    ).reshape(seq_count, local_rows, heads_local, head_dim)
    k_raw = jnp.einsum(
        "srd,dc->src", normed_all, k_weight, preferred_element_type=jnp.float32
    ).reshape(seq_count, local_rows, groups_local, head_dim)
    v_act = (
        jnp.einsum("srd,dc->src", normed_all, v_weight, preferred_element_type=jnp.float32)
        .astype(jnp.bfloat16)
        .reshape(seq_count, local_rows, groups_local, head_dim)
    )
    q_act = (
        head_prep(q_raw, q_gain, cos_rows, sin_rows)
        .astype(jnp.bfloat16)
        .reshape(seq_count, local_rows, groups_local, per_group, head_dim)
    )
    k_act = head_prep(k_raw, k_gain, cos_rows, sin_rows).astype(jnp.bfloat16)
    keys_all, values_all = (
        lax.all_gather(k_act, "ctx", axis=1, tiled=True),
        lax.all_gather(v_act, "ctx", axis=1, tiled=True),
    )

    def masked_scores(key_rows):
        scores = (
            jnp.einsum("srkgd,stkd->skgrt", q_act, key_rows, preferred_element_type=jnp.float32)
            * score_scale
        )
        return jnp.where(allowed, scores, MASKED_SCORE)

    scores = masked_scores(keys_all)
    row_top = jnp.max(scores, axis=-1, keepdims=True)
    exponent = jnp.exp(scores - row_top)
    totals = jnp.sum(exponent, axis=-1, keepdims=True)
    probabilities = exponent / totals
    log_total = row_top + jnp.log(totals)
    attended = jnp.einsum(
        "skgrt,stkd->srkgd",
        probabilities.astype(jnp.bfloat16),
        values_all,
        preferred_element_type=jnp.float32,
    )
    attended = attended.astype(jnp.bfloat16).reshape(seq_count, local_rows, heads_local * head_dim)
    selected = attended
    attn_out = lax.psum_scatter(
        jnp.einsum("src,cd->srd", selected, o_weight, preferred_element_type=jnp.float32).astype(
            jnp.bfloat16
        ),
        "fsdp",
        scatter_dimension=0,
        tiled=True,
    ).astype(jnp.float32)
    middle = residual + attn_out[0]
    hidden = rms_scale(middle, mlp_gain).astype(jnp.bfloat16)
    hidden_all = lax.all_gather(hidden[None], "fsdp", axis=0, tiled=True)
    gate_pre = jnp.einsum(
        "srd,df->srf", hidden_all, gate_weight, preferred_element_type=jnp.float32
    )
    up_pre = jnp.einsum("srd,df->srf", hidden_all, up_weight, preferred_element_type=jnp.float32)
    activation = (jax.nn.silu(gate_pre) * up_pre).astype(jnp.bfloat16)
    selected = activation
    mlp_out = lax.psum_scatter(
        jnp.einsum("srf,fd->srd", selected, down_weight, preferred_element_type=jnp.float32).astype(
            jnp.bfloat16
        ),
        "fsdp",
        scatter_dimension=0,
        tiled=True,
    ).astype(jnp.float32)
    out_rows = (middle + mlp_out[0]).astype(jnp.bfloat16)[None]
    cot_all = lax.all_gather(cotangent, "fsdp", axis=0, tiled=True)
    act_grad = jnp.einsum("srd,fd->srf", cot_all, down_weight, preferred_element_type=jnp.float32)
    _, silu_back = jax.vjp(lambda gate_in, up_in: jax.nn.silu(gate_in) * up_in, gate_pre, up_pre)
    gate_grad, up_grad = silu_back(act_grad)
    gate_grad = gate_grad.astype(jnp.bfloat16)
    up_grad = up_grad.astype(jnp.bfloat16)
    hidden_grad = lax.psum_scatter(
        (
            jnp.einsum("srf,df->srd", gate_grad, gate_weight, preferred_element_type=jnp.float32)
            + jnp.einsum("srf,df->srd", up_grad, up_weight, preferred_element_type=jnp.float32)
        ).astype(jnp.bfloat16),
        "fsdp",
        scatter_dimension=0,
        tiled=True,
    ).astype(jnp.float32)
    _, second_back = jax.vjp(rms_scale, middle, mlp_gain)
    middle_part, mlp_gain_grad = second_back(hidden_grad[0])
    middle_grad = cotangent[0].astype(jnp.float32) + middle_part
    branch_grad = middle_grad.astype(jnp.bfloat16)
    branch_all = lax.all_gather(branch_grad[None], "fsdp", axis=0, tiled=True)
    attended_grad = jnp.einsum(
        "srd,cd->src", branch_all, o_weight, preferred_element_type=jnp.float32
    )
    attended_grad = attended_grad.astype(jnp.bfloat16).reshape(
        seq_count, local_rows, groups_local, per_group, head_dim
    )
    keys_back, values_back = (keys_all, values_all)
    again_probs = jnp.exp(masked_scores(keys_back) - log_total)
    prob_grad = jnp.einsum(
        "srkgd,stkd->skgrt", attended_grad, values_back, preferred_element_type=jnp.float32
    )
    row_dot = jnp.sum(prob_grad * again_probs, axis=-1, keepdims=True)
    score_grad = (again_probs * (prob_grad - row_dot)).astype(jnp.bfloat16)
    query_grad = (
        jnp.einsum("skgrt,stkd->srkgd", score_grad, keys_back, preferred_element_type=jnp.float32)
        * score_scale
    )
    key_part = (
        jnp.einsum("skgrt,srkgd->stkd", score_grad, q_act, preferred_element_type=jnp.float32)
        * score_scale
    )
    value_part = jnp.einsum(
        "skgrt,srkgd->stkd",
        again_probs.astype(jnp.bfloat16),
        attended_grad,
        preferred_element_type=jnp.float32,
    )
    key_grad, value_grad = (
        lax.psum_scatter(
            key_part.astype(jnp.bfloat16), "ctx", scatter_dimension=1, tiled=True
        ).astype(jnp.float32),
        lax.psum_scatter(
            value_part.astype(jnp.bfloat16), "ctx", scatter_dimension=1, tiled=True
        ).astype(jnp.float32),
    )
    _, query_back = jax.vjp(
        lambda raw_rows, gain_vec: head_prep(raw_rows, gain_vec, cos_rows, sin_rows), q_raw, q_gain
    )
    q_raw_grad, q_gain_grad = query_back(
        query_grad.reshape(seq_count, local_rows, heads_local, head_dim)
    )
    _, key_back = jax.vjp(
        lambda raw_rows, gain_vec: head_prep(raw_rows, gain_vec, cos_rows, sin_rows), k_raw, k_gain
    )
    k_raw_grad, k_gain_grad = key_back(key_grad)
    q_low = q_raw_grad.astype(jnp.bfloat16).reshape(seq_count, local_rows, heads_local * head_dim)
    k_low = k_raw_grad.astype(jnp.bfloat16).reshape(seq_count, local_rows, groups_local * head_dim)
    v_low = value_grad.astype(jnp.bfloat16).reshape(seq_count, local_rows, groups_local * head_dim)
    total = jnp.einsum("src,dc->srd", q_low, q_weight, preferred_element_type=jnp.float32)
    total = total + jnp.einsum("src,dc->srd", k_low, k_weight, preferred_element_type=jnp.float32)
    normed_grad = lax.psum_scatter(
        (
            total + jnp.einsum("src,dc->srd", v_low, v_weight, preferred_element_type=jnp.float32)
        ).astype(jnp.bfloat16),
        "fsdp",
        scatter_dimension=0,
        tiled=True,
    ).astype(jnp.float32)
    _, first_back = jax.vjp(rms_scale, residual, attn_gain)
    residual_part, attn_gain_grad = first_back(normed_grad[0])
    tokens_grad = (middle_grad + residual_part).astype(jnp.bfloat16)[None]

    def contract(left_side, right_side):
        return jnp.einsum("src,srk->ck", left_side, right_side, preferred_element_type=jnp.float32)

    weight_grads = lax.psum_scatter(
        jnp.concatenate(
            [
                contract(normed_all, q_low),
                contract(normed_all, k_low),
                contract(normed_all, v_low),
                contract(branch_all, attended),
                contract(hidden_all, gate_grad),
                contract(hidden_all, up_grad),
                contract(cot_all, activation),
            ],
            axis=1,
        ).astype(jnp.bfloat16),
        "ctx",
        scatter_dimension=0,
        tiled=True,
    ).astype(jnp.float32)
    q_width = heads_local * head_dim
    k_width = groups_local * head_dim
    f_width = gate_weight.shape[1]
    edge_two = q_width + k_width
    edge_three = edge_two + k_width
    edge_four = edge_three + q_width
    edge_five = edge_four + f_width
    edge_six = edge_five + f_width
    q_weight_grad = weight_grads[:, :q_width]
    k_weight_grad = weight_grads[:, q_width:edge_two]
    v_weight_grad = weight_grads[:, edge_two:edge_three]
    o_weight_grad = weight_grads[:, edge_three:edge_four].T
    gate_weight_grad = weight_grads[:, edge_four:edge_five]
    up_weight_grad = weight_grads[:, edge_five:edge_six]
    down_weight_grad = weight_grads[:, edge_six:].T
    gain_totals = lax.psum(
        (attn_gain_grad, q_gain_grad, k_gain_grad, mlp_gain_grad), ("ctx", "fsdp")
    )
    return (
        out_rows,
        tokens_grad,
        gain_totals[0],
        q_weight_grad,
        k_weight_grad,
        v_weight_grad,
        gain_totals[1],
        gain_totals[2],
        o_weight_grad,
        gain_totals[3],
        gate_weight_grad,
        up_weight_grad,
        down_weight_grad,
    )


def solution(mesh):
    in_specs = (
        P("fsdp", "ctx", None),
        P("fsdp", "ctx", None),
        P(),
        P(None, "fsdp"),
        P(None, "fsdp"),
        P(None, "fsdp"),
        P(),
        P(),
        P("fsdp", None),
        P(),
        P(None, "fsdp"),
        P(None, "fsdp"),
        P("fsdp", None),
        P(),
        P(),
    )
    out_specs = (
        P("fsdp", "ctx", None),
        P("fsdp", "ctx", None),
        P(),
        P("ctx", "fsdp"),
        P("ctx", "fsdp"),
        P("ctx", "fsdp"),
        P(),
        P(),
        P("fsdp", "ctx"),
        P(),
        P("ctx", "fsdp"),
        P("ctx", "fsdp"),
        P("fsdp", "ctx"),
    )
    return jax.shard_map(
        per_device, mesh=mesh, in_specs=in_specs, out_specs=out_specs, check_vma=False
    )
```

profile of v0, /device:TPU:0, one launch (start us, length us, event | category | flops | bytes accessed | tf_op | source)
XLA Modules:
  0.0 1073.0 jit_solution(10052089340612364434)
XLA Ops:
  13.0 73.0 %all-gather.9.cloned.1.call-done = bf16[8,128,2048]{2,1,0:T(8,128)(2,1)} async-done(((bf16[1,128,2048]{2,1,0:T(8,128)(2,1)}), bf16[8,128,2048]{2,1,0:T(8,128)(2,1)}) %all-gather.9.cloned.1.call-update) | async-done | bytes 4194320 | tf_op jit(solution)/shard_map/all_gather | solution.py:84
  118.3 16.2 %all-gather.19.cloned.1.call-done = bf16[8,2048,128]{1,2,0:T(8,128)(2,1)} async-done(((bf16[8,128,128]{1,2,0:T(8,128)(2,1)}), bf16[8,2048,128]{1,2,0:T(8,128)(2,1)}) %all-gather.19.cloned.1.call-update) | async-done | bytes 4194320 | tf_op jit(solution)/shard_map/all_gather | solution.py:104
  134.4 12.1 %fusion.118 = (f32[8,2,128]{2,1,0:T(2,128)S(1)}, f32[8,1,2,128,2048]{3,4,2,0,1:T(8,128)}) fusion(bf16[8,128,2,128]{1,3,2,0:T(8,128)(2,1)} %fusion.81, bf16[8,2048,128]{1,2,0:T(8,128)(2,1)} %all-gather.19.cloned.1.call-done, pred[8,128,2048]{1,2,0:T(8,128)(4,1)} %compare_and_fusion), kind=kOutput, calls=%fused_computation.190 | convolution fusion | flops 1086322688 | bytes 23601152 | tf_op jit(solution)/shard_map/srkgd,stkd->skgrt/dot_general | solution.py:110
  146.5 8.2 fusion.3
  154.7 19.5 %all-gather.17.cloned.1.call-done = bf16[8,2048,128]{2,1,0:T(8,128)(2,1)} async-done(((bf16[8,128,128]{2,1,0:T(8,128)(2,1)}), bf16[8,2048,128]{2,1,0:T(8,128)(2,1)}) %all-gather.17.cloned.1.call-update) | async-done | bytes 4194320 | tf_op jit(solution)/shard_map/all_gather | solution.py:105
  174.2 10.4 fusion.61
  189.3 84.7 %reduce-scatter.14.cloned.1.call-done = bf16[1,128,2048]{2,1,0:T(8,128)(2,1)} async-done(((bf16[8,128,2048]{2,1,0:T(8,128)(2,1)}), bf16[1,128,2048]{2,1,0:T(8,128)(2,1)}) %reduce-scatter.14.cloned.1.call-update) | async-done | bytes 524304 | tf_op jit(solution)/shard_map/reduce_scatter | solution.py:129
  278.3 69.8 %all-gather.11.cloned.1.call-done = bf16[8,128,2048]{2,1,0:T(8,128)(2,1)} async-done(((bf16[1,128,2048]{2,1,0:T(8,128)(2,1)}), bf16[8,128,2048]{2,1,0:T(8,128)(2,1)}) %all-gather.11.cloned.1.call-update) | async-done | bytes 4194320 | tf_op jit(solution)/shard_map/all_gather | solution.py:139
  348.1 8.3 fusion.32
  361.5 58.2 %all-gather.13.cloned.1.call-done = bf16[8,128,2048]{2,1,0:T(8,128)(2,1)} async-done(((bf16[1,128,2048]{2,1,0:T(8,128)(2,1)}), bf16[8,128,2048]{2,1,0:T(8,128)(2,1)}) %all-gather.13.cloned.1.call-update) | async-done | bytes 4194320 | tf_op jit(solution)/shard_map/all_gather | solution.py:155
  419.6 9.8 multiply_convert_fusion
  438.2 82.8 %reduce-scatter.18.cloned.1.call-done = bf16[1,128,2048]{2,1,0:T(8,128)(2,1)} async-done(((bf16[8,128,2048]{2,1,0:T(8,128)(2,1)}), bf16[1,128,2048]{2,1,0:T(8,128)(2,1)}) %reduce-scatter.18.cloned.1.call-update) | async-done | bytes 524304 | tf_op jit(solution)/shard_map/reduce_scatter | solution.py:161
  526.4 70.3 %all-gather.15.cloned.1.call-done = bf16[8,128,2048]{2,1,0:T(8,128)(2,1)} async-done(((bf16[1,128,2048]{2,1,0:T(8,128)(2,1)}), bf16[8,128,2048]{2,1,0:T(8,128)(2,1)}) %all-gather.15.cloned.1.call-update) | async-done | bytes 4194320 | tf_op jit(solution)/shard_map/all_gather | solution.py:174
  603.3 15.8 %fusion = (f32[8,2,128]{2,1,0:T(2,128)S(1)}, f32[8,2048,128,2]{2,1,3,0:T(8,128)}) fusion(f32[8,1,2,128,2048]{3,4,2,0,1:T(8,128)} %get-tuple-element.115, f32[8,2,128]{2,1,0:T(2,128)S(1)} %bitcast.331, bf16[8,128,2,128]{1,3,2,0:T(8,128)(2,1)} %bitcast.321, bf16[8,2048,128]{2,1,0:T(8,128)(2,1)} %all-gather.17.cloned.1.call-done), kind=kOutput, calls=%fused_computation.3 | convolution fusion | flops 1086322688 | bytes 38289408 | tf_op jit(solution)/shard_map/srkgd,stkd->skgrt/dot_general | solution.py:183
  619.1 11.8 %fusion.8 = bf16[8,2,128,2048]{2,3,1,0:T(8,128)(2,1)S(1)} fusion(f32[8,2048,128,2]{2,1,3,0:T(8,128)} %get-tuple-element.117, f32[8,1,2,128,2048]{3,4,2,0,1:T(8,128)} %get-tuple-element.115, f32[8,2,128]{2,1,0:T(2,128)S(1)} %get-tuple-element.116, f32[8,2,128]{2,1,0:T(2,128)S(1)} %bitcast.332), kind=kLoop, calls=%fused_computation.13 | loop fusion | flops 16777216 | bytes 41959424 | tf_op jit(solution)/shard_map/reshape.43
  651.2 10.9 %fusion.13 = bf16[8,2048,1,128]{1,3,0,2:T(8,128)(2,1)} fusion(bf16[8,128,2,128]{1,3,2,0:T(8,128)(2,1)} %bitcast.322, f32[8,1,2,128,2048]{3,4,2,0,1:T(8,128)} %get-tuple-element.115, f32[8,2,128]{2,1,0:T(2,128)S(1)} %bitcast.333), kind=kOutput, calls=%fused_computation.27 | convolution fusion | flops 1084227584 | bytes 21504000 | tf_op jit(solution)/shard_map/skgrt,srkgd->stkd/dot_general | solution.py:196
  662.1 6.9 copy.196
  682.7 32.8 %reduce-scatter.22.cloned.1.call-done = bf16[128,1024]{1,0:T(8,128)(2,1)} async-done(((bf16[2048,1024]{1,0:T(8,128)(2,1)}), bf16[128,1024]{1,0:T(8,128)(2,1)}) %reduce-scatter.22.cloned.1.call-update) | async-done | bytes 262160
  721.7 61.6 %reduce-scatter.24.cloned.1.call-done = bf16[128,1024]{1,0:T(8,128)(2,1)} async-done(((bf16[2048,1024]{1,0:T(8,128)(2,1)}), bf16[128,1024]{1,0:T(8,128)(2,1)}) %reduce-scatter.24.cloned.1.call-update) | async-done | bytes 262160
  826.4 16.7 %copy.198 = bf16[2048,3072]{1,0:T(8,128)(2,1)} copy(bf16[2048,3072]{0,1:T(8,128)(2,1)} %bitcast_dynamic-update-slice_fusion) | data formatting | bytes 25165824
  843.2 34.1 %reduce-scatter.20.cloned.1.call-done = bf16[1,128,2048]{2,1,0:T(8,128)(2,1)} async-done(((bf16[8,128,2048]{2,1,0:T(8,128)(2,1)}), bf16[1,128,2048]{2,1,0:T(8,128)(2,1)}) %reduce-scatter.20.cloned.1.call-update) | async-done | bytes 524304 | tf_op jit(solution)/shard_map/reduce_scatter | solution.py:225
  879.1 72.4 %all-reduce.4 = (f32[2048]{0:T(1024)}, f32[128]{0:T(128)}, f32[128]{0:T(128)}, f32[2048]{0:T(1024)}) all-reduce(f32[2048]{0:T(1024)S(1)} %get-tuple-element.84, f32[128]{0:T(128)S(1)} %copy-done.25, f32[128]{0:T(128)S(1)} %get-tuple-element.82, f32[2048]{0:T(1024)S(1)} %copy-done.18), channel_id=1, replica_groups=mesh['ctx'=16,'fsdp'=8] {'ctx','fsdp'}, use_global_device_ids=true, to_apply=%region_20.21 | all-reduce | flops 4352 | bytes 34816 | tf_op jit(solution)/shard_map/psum | solution.py:272
  951.4 13.6 %reduce-scatter.16.cloned.1.call-done = bf16[1,128,2048]{2,1,0:T(8,128)(2,1)} async-done(((bf16[8,128,2048]{2,1,0:T(8,128)(2,1)}), bf16[1,128,2048]{2,1,0:T(8,128)(2,1)}) %reduce-scatter.16.cloned.1.call-update) | async-done | bytes 524304 | tf_op jit(solution)/shard_map/reduce_scatter | solution.py:146
  968.7 79.9 %reduce-scatter.26.cloned.1.call-done = bf16[128,3072]{1,0:T(8,128)(2,1)} async-done(((bf16[2048,3072]{1,0:T(8,128)(2,1)}), bf16[128,3072]{1,0:T(8,128)(2,1)}) %reduce-scatter.26.cloned.1.call-update) | async-done | bytes 786448
  (201 shorter events, 178.5 us)
Async XLA Ops:
  7.2 412.5 %copy-start = (bf16[768,2048]{1,0:T(8,128)(2,1)S(1)}, bf16[768,2048]{1,0:T(8,128)(2,1)}, u32[]{:S(2)}) copy-start(bf16[768,2048]{1,0:T(8,128)(2,1)} %param.27) | copy-start | bytes 9437188
  7.2 82.7 %copy-start.19 = (f32[128]{0:T(128)S(1)}, f32[128]{0:T(128)}, u32[]{:S(2)}) copy-start(f32[128]{0:T(128)} %param.22) | copy-start | bytes 1540
  7.2 78.8 %all-gather.9.cloned.1.call-start = ((), (), s32[]{:S(2)}) async-start(), calls=%async_computation.7 | async-start | bytes 4718592 | tf_op jit(solution)/shard_map/all_gather | solution.py:84
  11.7 122.7 %all-gather.19.cloned.1.call-start = ((), (), s32[]{:S(2)}) async-start(), calls=%async_computation.16 | async-start | bytes 4456448 | tf_op jit(solution)/shard_map/all_gather | solution.py:104
  91.6 82.6 %all-gather.17.cloned.1.call-start = ((), (), s32[]{:S(2)}) async-start(), calls=%async_computation.15 | async-start | bytes 4456448 | tf_op jit(solution)/shard_map/all_gather | solution.py:105
  95.9 178.1 %reduce-scatter.14.cloned.1.call-start = ((), (), s32[]{:S(2)}) async-start(), calls=%async_computation.8 | async-start | bytes 4718592 | tf_op jit(solution)/shard_map/reduce_scatter | solution.py:129
  185.4 90.0 %copy-start.14 = (f32[2048]{0:T(1024)S(1)}, f32[2048]{0:T(1024)}, u32[]{:S(2)}) copy-start(f32[2048]{0:T(1024)} %param.24) | copy-start | bytes 24580
  188.8 159.3 %all-gather.11.cloned.1.call-start = ((), (), s32[]{:S(2)}) async-start(), calls=%async_computation.9 | async-start | bytes 4718592 | tf_op jit(solution)/shard_map/all_gather | solution.py:139
  275.5 248.0 %copy-start.21 = (f32[128]{0:T(128)}, f32[128]{0:T(128)S(1)}, u32[]{:S(2)}) copy-start(f32[128]{0:T(128)S(1)} %fusion.111) | copy-start | bytes 1540
  277.7 141.9 %all-gather.13.cloned.1.call-start = ((), (), s32[]{:S(2)}) async-start(), calls=%async_computation.11 | async-start | bytes 4718592 | tf_op jit(solution)/shard_map/all_gather | solution.py:155
  278.3 242.8 %reduce-scatter.18.cloned.1.call-start = ((), (), s32[]{:S(2)}) async-start(), calls=%async_computation.12 | async-start | bytes 4718592 | tf_op jit(solution)/shard_map/reduce_scatter | solution.py:161
  438.2 158.5 %all-gather.15.cloned.1.call-start = ((), (), s32[]{:S(2)}) async-start(), calls=%async_computation.13 | async-start | bytes 4718592 | tf_op jit(solution)/shard_map/all_gather | solution.py:174
  526.3 189.2 %reduce-scatter.22.cloned.1.call-start = ((), (), s32[]{:S(2)}) async-start(), calls=%async_computation.17 | async-start | bytes 4456448
  650.9 132.3 %reduce-scatter.24.cloned.1.call-start = ((), (), s32[]{:S(2)}) async-start(), calls=%async_computation.18 | async-start | bytes 4456448
  674.3 203.0 %reduce-scatter.20.cloned.1.call-start = ((), (), s32[]{:S(2)}) async-start(), calls=%async_computation.14 | async-start | bytes 4718592 | tf_op jit(solution)/shard_map/reduce_scatter | solution.py:225
  681.6 38.1 %copy-start.17 = (f32[8,128]{1,0:T(8,128)S(1)}, f32[8,128]{1,0:T(8,128)}, u32[]{:S(2)}) copy-start(f32[8,128]{1,0:T(8,128)} %copy-done.16) | copy-start | bytes 12292
  793.3 171.8 %reduce-scatter.16.cloned.1.call-start = ((), (), s32[]{:S(2)}) async-start(), calls=%async_computation.10 | async-start | bytes 4718592 | tf_op jit(solution)/shard_map/reduce_scatter | solution.py:146
  799.7 248.9 %reduce-scatter.26.cloned.1.call-start = ((), (), s32[]{:S(2)}) async-start(), calls=%async_computation.19 | async-start | bytes 13369344
  843.1 34.2 %copy-start.24 = (f32[128]{0:T(128)S(1)}, f32[128]{0:T(128)}, u32[]{:S(2)}) copy-start(f32[128]{0:T(128)} %copy-done.23) | copy-start | bytes 1540
  843.1 36.0 %copy-start.18 = (f32[2048]{0:T(1024)S(1)}, f32[2048]{0:T(1024)}, u32[]{:S(2)}) copy-start(f32[2048]{0:T(1024)} %get-tuple-element.80) | copy-start | bytes 24580
  843.1 36.0 %copy-start.25 = (f32[128]{0:T(128)S(1)}, f32[128]{0:T(128)}, u32[]{:S(2)}) copy-start(f32[128]{0:T(128)} %get-tuple-element.78) | copy-start | bytes 1540
  843.1 108.3 %copy-start.30 = (f32[128]{0:T(128)S(1)}, f32[128]{0:T(128)}, u32[]{:S(2)}) copy-start(f32[128]{0:T(128)} %copy-done.29) | copy-start | bytes 1540
  843.1 121.9 %copy-start.22 = (f32[128]{0:T(128)S(1)}, f32[128]{0:T(128)}, u32[]{:S(2)}) copy-start(f32[128]{0:T(128)} %copy-done.21) | copy-start | bytes 1540
  843.1 121.9 %copy-start.28 = (f32[128]{0:T(128)S(1)}, f32[128]{0:T(128)}, u32[]{:S(2)}) copy-start(f32[128]{0:T(128)} %copy-done.27) | copy-start | bytes 1540
  (32 other events, 172.6 us)
Sparse Core Ops, SparseCore 0:
  11.8 74.0 all-gather.8
  91.7 42.6 all-gather.18
  136.7 37.4 all-gather.16
  188.9 84.9 reduce-scatter.13
  277.8 70.2 all-gather.10
  350.3 69.3 all-gather.12
  438.3 82.7 reduce-scatter.17
  526.4 70.2 all-gather.14
  651.1 64.4 reduce-scatter.21
  717.8 65.4 reduce-scatter.23
  793.4 83.8 reduce-scatter.19
  881.0 83.9 reduce-scatter.15
  967.5 81.0 reduce-scatter.25
where the time goes:
time: 1080 us; the launch traced here: 1070 us
  waiting for transfers between devices  697 us (65%)
  matrix products  152 us (14%)
  local copies, waits for them, and re-layouts  77.9 us (7%)
  blocking collectives  72.4 us (7%)
  other arithmetic  57.5 us (5%)
  between operations  14.9 us (1%)
    unnamed x16, waiting for transfers between devices  175 us
    reduce_scatter x1, waiting for transfers between devices, per_device(): lax.psum_scatter(jnp.einsum('src,cd->srd', selected, o_weight, preferred_...  84.7 us
    reduce_scatter x1, waiting for transfers between devices, per_device(): lax.psum_scatter((jnp.einsum('srf,df->srd', gate_grad, gate_weight, prefe...  82.8 us
    all_gather x1, waiting for transfers between devices, per_device(): normed_all = lax.all_gather(normed[None], 'fsdp', axis=0, tiled=True)  73 us
    psum x1, blocking collectives, per_device(): lax.psum((attn_gain_grad, q_gain_grad, k_gain_grad, mlp_gain_grad), ('ctx...  72.4 us
    all_gather x1, waiting for transfers between devices, per_device(): branch_all = lax.all_gather(branch_grad[None], 'fsdp', axis=0, tiled=True)  70.3 us
    all_gather x1, waiting for transfers between devices, per_device(): hidden_all = lax.all_gather(hidden[None], 'fsdp', axis=0, tiled=True)  69.8 us
    unnamed x101, local copies, waits for them, and re-layouts  63.1 us
  transfers between devices with their start and end apart: 13, of which 13 were waited for; matrix products, arithmetic and copies ran while one was open for 14% of the time, Pallas kernels for 0%

commit v1 on v0

v1 whole, which is shorter than its diff:
```python
import jax
import jax.numpy as jnp
from jax import lax
from jax.experimental import pallas as pl
from jax.experimental.pallas import tpu as pltpu
from jax.sharding import Mesh, PartitionSpec as P

EPSILON = 1e-06
ROPE_BASE = 1000000.0
MASKED_SCORE = -1e30
HD = 128
BLK = 64
AXES = ("zl", "x", "core", "zh", "y")
SIZES = (2, 4, 2, 2, 4)
CTX = ("zl", "x", "core")
FSDP = ("zh", "y")
F32 = jnp.float32
BF16 = jnp.bfloat16


def rms_scale(values, gain_vec):
    inverse = lax.rsqrt(jnp.mean(values * values, axis=-1, keepdims=True) + EPSILON)
    return values * inverse * gain_vec


def head_prep(values, gain_vec, cos_table, sin_table):
    scaled = rms_scale(values, gain_vec)
    midway = scaled.shape[-1] // 2
    turned = jnp.concatenate([-scaled[..., midway:], scaled[..., :midway]], axis=-1)
    return scaled * cos_table + turned * sin_table


def tables(positions, head_dim):
    exponent_steps = jnp.arange(head_dim // 2, dtype=jnp.int32).astype(F32) * (2.0 / head_dim)
    frequency = ROPE_BASE ** (-exponent_steps)
    phases = positions.astype(F32)[:, None] * frequency[None, :]
    phases = jnp.concatenate([phases, phases], axis=-1)
    return (jnp.cos(phases), jnp.sin(phases))


def dot(left, right, contract=((1,), (0,))):
    return lax.dot_general(left, right, (contract, ((), ())), preferred_element_type=F32)


def from_next(value, axis, step):
    size = dict(zip(AXES, SIZES))[axis]
    return lax.ppermute(value, axis, [((i + step) % size, i) for i in range(size)])


def along_z(value, source):
    place = [(z % 2) * 2 + z // 2 for z in range(4)]
    return lax.ppermute(value, ("zl", "zh"), [(place[source(z)], place[z]) for z in range(4)])


def from_next_z(value, step):
    return along_z(value, lambda z: (z + step) % 4)


def gather_y(rows):
    return jnp.stack([rows] + [from_next(rows, "y", k) for k in (1, 2, 3)])


def scatter_y(parts):
    total = parts[0]
    for k in (1, 2, 3):
        total = total + from_next(parts[k].astype(BF16), "y", 4 - k).astype(F32)
    return total


def partner_shard(shard):
    rows, cols = shard.shape
    eighth = rows // 8
    x, core = lax.axis_index("x"), lax.axis_index("core")
    piece = lax.dynamic_slice_in_dim(shard, (x * 2 + core) * eighth, eighth, 0)
    piece = along_z(piece, lambda z: 3 - z)
    ring = jnp.stack([piece] + [from_next(piece, "x", k) for k in (1, 2, 3)])
    other = from_next(ring, "core", 1)
    low = jnp.where(core == 0, ring, other)
    high = jnp.where(core == 0, other, ring)
    both = jnp.stack([low, high], axis=1)
    both = jnp.concatenate([both, both], axis=0)
    both = lax.dynamic_slice_in_dim(both, lax.rem(4 - x, 4), 4, 0)
    return both.reshape(rows, cols)


def weight_grad(left, right):
    rows, width = left.shape
    n = right.shape[1] // 2
    x, core = lax.axis_index("x"), lax.axis_index("core")
    z = lax.axis_index("zh") * 2 + lax.axis_index("zl")
    zh = lax.axis_index("zh")
    split = left.reshape(rows, 8, 2, width // 16)
    theirs = lax.dynamic_index_in_dim(split, 1 - core, 2, keepdims=False).reshape(rows, width // 2)
    mine = lax.dynamic_index_in_dim(split, core, 2, keepdims=False).reshape(rows, width // 2)
    sent = dot(theirs, right, ((0,), (0,))).astype(BF16)
    got = from_next(sent, "core", 1)
    part = (dot(mine, right, ((0,), (0,))) + got.astype(F32)).astype(BF16)
    part = part.reshape(2, 4, width // 16, 2 * n)

    def for_x(k):
        return lax.dynamic_index_in_dim(part, lax.rem(x + k, 4), 1, keepdims=False)

    total = for_x(0).astype(F32)
    for k in (1, 2, 3):
        total = total + from_next(for_x(k), "x", 4 - k).astype(F32)
    part = total.astype(BF16)
    part = part.reshape(2, width // 16, 2, n)

    def for_z(k):
        dest = lax.rem(z + k, 4)
        rows_of = lax.dynamic_index_in_dim(part, lax.rem(dest, 2), 0, keepdims=False)
        side = jnp.where(dest // 2 == zh, 0, 1)
        return lax.dynamic_index_in_dim(rows_of, side, 1, keepdims=False)

    total = for_z(0).astype(F32)
    for k in (1, 2, 3):
        total = total + from_next_z(for_z(k), 4 - k).astype(F32)
    return total


def sum_all(vector):
    for axis, steps in (("y", (1, 2, 3)), ("x", (1, 2, 3)), ("core", (1,))):
        vector = vector + sum(from_next(vector, axis, k) for k in steps)
    return vector + sum(from_next_z(vector, k) for k in (1, 2, 3))


TILE = 256


def keep_mask(ends, first_row, rows, cols):
    place = first_row + lax.broadcasted_iota(jnp.int32, (rows, 1), 0)
    start = jnp.zeros((rows, 1), jnp.int32)
    for j in range(ends.shape[0]):
        start = jnp.where(place >= ends[j], ends[j], start)
    key = lax.broadcasted_iota(jnp.int32, (rows, cols), 1)
    return (key >= start) & (key <= place)


def attend_kernel(place, ends, core, q_in, mine, other, out, q_pos, k_pos, v_pos, log_total, out_pos):
    rows = q_in.shape[0]
    blocks = rows // BLK
    scale = HD ** (-0.5)

    @pl.when(core[0] == 0)
    def _():
        @pl.loop(0, blocks)
        def _(b):
            src = pl.ds(pl.multiple_of(b * BLK, BLK), BLK)
            dst = pl.ds(pl.multiple_of(place[b] * BLK, BLK), BLK)
            q_pos[dst, :] = q_in[src, :]
            k_pos[dst, :] = mine[src, :]
            v_pos[dst, :] = other[src, :]

    @pl.when(core[0] == 1)
    def _():
        @pl.loop(0, blocks)
        def _(b):
            src = pl.ds(pl.multiple_of(b * BLK, BLK), BLK)
            dst = pl.ds(pl.multiple_of(place[b] * BLK, BLK), BLK)
            q_pos[dst, :] = q_in[src, :]
            k_pos[dst, :] = other[src, :]
            v_pos[dst, :] = mine[src, :]

    for i in range(rows // TILE):
        span = pl.ds(i * TILE, TILE)
        n = (i + 1) * TILE
        scores = dot(q_pos[span, :], k_pos[:n, :], ((1,), (1,))) * scale
        scores = jnp.where(keep_mask(ends, i * TILE, TILE, n), scores, MASKED_SCORE)
        top = jnp.max(scores, axis=-1, keepdims=True)
        weights = jnp.exp(scores - top)
        total = jnp.sum(weights, axis=-1, keepdims=True)
        log_total[span, :] = top + jnp.log(total)
        probs = (weights * (1.0 / total)).astype(BF16)
        out_pos[span, :] = dot(probs, v_pos[:n, :]).astype(BF16)

    @pl.loop(0, blocks)
    def _(b):
        src = pl.ds(pl.multiple_of(b * BLK, BLK), BLK)
        dst = pl.ds(pl.multiple_of(place[b] * BLK, BLK), BLK)
        out[src, :] = out_pos[dst, :]


def attend_back_kernel(
    place, ends, core, grad_in, q_pos, k_pos, v_pos, log_total, q_grad, keep_grad, send_grad,
    grad_pos, q_acc, k_acc, v_acc,
):
    rows = grad_in.shape[0]
    blocks = rows // BLK
    scale = HD ** (-0.5)

    @pl.loop(0, blocks)
    def _(b):
        src = pl.ds(pl.multiple_of(b * BLK, BLK), BLK)
        dst = pl.ds(pl.multiple_of(place[b] * BLK, BLK), BLK)
        grad_pos[dst, :] = grad_in[src, :]

    k_acc[...] = jnp.zeros_like(k_acc)
    v_acc[...] = jnp.zeros_like(v_acc)
    for i in range(rows // TILE):
        span = pl.ds(i * TILE, TILE)
        n = (i + 1) * TILE
        queries = q_pos[span, :]
        grads = grad_pos[span, :]
        scores = dot(queries, k_pos[:n, :], ((1,), (1,))) * scale
        kept = keep_mask(ends, i * TILE, TILE, n)
        probs = jnp.where(kept, jnp.exp(scores - log_total[span, :]), 0.0)
        prob_grad = dot(grads, v_pos[:n, :], ((1,), (1,)))
        row_dot = jnp.sum(prob_grad * probs, axis=-1, keepdims=True)
        score_grad = (probs * (prob_grad - row_dot)).astype(BF16)
        q_acc[span, :] = (dot(score_grad, k_pos[:n, :]) * scale).astype(BF16)
        k_acc[:n, :] += dot(score_grad, queries, ((0,), (0,)))
        v_acc[:n, :] += dot(probs.astype(BF16), grads, ((0,), (0,)))

    @pl.loop(0, blocks)
    def _(b):
        src = pl.ds(pl.multiple_of(b * BLK, BLK), BLK)
        dst = pl.ds(pl.multiple_of(place[b] * BLK, BLK), BLK)
        q_grad[src, :] = q_acc[dst, :]
        k_rows = k_acc[dst, :] * scale
        v_rows = v_acc[dst, :]
        first = core[0] == 0
        keep_grad[src, :] = jnp.where(first, k_rows, v_rows)
        send_grad[src, :] = jnp.where(first, v_rows, k_rows).astype(BF16)


def attend(place, ends, core, q_in, mine, other):
    rows = q_in.shape[0]
    low = jax.ShapeDtypeStruct((rows, HD), BF16)
    smem = pl.BlockSpec(memory_space=pltpu.SMEM)
    vmem = pl.BlockSpec(memory_space=pltpu.VMEM)
    return pl.pallas_call(
        attend_kernel,
        out_shape=(low, low, low, low, jax.ShapeDtypeStruct((rows, 1), F32)),
        in_specs=[smem] * 3 + [vmem] * 3,
        out_specs=(vmem,) * 5,
        scratch_shapes=[pltpu.VMEM((rows, HD), BF16)],
        compiler_params=pltpu.CompilerParams(vmem_limit_bytes=40 * 2**20),
        cost_estimate=pl.CostEstimate(
            flops=2 * rows * rows * HD, bytes_accessed=rows * HD * 16, transcendentals=rows * rows // 2
        ),
        name="attend",
    )(place, ends, core, q_in, mine, other)


def attend_back(place, ends, core, grad_in, q_pos, k_pos, v_pos, log_total):
    rows = grad_in.shape[0]
    low = jax.ShapeDtypeStruct((rows, HD), BF16)
    smem = pl.BlockSpec(memory_space=pltpu.SMEM)
    vmem = pl.BlockSpec(memory_space=pltpu.VMEM)
    return pl.pallas_call(
        attend_back_kernel,
        out_shape=(low, jax.ShapeDtypeStruct((rows, HD), F32), low),
        in_specs=[smem] * 3 + [vmem] * 5,
        out_specs=(vmem,) * 3,
        scratch_shapes=[
            pltpu.VMEM((rows, HD), BF16),
            pltpu.VMEM((rows, HD), BF16),
            pltpu.VMEM((rows, HD), F32),
            pltpu.VMEM((rows, HD), F32),
        ],
        compiler_params=pltpu.CompilerParams(vmem_limit_bytes=48 * 2**20),
        cost_estimate=pl.CostEstimate(
            flops=5 * rows * rows * HD, bytes_accessed=rows * HD * 20, transcendentals=rows * rows // 2
        ),
        name="attend_back",
    )(place, ends, core, grad_in, q_pos, k_pos, v_pos, log_total)


def per_device(
    tokens,
    cotangent,
    attn_gain,
    q_weight,
    k_weight,
    v_weight,
    q_gain,
    k_gain,
    o_weight,
    mlp_gain,
    gate_weight,
    up_weight,
    down_weight,
    doc_lengths,
    block_place,
):
    rows = tokens.shape[1]
    zl, x, core = (lax.axis_index(a) for a in CTX)
    zh, y = (lax.axis_index(a) for a in FSDP)
    ctx_place = zl * 8 + x * 2 + core
    sequence = zh * 4 + lax.rem(y + ctx_place // 4, 4)
    ends = jnp.cumsum(lax.dynamic_index_in_dim(doc_lengths, sequence, 0, keepdims=False))
    ends = ends.astype(jnp.int32)
    core_flag = core.astype(jnp.int32).reshape(1)
    own_blocks = lax.dynamic_slice_in_dim(block_place, ctx_place * (rows // BLK), rows // BLK)
    own_positions = (own_blocks[:, None] * BLK + jnp.arange(BLK, dtype=jnp.int32)[None, :]).reshape(-1)
    cos_rows, sin_rows = tables(own_positions, HD)
    cos_rows = cos_rows[None, :, None, :]
    sin_rows = sin_rows[None, :, None, :]

    residual = tokens[0].astype(F32)
    normed = rms_scale(residual, attn_gain).astype(BF16)
    normed_all = gather_y(normed).reshape(4 * rows, -1)
    qkv_own = jnp.concatenate([q_weight, k_weight, v_weight], axis=1)
    qkv_cat = jnp.concatenate([qkv_own, partner_shard(qkv_own)], axis=1)
    raw = dot(normed_all, qkv_cat)
    raw = raw.reshape(4, rows, 2, 4, HD)
    q_raw = raw[:, :, :, :2].reshape(4, rows, 4, HD)
    k_raw = raw[:, :, :, 2]
    values = raw[:, :, :, 3].astype(BF16)
    queries = head_prep(q_raw, q_gain, cos_rows, sin_rows).astype(BF16)
    keys = head_prep(k_raw, k_gain, cos_rows, sin_rows).astype(BF16)
    q_out = queries.transpose(0, 2, 1, 3).reshape(16, 1, rows, HD)
    kv_out = jnp.stack([keys.transpose(0, 2, 1, 3), values.transpose(0, 2, 1, 3)], axis=2)
    kv_out = kv_out.reshape(16, 1, rows, HD)
    got = lax.all_to_all(jnp.concatenate([q_out, kv_out], axis=1), CTX, 0, 0, tiled=True)
    q_in = got[:, 0].reshape(16 * rows, HD)
    mine = got[:, 1].reshape(16 * rows, HD)
    other = from_next(mine, "core", 1)
    out, q_pos, k_pos, v_pos, log_total = attend(block_place, ends, core_flag, q_in, mine, other)
    attended = lax.all_to_all(out.reshape(16, rows, HD), CTX, 0, 0, tiled=True)
    attended = attended.reshape(4, 4, rows, HD).transpose(0, 2, 1, 3).reshape(4 * rows, 4 * HD)

    o_cat = jnp.concatenate([o_weight, partner_shard(o_weight)], axis=0)
    middle = residual + scatter_y(dot(attended, o_cat).reshape(4, rows, -1))
    hidden = rms_scale(middle, mlp_gain).astype(BF16)
    hidden_all = gather_y(hidden).reshape(4 * rows, -1)
    gate_up_own = jnp.concatenate([gate_weight, up_weight], axis=1)
    gate_up = jnp.concatenate([gate_up_own, partner_shard(gate_up_own)], axis=1)
    down_cat = jnp.concatenate([down_weight, partner_shard(down_weight)], axis=0)
    cot_all = gather_y(cotangent[0]).reshape(4 * rows, -1)
    act_grad = dot(cot_all, down_cat, ((1,), (1,)))
    width = gate_weight.shape[1]
    pre = dot(hidden_all, gate_up).reshape(4 * rows, 2, 2, width)
    gate_pre = pre[:, :, 0].reshape(4 * rows, 2 * width)
    up_pre = pre[:, :, 1].reshape(4 * rows, 2 * width)
    activation, silu_back = jax.vjp(lambda g, u: jax.nn.silu(g) * u, gate_pre, up_pre)
    activation = activation.astype(BF16)
    gate_grad, up_grad = silu_back(act_grad)
    gate_up_grad = jnp.stack(
        [gate_grad.reshape(-1, 2, width), up_grad.reshape(-1, 2, width)], axis=2
    )
    gate_up_grad = gate_up_grad.reshape(4 * rows, 4 * width).astype(BF16)
    hidden_grad = scatter_y(dot(gate_up_grad, gate_up, ((1,), (1,))).reshape(4, rows, -1))
    _, second_back = jax.vjp(rms_scale, middle, mlp_gain)
    middle_part, mlp_gain_grad = second_back(hidden_grad)
    middle_grad = cotangent[0].astype(F32) + middle_part
    branch_grad = middle_grad.astype(BF16)
    branch_all = gather_y(branch_grad).reshape(4 * rows, -1)
    attended_grad = dot(branch_all, o_cat, ((1,), (1,))).astype(BF16)
    grad_out = attended_grad.reshape(4, rows, 4, HD).transpose(0, 2, 1, 3).reshape(16, rows, HD)
    grad_in = lax.all_to_all(grad_out, CTX, 0, 0, tiled=True).reshape(16 * rows, HD)
    q_grad, keep_grad, send_grad = attend_back(
        block_place, ends, core_flag, grad_in, q_pos, k_pos, v_pos, log_total
    )
    kv_grad = (keep_grad + from_next(send_grad, "core", 1).astype(F32)).astype(BF16)
    back = jnp.stack([q_grad.reshape(16, rows, HD), kv_grad.reshape(16, rows, HD)], axis=1)
    back = lax.all_to_all(back, CTX, 0, 0, tiled=True)
    query_grad = back[:, 0].reshape(4, 4, rows, HD).transpose(0, 2, 1, 3).astype(F32)
    kv_back = back[:, 1].reshape(4, 2, 2, rows, HD)
    key_grad = kv_back[:, :, 0].transpose(0, 2, 1, 3).astype(F32)
    value_low = kv_back[:, :, 1].transpose(0, 2, 1, 3)
    _, query_back = jax.vjp(lambda u, g: head_prep(u, g, cos_rows, sin_rows), q_raw, q_gain)
    q_raw_grad, q_gain_grad = query_back(query_grad)
    _, key_back = jax.vjp(lambda u, g: head_prep(u, g, cos_rows, sin_rows), k_raw, k_gain)
    k_raw_grad, k_gain_grad = key_back(key_grad)
    low = jnp.concatenate(
        [
            q_raw_grad.astype(BF16).reshape(4, rows, 2, 2, HD),
            k_raw_grad.astype(BF16)[:, :, :, None],
            value_low[:, :, :, None],
        ],
        axis=3,
    ).reshape(4 * rows, 8 * HD)
    normed_grad = scatter_y(dot(low, qkv_cat, ((1,), (1,))).reshape(4, rows, -1))
    _, first_back = jax.vjp(rms_scale, residual, attn_gain)
    residual_part, attn_gain_grad = first_back(normed_grad)
    tokens_grad = (middle_grad + residual_part).astype(BF16)[None]

    mlp_out = scatter_y(dot(activation, down_cat).reshape(4, rows, -1))
    out_rows = (middle + mlp_out).astype(BF16)[None]

    gate_up_wgrad = weight_grad(hidden_all, gate_up_grad)
    down_wgrad = weight_grad(cot_all, activation)
    o_wgrad = weight_grad(branch_all, attended)
    qkv_wgrad = weight_grad(normed_all, low)
    gains = sum_all(jnp.concatenate([attn_gain_grad, q_gain_grad, k_gain_grad, mlp_gain_grad]))
    d = attn_gain.shape[0]
    return (
        out_rows,
        tokens_grad,
        gains[:d],
        qkv_wgrad[:, : 2 * HD],
        qkv_wgrad[:, 2 * HD : 3 * HD],
        qkv_wgrad[:, 3 * HD :],
        gains[d : d + HD],
        gains[d + HD : d + 2 * HD],
        o_wgrad.T,
        gains[d + 2 * HD :],
        gate_up_wgrad[:, :width],
        gate_up_wgrad[:, width:],
        down_wgrad.T,
    )


def solution(mesh):
    fine = Mesh(mesh.devices.reshape(SIZES), AXES)
    rows = P(FSDP, CTX, None)
    in_specs = (
        rows,
        rows,
        P(),
        P(None, FSDP),
        P(None, FSDP),
        P(None, FSDP),
        P(),
        P(),
        P(FSDP, None),
        P(),
        P(None, FSDP),
        P(None, FSDP),
        P(FSDP, None),
        P(),
        P(),
    )
    out_specs = (
        rows,
        rows,
        P(),
        P(CTX, FSDP),
        P(CTX, FSDP),
        P(CTX, FSDP),
        P(),
        P(),
        P(FSDP, CTX),
        P(),
        P(CTX, FSDP),
        P(CTX, FSDP),
        P(FSDP, CTX),
    )
    return jax.shard_map(
        per_device, mesh=fine, in_specs=in_specs, out_specs=out_specs, check_vma=False
    )
```

time: 1080 us -> 788 us (0.73)
  waiting for transfers between devices: 697 us -> 252 us
  starting transfers between devices: 1.41 us -> 131 us
  local copies, waits for them, and re-layouts: 77.9 us -> 189 us
  blocking collectives: 72.4 us -> 0 us
  matrix products: 152 us -> 90 us
  other arithmetic: 57.5 us -> 92.9 us
  Pallas kernels: 0 us -> 18.7 us
  between operations: 14.9 us -> 2.27 us
    all_gather x6 -> x0, waiting for transfers between devices: 307 us -> none  [the longest x1 73 us: per_device(): normed_all = lax.all_gather(normed[None], 'fsdp', axis=0, tiled=True)]
    ppermute x0 -> x84, waiting for transfers between devices: none -> 250 us  [the longest x65 223 us: from_next(): lax.ppermute(value, axis, [((i + step) % size, i) for i in range(size)])]
    reduce_scatter x4 -> x0, waiting for transfers between devices: 215 us -> none  [the longest x1 84.7 us: per_device(): lax.psum_scatter(jnp.einsum('src,cd->srd', selected, o_weight, preferred_...]
    unnamed x16 -> x0, waiting for transfers between devices: 175 us -> none
    ppermute x0 -> x84, starting transfers between devices: none -> 112 us  [the longest x65 79.6 us: from_next(): lax.ppermute(value, axis, [((i + step) % size, i) for i in range(size)])]
    psum x1 -> x0, blocking collectives: 72.4 us -> none  [per_device(): lax.psum((attn_gain_grad, q_gain_grad, k_gain_grad, mlp_gain_grad), ('ctx...]
    dot_general x27 -> x16, matrix products: 152 us -> 90 us  [dot(): lax.dot_general(left, right, (contract, ((), ())), preferred_element_type...]
    dynamic_slice x1 -> x15, local copies, waits for them, and re-layouts: 0.01 us -> 43.4 us  [the longest x8 15.8 us: for_x(): return lax.dynamic_index_in_dim(part, lax.rem(x + k, 4), 1, keepdims=False)]
  transfers between devices with their start and end apart: 13 -> 88, of which waited for: 13 -> 29; matrix products, arithmetic and copies ran while one was open for 14% -> 33% of each run, Pallas kernels for 0% -> 1%
where the time goes in v1:
time: 788 us; the launch traced here: 776 us
  waiting for transfers between devices  252 us (32%)
  local copies, waits for them, and re-layouts  189 us (24%)
  starting transfers between devices  131 us (17%)
  other arithmetic  92.9 us (12%)
  matrix products  90 us (11%)
  Pallas kernels  18.7 us (2%)
    ppermute x65, waiting for transfers between devices, from_next(): lax.ppermute(value, axis, [((i + step) % size, i) for i in range(size)])  223 us
    dot_general x16, matrix products, dot(): lax.dot_general(left, right, (contract, ((), ())), preferred_element_type...  90 us
    ppermute x65, starting transfers between devices, from_next(): lax.ppermute(value, axis, [((i + step) % size, i) for i in range(size)])  79.6 us
    unnamed x208, local copies, waits for them, and re-layouts  61 us
    ppermute x19, starting transfers between devices, along_z(): lax.ppermute(value, ('zl', 'zh'), [(place[source(z)], place[z]) for z in...  32.3 us
    ppermute x19, waiting for transfers between devices, along_z(): lax.ppermute(value, ('zl', 'zh'), [(place[source(z)], place[z]) for z in...  26.9 us
    dot_general x2, local copies, waits for them, and re-layouts, dot(): lax.dot_general(left, right, (contract, ((), ())), preferred_element_type...  23.2 us
    another operation x4, local copies, waits for them, and re-layouts, weight_grad(): split = left.reshape(rows, 8, 2, width // 16)  16.6 us
  transfers between devices with their start and end apart: 88, of which 29 were waited for; matrix products, arithmetic and copies ran while one was open for 33% of the time, Pallas kernels for 1%

profile of v1, /device:TPU:0, one launch (start us, length us, event | category | flops | bytes accessed | tf_op | source)
XLA Modules:
  0.0 775.7 jit_solution(1935696856684147869)
XLA Ops:
  43.2 6.5 copy.144
  79.8 8.1 %collective-permute-done.10 = bf16[32,2048]{1,0:T(8,128)(2,1)S(1)} collective-permute-done((bf16[32,2048]{1,0:T(8,128)(2,1)S(1)}, bf16[32,2048]{1,0:T(8,128)(2,1)S(1)}, u32[]{:S(2)}, u32[]{:S(2)}) %collective-permute-start.10) | collective-permute-done | bytes 131104 | tf_op jit(solution)/shard_map/ppermute | solution.py:47
  92.7 9.9 %collective-permute-done.25 = bf16[96,2048]{1,0:T(8,128)(2,1)S(1)} collective-permute-done((bf16[96,2048]{1,0:T(8,128)(2,1)}, bf16[96,2048]{1,0:T(8,128)(2,1)S(1)}, u32[]{:S(2)}, u32[]{:S(2)}) %collective-permute-start.25) | collective-permute-done | bytes 393248 | tf_op jit(solution)/shard_map/ppermute | solution.py:52
  117.5 7.9 %collective-permute-done.27 = bf16[96,2048]{1,0:T(8,128)(2,1)} collective-permute-done((bf16[96,2048]{1,0:T(8,128)(2,1)S(1)}, bf16[96,2048]{1,0:T(8,128)(2,1)}, u32[]{:S(2)}, u32[]{:S(2)}) %collective-permute-start.27) | collective-permute-done | bytes 393248 | tf_op jit(solution)/shard_map/ppermute | solution.py:47
  129.8 8.4 %attend.1 = (bf16[2048,128]{1,0:T(8,128)(2,1)}, bf16[2048,128]{1,0:T(8,128)(2,1)S(1)}, bf16[2048,128]{1,0:T(8,128)(2,1)S(1)}, bf16[2048,128]{1,0:T(8,128)(2,1)S(1)}, f32[2048,1]{1,0:T(8,128)S(1)}) custom-call(s32[32]{0:T(128)S(1)} %copy-done.2, s32[4]{0:T(128)S(1)} %bitcast.348, s32[1]{0:T(128)} %bitcast.2.core, bf16[2048,128]{1,0:T(8,128)(2,1)S(1)} %bitcast.346, ...), custom_call_target="tpu_custom_call" | custom-call | flops 1073741824 | bytes 4194304 | tf_op jit(solution)/shard_map/attend/pallas_call | solution.py:231
  145.7 13.5 %collective-permute-done.22 = bf16[256,1536]{1,0:T(8,128)(2,1)} collective-permute-done((bf16[256,1536]{1,0:T(8,128)(2,1)S(1)}, bf16[256,1536]{1,0:T(8,128)(2,1)}, u32[]{:S(2)}, u32[]{:S(2)}) %collective-permute-start.22) | collective-permute-done | bytes 786464 | tf_op jit(solution)/shard_map/ppermute | solution.py:47
  173.1 10.0 %collective-permute-done.16 = bf16[128,2048]{1,0:T(8,128)(2,1)S(1)} collective-permute-done((bf16[128,2048]{1,0:T(8,128)(2,1)S(1)}, bf16[128,2048]{1,0:T(8,128)(2,1)S(1)}, u32[]{:S(2)}, u32[]{:S(2)}) %collective-permute-start.16) | collective-permute-done | bytes 524320 | tf_op jit(solution)/shard_map/ppermute | solution.py:47
  184.8 10.4 %collective-permute-done.14 = bf16[128,2048]{1,0:T(8,128)(2,1)S(1)} collective-permute-done((bf16[128,2048]{1,0:T(8,128)(2,1)S(1)}, bf16[128,2048]{1,0:T(8,128)(2,1)S(1)}, u32[]{:S(2)}, u32[]{:S(2)}) %collective-permute-start.14) | collective-permute-done | bytes 524320 | tf_op jit(solution)/shard_map/ppermute | solution.py:47
  204.2 18.0 %collective-permute-done.19 = bf16[128,2048]{1,0:T(8,128)(2,1)S(1)} collective-permute-done((bf16[128,2048]{1,0:T(8,128)(2,1)S(1)}, bf16[128,2048]{1,0:T(8,128)(2,1)S(1)}, u32[]{:S(2)}, u32[]{:S(2)}) %collective-permute-start.19) | collective-permute-done | bytes 524320 | tf_op jit(solution)/shard_map/ppermute | solution.py:47
  238.7 16.7 %copy.152 = bf16[3072,2048]{1,0:T(8,128)(2,1)} copy(bf16[3072,2048]{0,1:T(8,128)(2,1)} %fusion.4) | data formatting | bytes 25165824 | tf_op jit(solution)/shard_map/dot_general | solution.py:42
  255.4 10.2 %fusion.140 = f32[512,2,2,768]{3,0,2,1:T(8,128)S(1)} fusion(bf16[512,2048,1,1]{1,0,3,2:T(8,128)(2,1)} %bitcast.360, bf16[2,2,768,2048]{3,2,1,0:T(8,128)(2,1)} %bitcast.356), kind=kOutput, calls=%fused_computation.290 | convolution fusion | flops 6442450944 | bytes 20971520 | tf_op jit(solution)/shard_map/dot_general | solution.py:42
  283.7 11.3 %fusion.8 = (bf16[512,1536]{1,0:T(8,128)(2,1)}, bf16[512,1536]{1,0:T(8,128)(2,1)}) fusion(f32[512,1536]{1,0:T(8,128)} %copy.155, f32[512,1536]{1,0:T(8,128)} %copy.157, bf16[512,2048]{1,0:T(8,128)(2,1)} %bitcast.359, bf16[768,2048]{1,0:T(8,128)(2,1)} %bitcast.380, bf16[768,2048]{1,0:T(8,128)(2,1)} %param.27), kind=kOutput, calls=%fused_computation.32 | convolution fusion | flops 3244818432 | bytes 17825792 | tf_op jit(solution)/shard_map/dot_general | solution.py:42
  305.1 11.5 %fusion.137 = (bf16[512,2048]{1,0:T(8,128)(2,1)}, f32[512,2048]{1,0:T(8,128)}) fusion(bf16[512,3072]{0,1:T(8,128)(2,1)} %bitcast.377, bf16[2048,1536]{1,0:T(8,128)(2,1)} %bitcast.355, bf16[2048,768]{1,0:T(8,128)(2,1)S(1)} %copy-done.21, bf16[2048,768]{1,0:T(8,128)(2,1)S(1)} %copy-done.19), kind=kOutput, calls=%fused_computation.287 | convolution fusion | flops 6481248256 | bytes 22020096 | tf_op jit(solution)/shard_map/dot_general | solution.py:42
  321.8 21.6 %collective-permute-done.38 = bf16[128,2048]{1,0:T(8,128)(2,1)S(1)} collective-permute-done((bf16[128,2048]{1,0:T(8,128)(2,1)S(1)}, bf16[128,2048]{1,0:T(8,128)(2,1)S(1)}, u32[]{:S(2)}, u32[]{:S(2)}) %collective-permute-start.38) | collective-permute-done | bytes 524320 | tf_op jit(solution)/shard_map/ppermute | solution.py:47
  368.6 8.0 %collective-permute-done.41 = bf16[128,2048]{1,0:T(8,128)(2,1)} collective-permute-done((bf16[128,2048]{1,0:T(8,128)(2,1)}, bf16[128,2048]{1,0:T(8,128)(2,1)}, u32[]{:S(2)}, u32[]{:S(2)}) %collective-permute-start.41) | collective-permute-done | bytes 524320 | tf_op jit(solution)/shard_map/ppermute | solution.py:47
  389.6 11.9 %constant_dynamic-slice_fusion = (bf16[512,8,1,128]{3,2,1,0:T(2,128)(2,1)}, bf16[512,8,1,128]{3,2,1,0:T(2,128)(2,1)}, bf16[512,8,1,128]{3,2,1,0:T(2,128)(2,1)}, bf16[512,8,1,128]{3,2,1,0:T(2,128)(2,1)}) fusion(bf16[512,8,2,128]{3,2,1,0:T(2,128)(2,1)S(1)} %reshape_reshape.15, s32[]{:T(128)S(6)} %select_n.250, s32[]{:T(128)S(6)} %select_n.249, ...), kind=kLoop, calls=%fused_computation.231 | loop fusion | bytes 8388616 | tf_op jit(solution)/shard_map/jit(dynamic_index_in_dim)/dynamic_slice | solution.py:93
  431.0 10.3 %attend_back.1 = (bf16[2048,128]{1,0:T(8,128)(2,1)S(1)}, f32[2048,128]{1,0:T(8,128)S(1)}, bf16[2048,128]{1,0:T(8,128)(2,1)S(1)}) custom-call(s32[32]{0:T(128)S(1)} %copy-done.2, s32[4]{0:T(128)S(1)} %bitcast.349, s32[1]{0:T(128)} %bitcast.2.core, bf16[2048,128]{1,0:T(8,128)(2,1)S(1)} %bitcast.343, bf16[2048,128]{1,0:T(8,128)(2,1)S(1)} %get-tuple-element.22.q_pos, ...), custom_call_target="tpu_custom_call" | custom-call | flops 2684354560 | bytes 5242880 | tf_op jit(solution)/shard_map/attend_back/pallas_call | solution.py:250
  442.1 9.9 %constant_dynamic-slice_fusion.9 = (bf16[512,8,1,128]{3,2,1,0:T(2,128)(2,1)}, bf16[512,8,1,128]{3,2,1,0:T(2,128)(2,1)}, bf16[512,8,1,128]{3,2,1,0:T(2,128)(2,1)}, bf16[512,8,1,128]{3,2,1,0:T(2,128)(2,1)}) fusion(bf16[512,8,2,128]{3,2,1,0:T(2,128)(2,1)S(1)} %copy-done.17, s32[]{:T(128)S(6)} %select_n.249, s32[]{:T(128)S(6)} %select_n.250, ...), kind=kLoop, calls=%fused_computation.240 | loop fusion | bytes 8388616 | tf_op jit(solution)/shard_map/jit(dynamic_index_in_dim)/dynamic_slice | solution.py:94
  467.8 8.5 %convolution_convert_fusion = bf16[1024,3072]{1,0:T(8,128)(2,1)} fusion(bf16[512,1024]{0,1:T(8,128)(2,1)} %bitcast.410, bf16[512,3072]{0,1:T(8,128)(2,1)} %bitcast.378), kind=kOutput, calls=%fused_computation.18 | convolution fusion | flops 3224371200 | bytes 10485760 | tf_op jit(solution)/shard_map/dot_general | solution.py:42
  534.7 9.3 %collective-permute-done.45 = bf16[128,2048]{1,0:T(8,128)(2,1)} collective-permute-done((bf16[128,2048]{1,0:T(8,128)(2,1)}, bf16[128,2048]{1,0:T(8,128)(2,1)}, u32[]{:S(2)}, u32[]{:S(2)}) %collective-permute-start.45) | collective-permute-done | bytes 524320 | tf_op jit(solution)/shard_map/ppermute | solution.py:47
  585.6 23.6 %collective-permute-done.80 = bf16[2,128,1536]{2,1,0:T(8,128)(2,1)} collective-permute-done((bf16[2,128,1536]{2,1,0:T(8,128)(2,1)}, bf16[2,128,1536]{2,1,0:T(8,128)(2,1)}, u32[]{:S(2)}, u32[]{:S(2)}) %collective-permute-start.80) | collective-permute-done | bytes 786464 | tf_op jit(solution)/shard_map/ppermute | solution.py:47
  625.3 6.5 add_convert_fusion
  669.4 63.6 %collective-permute-done.58 = bf16[2,128,1024]{1,2,0:T(8,128)(2,1)S(1)} collective-permute-done((bf16[2,128,1024]{1,2,0:T(8,128)(2,1)}, bf16[2,128,1024]{1,2,0:T(8,128)(2,1)S(1)}, u32[]{:S(2)}, u32[]{:S(2)}) %collective-permute-start.58) | collective-permute-done | bytes 524320 | tf_op jit(solution)/shard_map/ppermute | solution.py:47
  757.1 11.4 %collective-permute-done.76 = bf16[128,1536]{0,1:T(8,128)(2,1)S(1)} collective-permute-done((bf16[128,1536]{0,1:T(8,128)(2,1)S(1)}, bf16[128,1536]{0,1:T(8,128)(2,1)S(1)}, u32[]{:S(2)}, u32[]{:S(2)}) %collective-permute-start.76) | collective-permute-done | bytes 393248 | tf_op jit(solution)/shard_map/ppermute | solution.py:52
  (521 shorter events, 446.7 us)
Async XLA Ops:
  8.9 43.7 %collective-permute-start.2 = (bf16[128,2048]{1,0:T(8,128)(2,1)}, bf16[128,2048]{1,0:T(8,128)(2,1)}, u32[]{:S(2)}, u32[]{:S(2)}) collective-permute-start(bf16[128,2048]{1,0:T(8,128)(2,1)} %fusion.34), channel_id=1, source_target_pairs={{3,0},{0,1},{1,2},{2,3},{7,4},{4,5},{5,6},{6,7},{11,8},{8,9},{9,10... | collective-permute-start | bytes 1572872 | tf_op jit(solution)/shard_map/ppermute | solution.py:47
  10.5 43.5 %collective-permute-start.1 = (bf16[128,2048]{1,0:T(8,128)(2,1)}, bf16[128,2048]{1,0:T(8,128)(2,1)}, u32[]{:S(2)}, u32[]{:S(2)}) collective-permute-start(bf16[128,2048]{1,0:T(8,128)(2,1)} %fusion.34), channel_id=1, source_target_pairs={{2,0},{3,1},{0,2},{1,3},{6,4},{7,5},{4,6},{5,7},{10,8},{11,9},{8,1... | collective-permute-start | bytes 1572872 | tf_op jit(solution)/shard_map/ppermute | solution.py:47
  35.3 67.3 %collective-permute-start.35 = (bf16[128,2048]{1,0:T(8,128)(2,1)S(1)}, bf16[128,2048]{1,0:T(8,128)(2,1)}, u32[]{:S(2)}, u32[]{:S(2)}) collective-permute-start(bf16[128,2048]{1,0:T(8,128)(2,1)S(1)} %bitcast.369), channel_id=1, source_target_pairs={{3,0},{0,1},{1,2},{2,3},{7,4},{4,5},{5,6},{6,7},{11,8},{8,9},{9,10... | collective-permute-start | bytes 1572872 | tf_op jit(solution)/shard_map/ppermute | solution.py:47
  49.7 54.5 %collective-permute-start.34 = (bf16[128,2048]{1,0:T(8,128)(2,1)S(1)}, bf16[128,2048]{1,0:T(8,128)(2,1)}, u32[]{:S(2)}, u32[]{:S(2)}) collective-permute-start(bf16[128,2048]{1,0:T(8,128)(2,1)S(1)} %bitcast.370), channel_id=1, source_target_pairs={{2,0},{3,1},{0,2},{1,3},{6,4},{7,5},{4,6},{5,7},{10,8},{11,9},{8,1... | collective-permute-start | bytes 1572872 | tf_op jit(solution)/shard_map/ppermute | solution.py:47
  52.6 54.3 %collective-permute-start.33 = (bf16[128,2048]{1,0:T(8,128)(2,1)S(1)}, bf16[128,2048]{1,0:T(8,128)(2,1)}, u32[]{:S(2)}, u32[]{:S(2)}) collective-permute-start(bf16[128,2048]{1,0:T(8,128)(2,1)S(1)} %bitcast.371), channel_id=1, source_target_pairs={{1,0},{2,1},{3,2},{0,3},{5,4},{6,5},{7,6},{4,7},{9,8},{10,9},{11,1... | collective-permute-start | bytes 1572872 | tf_op jit(solution)/shard_map/ppermute | solution.py:47
  66.4 45.6 %all-to-all-start = ((bf16[16,2,128,128]{3,2,1,0:T(8,128)(2,1)}), bf16[16,2,128,128]{3,2,1,0:T(8,128)(2,1)S(1)}, u32[]{:S(2)}, u32[]{:S(2)}) async-start(bf16[16,2,128,128]{3,2,1,0:T(8,128)(2,1)} %copy.148), calls=%async_computation | async-start | bytes 2097152 | tf_op jit(solution)/shard_map/all_to_all | solution.py:315
  72.8 38.6 %collective-permute-start.20 = (bf16[256,1536]{1,0:T(8,128)(2,1)}, bf16[256,1536]{1,0:T(8,128)(2,1)S(1)}, u32[]{:S(2)}, u32[]{:S(2)}) collective-permute-start(bf16[256,1536]{1,0:T(8,128)(2,1)} %fusion.63), channel_id=1, source_target_pairs={{68,0},{4,64},{64,4},{0,68},{69,1},{5,65},{65,5},{1,69},{70,2},{6,... | collective-permute-start | bytes 2359304 | tf_op jit(solution)/shard_map/ppermute | solution.py:52
  111.4 34.3 %collective-permute-start.23 = (bf16[256,1536]{1,0:T(8,128)(2,1)S(1)}, bf16[256,1536]{1,0:T(8,128)(2,1)}, u32[]{:S(2)}, u32[]{:S(2)}) collective-permute-start(bf16[256,1536]{1,0:T(8,128)(2,1)S(1)} %collective-permute-done.20), channel_id=1, source_target_pairs={{48,0},{0,16},{16,32},{32,48},{49,1},{1,17},{17,33},{33,49},{50,2}... | collective-permute-start | bytes 2359304 | tf_op jit(solution)/shard_map/ppermute | solution.py:47
  112.1 47.1 %collective-permute-start.22 = (bf16[256,1536]{1,0:T(8,128)(2,1)S(1)}, bf16[256,1536]{1,0:T(8,128)(2,1)}, u32[]{:S(2)}, u32[]{:S(2)}) collective-permute-start(bf16[256,1536]{1,0:T(8,128)(2,1)S(1)} %collective-permute-done.20), channel_id=1, source_target_pairs={{32,0},{48,16},{0,32},{16,48},{33,1},{49,17},{1,33},{17,49},{34,2}... | collective-permute-start | bytes 2359304 | tf_op jit(solution)/shard_map/ppermute | solution.py:47
  115.9 43.3 %collective-permute-start.21 = (bf16[256,1536]{1,0:T(8,128)(2,1)S(1)}, bf16[256,1536]{1,0:T(8,128)(2,1)}, u32[]{:S(2)}, u32[]{:S(2)}) collective-permute-start(bf16[256,1536]{1,0:T(8,128)(2,1)S(1)} %collective-permute-done.20), channel_id=1, source_target_pairs={{16,0},{32,16},{48,32},{0,48},{17,1},{33,17},{49,33},{1,49},{18,2}... | collective-permute-start | bytes 2359304 | tf_op jit(solution)/shard_map/ppermute | solution.py:47
  129.3 41.8 %collective-permute-start.29 = (bf16[4,96,2048]{2,1,0:T(8,128)(2,1)}, bf16[4,96,2048]{2,1,0:T(8,128)(2,1)}, u32[]{:S(2)}, u32[]{:S(2)}) collective-permute-start(bf16[4,96,2048]{2,1,0:T(8,128)(2,1)} %pad_maximum_fusion.12), channel_id=1, source_target_pairs={{8,0},{0,8},{9,1},{1,9},{10,2},{2,10},{11,3},{3,11},{12,4},{4,12},... | collective-permute-start | bytes 4718600 | tf_op jit(solution)/shard_map/ppermute | solution.py:47
  162.3 62.1 %collective-permute-start.24 = (bf16[4,256,1536]{2,1,0:T(8,128)(2,1)}, bf16[4,256,1536]{2,1,0:T(8,128)(2,1)}, u32[]{:S(2)}, u32[]{:S(2)}) collective-permute-start(bf16[4,256,1536]{2,1,0:T(8,128)(2,1)} %pad_maximum_fusion.6), channel_id=1, source_target_pairs={{8,0},{0,8},{9,1},{1,9},{10,2},{2,10},{11,3},{3,11},{12,4},{4,12},... | collective-permute-start | bytes 9437192 | tf_op jit(solution)/shard_map/ppermute | solution.py:47
  384.5 43.2 %all-to-all-start.2 = ((bf16[16,128,128]{2,1,0:T(8,128)(2,1)}), bf16[16,128,128]{2,1,0:T(8,128)(2,1)S(1)}, u32[]{:S(2)}, u32[]{:S(2)}) async-start(bf16[16,128,128]{2,1,0:T(8,128)(2,1)} %bitcast.393), calls=%async_computation.2 | async-start | bytes 1048576 | tf_op jit(solution)/shard_map/all_to_all | solution.py:351
  462.0 34.6 %all-to-all-start.3 = ((bf16[16,2,128,128]{3,2,1,0:T(8,128)(2,1)}), bf16[16,2,128,128]{3,2,1,0:T(8,128)(2,1)S(1)}, u32[]{:S(2)}, u32[]{:S(2)}) async-start(bf16[16,2,128,128]{3,2,1,0:T(8,128)(2,1)} %pad_maximum_fusion.19), calls=%async_computation.3 | async-start | bytes 2097152 | tf_op jit(solution)/shard_map/all_to_all | solution.py:357
  476.3 146.7 %collective-permute-start.70 = (bf16[1024,3072]{1,0:T(8,128)(2,1)}, bf16[1024,3072]{1,0:T(8,128)(2,1)}, u32[]{:S(2)}, u32[]{:S(2)}) collective-permute-start(bf16[1024,3072]{1,0:T(8,128)(2,1)} %convolution_convert_fusion), channel_id=1, source_target_pairs={{8,0},{0,8},{9,1},{1,9},{10,2},{2,10},{11,3},{3,11},{12,4},{4,12},... | collective-permute-start | bytes 18874376 | tf_op jit(solution)/shard_map/ppermute | solution.py:47
  483.6 79.1 %collective-permute-start.77 = (bf16[1024,1536]{1,0:T(8,128)(2,1)}, bf16[1024,1536]{1,0:T(8,128)(2,1)}, u32[]{:S(2)}, u32[]{:S(2)}) collective-permute-start(bf16[1024,1536]{1,0:T(8,128)(2,1)} %convolution_convert_fusion.1), channel_id=1, source_target_pairs={{8,0},{0,8},{9,1},{1,9},{10,2},{2,10},{11,3},{3,11},{12,4},{4,12},... | collective-permute-start | bytes 9437192 | tf_op jit(solution)/shard_map/ppermute | solution.py:47
  570.6 45.8 %collective-permute-start.56 = (bf16[1024,1024]{1,0:T(8,128)(2,1)}, bf16[1024,1024]{1,0:T(8,128)(2,1)}, u32[]{:S(2)}, u32[]{:S(2)}) collective-permute-start(bf16[1024,1024]{1,0:T(8,128)(2,1)} %convolution_convert_fusion.2), channel_id=1, source_target_pairs={{8,0},{0,8},{9,1},{1,9},{10,2},{2,10},{11,3},{3,11},{12,4},{4,12},... | collective-permute-start | bytes 6291464 | tf_op jit(solution)/shard_map/ppermute | solution.py:47
  573.2 36.0 %collective-permute-start.80 = (bf16[2,128,1536]{2,1,0:T(8,128)(2,1)}, bf16[2,128,1536]{2,1,0:T(8,128)(2,1)}, u32[]{:S(2)}, u32[]{:S(2)}) collective-permute-start(bf16[2,128,1536]{2,1,0:T(8,128)(2,1)} %get-tuple-element.93), channel_id=1, source_target_pairs={{16,0},{32,16},{48,32},{0,48},{17,1},{33,17},{49,33},{1,49},{18,2}... | collective-permute-start | bytes 2359304 | tf_op jit(solution)/shard_map/ppermute | solution.py:47
  577.8 35.1 %collective-permute-start.78 = (bf16[2,128,1536]{2,1,0:T(8,128)(2,1)}, bf16[2,128,1536]{2,1,0:T(8,128)(2,1)}, u32[]{:S(2)}, u32[]{:S(2)}) collective-permute-start(bf16[2,128,1536]{2,1,0:T(8,128)(2,1)} %get-tuple-element.92), channel_id=1, source_target_pairs={{48,0},{0,16},{16,32},{32,48},{49,1},{1,17},{17,33},{33,49},{50,2}... | collective-permute-start | bytes 2359304 | tf_op jit(solution)/shard_map/ppermute | solution.py:47
  648.8 96.6 %collective-permute-start.73 = (bf16[2,128,3072]{1,2,0:T(8,128)(2,1)}, bf16[2,128,3072]{1,2,0:T(8,128)(2,1)}, u32[]{:S(2)}, u32[]{:S(2)}) collective-permute-start(bf16[2,128,3072]{1,2,0:T(8,128)(2,1)} %bitcast.406), channel_id=1, source_target_pairs={{16,0},{32,16},{48,32},{0,48},{17,1},{33,17},{49,33},{1,49},{18,2}... | collective-permute-start | bytes 4718600 | tf_op jit(solution)/shard_map/ppermute | solution.py:47
  648.9 96.7 %collective-permute-start.72 = (bf16[2,128,3072]{1,2,0:T(8,128)(2,1)}, bf16[2,128,3072]{1,2,0:T(8,128)(2,1)}, u32[]{:S(2)}, u32[]{:S(2)}) collective-permute-start(bf16[2,128,3072]{1,2,0:T(8,128)(2,1)} %bitcast.405), channel_id=1, source_target_pairs={{32,0},{48,16},{0,32},{16,48},{33,1},{49,17},{1,33},{17,49},{34,2}... | collective-permute-start | bytes 4718600 | tf_op jit(solution)/shard_map/ppermute | solution.py:47
  649.5 96.1 %collective-permute-start.71 = (bf16[2,128,3072]{1,2,0:T(8,128)(2,1)}, bf16[2,128,3072]{1,2,0:T(8,128)(2,1)}, u32[]{:S(2)}, u32[]{:S(2)}) collective-permute-start(bf16[2,128,3072]{1,2,0:T(8,128)(2,1)} %bitcast.404), channel_id=1, source_target_pairs={{48,0},{0,16},{16,32},{32,48},{49,1},{1,17},{17,33},{33,49},{50,2}... | collective-permute-start | bytes 4718600 | tf_op jit(solution)/shard_map/ppermute | solution.py:47
  661.9 71.0 %collective-permute-start.58 = (bf16[2,128,1024]{1,2,0:T(8,128)(2,1)}, bf16[2,128,1024]{1,2,0:T(8,128)(2,1)S(1)}, u32[]{:S(2)}, u32[]{:S(2)}) collective-permute-start(bf16[2,128,1024]{1,2,0:T(8,128)(2,1)} %bitcast.109), channel_id=1, source_target_pairs={{32,0},{48,16},{0,32},{16,48},{33,1},{49,17},{1,33},{17,49},{34,2}... | collective-permute-start | bytes 1572872 | tf_op jit(solution)/shard_map/ppermute | solution.py:47
  666.0 73.2 %collective-permute-start.57 = (bf16[2,128,1024]{1,2,0:T(8,128)(2,1)}, bf16[2,128,1024]{1,2,0:T(8,128)(2,1)}, u32[]{:S(2)}, u32[]{:S(2)}) collective-permute-start(bf16[2,128,1024]{1,2,0:T(8,128)(2,1)} %bitcast.108), channel_id=1, source_target_pairs={{48,0},{0,16},{16,32},{32,48},{49,1},{1,17},{17,33},{33,49},{50,2}... | collective-permute-start | bytes 1572872 | tf_op jit(solution)/shard_map/ppermute | solution.py:47
  (160 other events, 2442.0 us)

commit v2 on v1

--- a/solution.py
+++ b/solution.py
@@ -264,6 +264,252 @@
         ),
         name="attend_back",
     )(place, ends, core, grad_in, q_pos, k_pos, v_pos, log_total)
+
+
+def peers(pairs):
+    barrier = pltpu.get_barrier_semaphore()
+    for place in pairs:
+        pl.semaphore_signal(barrier, inc=1, device_id=place, device_id_type=pl.DeviceIdType.MESH)
+    pl.semaphore_wait(barrier, len(pairs))
+
+
+def remote(src, dst, sent, landed, place):
+    return pltpu.make_async_remote_copy(
+        src_ref=src, dst_ref=dst, send_sem=sent, recv_sem=landed, device_id=place,
+        device_id_type=pl.DeviceIdType.MESH,
+    )
+
+
+ROWS = 128
+WIDE = 256
+
+
+def mlp_kernel(
+    middle, cot, gain, cot_hbm, gate_hbm, up_hbm, down_hbm,
+    middle_grad, branch, gain_grad, part_hbm, wgrad_hbm,
+    hid, cots, gate_w, up_w, down_w, act_grad, gu_grad, act, parts, got, z_out, z_got, part, stage,
+    load_sem, sent, landed, sent_back, landed_back, stage_sem, part_sem,
+):
+    y, zh = lax.axis_index("y"), lax.axis_index("zh")
+    half = 4 * ROWS
+    width = gate_w.shape[1]
+    model = hid.shape[1]
+
+    def along(k):
+        return {"y": lax.rem(y + k, 4)}
+
+    across = {"zh": 1 - zh}
+    loads = [
+        pltpu.make_async_copy(src, dst, load_sem.at[i])
+        for i, (src, dst) in enumerate(
+            ((cot_hbm, cots), (down_hbm, down_w), (gate_hbm, gate_w), (up_hbm, up_w))
+        )
+    ]
+    for load in loads:
+        load.start()
+
+    rows_in = middle[...]
+    inverse = lax.rsqrt(jnp.mean(rows_in * rows_in, axis=-1, keepdims=True) + EPSILON)
+    hid[:ROWS, :] = (rows_in * inverse * gain[...]).astype(BF16)
+    peers([along(1), along(2), along(3), across])
+
+    def slot(r):
+        return hid.at[pl.ds(r * ROWS, ROWS), :]
+
+    out = []
+    for k in (1, 3, 2):
+        out.append(remote(slot(0), slot(4 - k), sent.at[k], landed.at[4 - k], along(k)))
+    out.append(remote(slot(0), slot(4), sent.at[4], landed.at[4], across))
+    for copy in out:
+        copy.start()
+
+    def grads_of_cot(first):
+        rows = pl.ds(first, half)
+
+        @pl.loop(0, width // WIDE)
+        def _(n):
+            cols = pl.ds(pl.multiple_of(n * WIDE, WIDE), WIDE)
+            act_grad[rows, cols] = dot(cots[rows, :], down_w[cols, :], ((1,), (1,)))
+
+    loads[0].wait()
+    loads[1].wait()
+    grads_of_cot(0)
+    loads[2].wait()
+    loads[3].wait()
+    grads_of_cot(half)
+
+    out[3].wait_recv()
+    on = []
+    for k in (1, 3, 2):
+        on.append(remote(slot(4), slot(8 - k), sent.at[4 + k], landed.at[8 - k], along(k)))
+    for copy in on:
+        copy.start()
+
+    def forward(first):
+        rows = pl.ds(first, half)
+
+        @pl.loop(0, width // WIDE)
+        def _(n):
+            cols = pl.ds(pl.multiple_of(n * WIDE, WIDE), WIDE)
+            gate = dot(hid[rows, :], gate_w[:, cols])
+            up = dot(hid[rows, :], up_w[:, cols])
+            sig = jax.nn.sigmoid(gate)
+            silu = gate * sig
+            grad = act_grad[rows, cols]
+            act[rows, cols] = (silu * up).astype(BF16)
+            gu_grad[rows, cols] = (grad * up * sig * (1.0 + gate * (1.0 - sig))).astype(BF16)
+            gu_grad[rows, pl.ds(pl.multiple_of(width + n * WIDE, WIDE), WIDE)] = (grad * silu).astype(BF16)
+
+    def backward(first):
+        rows = pl.ds(first, half)
+
+        @pl.loop(0, model // WIDE)
+        def _(n):
+            cols = pl.ds(pl.multiple_of(n * WIDE, WIDE), WIDE)
+            total = dot(gu_grad[rows, :width], gate_w[cols, :], ((1,), (1,)))
+            total += dot(gu_grad[rows, width:], up_w[cols, :], ((1,), (1,)))
+            parts[rows, cols] = total.astype(BF16)
+
+    def share(r):
+        return parts.at[pl.ds(r * ROWS, ROWS), :]
+
+    def got_at(r):
+        return got.at[pl.ds(r * ROWS, ROWS), :]
+
+    for copy in out[:3]:
+        copy.wait_recv()
+    forward(0)
+    backward(0)
+    for copy in on:
+        copy.wait_recv()
+    forward(half)
+    backward(half)
+    back = {}
+    for r in (4, 0):
+        for k in (1, 3, 2):
+            copy = remote(share(r + k), got_at(r + 4 - k), sent_back.at[r + k], landed_back.at[r + 4 - k], along(k))
+            copy.start()
+            back[r + 4 - k] = copy
+
+    def down_part(first):
+        rows = pl.ds(first, half)
+
+        @pl.loop(0, model // WIDE)
+        def _(n):
+            cols = pl.ds(pl.multiple_of(n * WIDE, WIDE), WIDE)
+            part[rows, cols] = dot(act[rows, :], down_w[:, cols]).astype(BF16)
+
+    down_part(0)
+    down_part(half)
+    part_copy = pltpu.make_async_copy(part, part_hbm, part_sem)
+    part_copy.start()
+
+    def stage_copy(b, n):
+        rows = pl.ds(pl.multiple_of(n * WIDE, WIDE), WIDE)
+        return pltpu.make_async_copy(stage.at[b], wgrad_hbm.at[rows, :], stage_sem.at[b])
+
+    def weight_grads(begin, end):
+        @pl.loop(begin, end)
+        def _(m):
+            for b in range(2):
+                n = m * 2 + b
+                cols = pl.ds(pl.multiple_of(n * WIDE, WIDE), WIDE)
+
+                @pl.when(m > 0)
+                def _():
+                    stage_copy(b, n - 2).wait()
+
+                stage[b, :, : 2 * width] = dot(hid[:, cols], gu_grad[...], ((0,), (0,))).astype(BF16)
+                stage[b, :, 2 * width :] = dot(cots[:, cols], act[...], ((0,), (0,))).astype(BF16)
+                stage_copy(b, n).start()
+
+    steps = model // WIDE // 2
+    weight_grads(0, steps // 2)
+    for k in (1, 2, 3):
+        back[4 + k].wait_recv()
+
+    def summed(r):
+        total = parts[pl.ds(r * ROWS, ROWS), :].astype(F32)
+        for k in (1, 2, 3):
+            total += got[pl.ds((r + k) * ROWS, ROWS), :].astype(F32)
+        return total
+
+    z_out[...] = summed(4).astype(BF16)
+    z_copy = remote(z_out, z_got, sent_back.at[0], landed_back.at[0], across)
+    z_copy.start()
+    weight_grads(steps // 2, steps)
+    for k in (1, 2, 3):
+        back[k].wait_recv()
+    z_copy.wait_recv()
+
+    grad = summed(0) + z_got[...].astype(F32)
+    rows_in = middle[...]
+    inverse = lax.rsqrt(jnp.mean(rows_in * rows_in, axis=-1, keepdims=True) + EPSILON)
+    gain_grad[...] = jnp.sum(grad * rows_in * inverse, axis=0, keepdims=True)
+    scaled = grad * gain[...]
+    inner = jnp.mean(rows_in * scaled, axis=-1, keepdims=True)
+    total = cot[...].astype(F32) + inverse * scaled - rows_in * (inverse * inverse * inverse * inner)
+    middle_grad[...] = total
+    branch[...] = total.astype(BF16)
+
+    for copy in out + on:
+        copy.wait_send()
+    for copy in back.values():
+        copy.wait_send()
+    z_copy.wait_send()
+    part_copy.wait()
+    for b in range(2):
+        stage_copy(b, 2 * steps - 2 + b).wait()
+
+
+def mlp(middle, cot, gain, cot_all, gate_w, up_w, down_w):
+    rows, model = middle.shape
+    width = gate_w.shape[1]
+    anywhere = pl.BlockSpec(memory_space=pl.ANY)
+    vmem = pl.BlockSpec(memory_space=pltpu.VMEM)
+    dma = pltpu.SemaphoreType.DMA
+    return pl.pallas_call(
+        mlp_kernel,
+        out_shape=(
+            jax.ShapeDtypeStruct((rows, model), F32),
+            jax.ShapeDtypeStruct((rows, model), BF16),
+            jax.ShapeDtypeStruct((1, model), F32),
+            jax.ShapeDtypeStruct((8 * rows, model), BF16),
+            jax.ShapeDtypeStruct((model, 3 * width), BF16),
+        ),
+        in_specs=[vmem] * 3 + [anywhere] * 4,
+        out_specs=(vmem, vmem, vmem, anywhere, anywhere),
+        scratch_shapes=[
+            pltpu.VMEM((8 * rows, model), BF16),
+            pltpu.VMEM((8 * rows, model), BF16),
+            pltpu.VMEM((model, width), BF16),
+            pltpu.VMEM((model, width), BF16),
+            pltpu.VMEM((width, model), BF16),
+            pltpu.VMEM((8 * rows, width), F32),
+            pltpu.VMEM((8 * rows, 2 * width), BF16),
+            pltpu.VMEM((8 * rows, width), BF16),
+            pltpu.VMEM((8 * rows, model), BF16),
+            pltpu.VMEM((8 * rows, model), BF16),
+            pltpu.VMEM((rows, model), BF16),
+            pltpu.VMEM((rows, model), BF16),
+            pltpu.VMEM((8 * rows, model), BF16),
+            pltpu.VMEM((2, WIDE, 3 * width), BF16),
+            dma((4,)),
+            dma((8,)),
+            dma((8,)),
+            dma((8,)),
+            dma((8,)),
+            dma((2,)),
+            dma,
+        ],
+        compiler_params=pltpu.CompilerParams(
+            collective_id=1, has_side_effects=True, vmem_limit_bytes=58 * 2**20
+        ),
+        cost_estimate=pl.CostEstimate(
+            flops=2 * 9 * 8 * rows * model * width, bytes_accessed=40 * 2**20, transcendentals=8 * rows * width
+        ),
+        name="mlp",
+    )(middle, cot, gain.reshape(1, model), cot_all, gate_w, up_w, down_w)
 
 
 def per_device(
@@ -300,6 +546,8 @@
     residual = tokens[0].astype(F32)
     normed = rms_scale(residual, attn_gain).astype(BF16)
     normed_all = gather_y(normed).reshape(4 * rows, -1)
+    pair = jnp.stack([cotangent[0], from_next(cotangent[0], "zh", 1)])
+    cot_all = jnp.stack([pair] + [from_next(pair, "y", k) for k in (1, 2, 3)], axis=1).reshape(8 * rows, -1)
     qkv_own = jnp.concatenate([q_weight, k_weight, v_weight], axis=1)
     qkv_cat = jnp.concatenate([qkv_own, partner_shard(qkv_own)], axis=1)
     raw = dot(normed_all, qkv_cat)
@@ -322,29 +570,9 @@
 
     o_cat = jnp.concatenate([o_weight, partner_shard(o_weight)], axis=0)
     middle = residual + scatter_y(dot(attended, o_cat).reshape(4, rows, -1))
-    hidden = rms_scale(middle, mlp_gain).astype(BF16)
-    hidden_all = gather_y(hidden).reshape(4 * rows, -1)
-    gate_up_own = jnp.concatenate([gate_weight, up_weight], axis=1)
-    gate_up = jnp.concatenate([gate_up_own, partner_shard(gate_up_own)], axis=1)
-    down_cat = jnp.concatenate([down_weight, partner_shard(down_weight)], axis=0)
-    cot_all = gather_y(cotangent[0]).reshape(4 * rows, -1)
-    act_grad = dot(cot_all, down_cat, ((1,), (1,)))
-    width = gate_weight.shape[1]
-    pre = dot(hidden_all, gate_up).reshape(4 * rows, 2, 2, width)
-    gate_pre = pre[:, :, 0].reshape(4 * rows, 2 * width)
-    up_pre = pre[:, :, 1].reshape(4 * rows, 2 * width)
-    activation, silu_back = jax.vjp(lambda g, u: jax.nn.silu(g) * u, gate_pre, up_pre)
-    activation = activation.astype(BF16)
-    gate_grad, up_grad = silu_back(act_grad)
-    gate_up_grad = jnp.stack(
-        [gate_grad.reshape(-1, 2, width), up_grad.reshape(-1, 2, width)], axis=2
+    middle_grad, branch_grad, mlp_gain_grad, mlp_part, mlp_wgrad = mlp(
+        middle, cotangent[0], mlp_gain, cot_all, gate_weight, up_weight, down_weight
     )
-    gate_up_grad = gate_up_grad.reshape(4 * rows, 4 * width).astype(BF16)
-    hidden_grad = scatter_y(dot(gate_up_grad, gate_up, ((1,), (1,))).reshape(4, rows, -1))
-    _, second_back = jax.vjp(rms_scale, middle, mlp_gain)
-    middle_part, mlp_gain_grad = second_back(hidden_grad)
-    middle_grad = cotangent[0].astype(F32) + middle_part
-    branch_grad = middle_grad.astype(BF16)
     branch_all = gather_y(branch_grad).reshape(4 * rows, -1)
     attended_grad = dot(branch_all, o_cat, ((1,), (1,))).astype(BF16)
     grad_out = attended_grad.reshape(4, rows, 4, HD).transpose(0, 2, 1, 3).reshape(16, rows, HD)
@@ -376,14 +604,18 @@
     residual_part, attn_gain_grad = first_back(normed_grad)
     tokens_grad = (middle_grad + residual_part).astype(BF16)[None]
 
-    mlp_out = scatter_y(dot(activation, down_cat).reshape(4, rows, -1))
+    mlp_part = mlp_part.reshape(2, 4, rows, -1)
+    mlp_sum = mlp_part[:, 0].astype(F32)
+    for k in (1, 2, 3):
+        mlp_sum = mlp_sum + from_next(mlp_part[:, k], "y", 4 - k).astype(F32)
+    mlp_out = mlp_sum[0] + from_next(mlp_sum[1].astype(BF16), "zh", 1).astype(F32)
     out_rows = (middle + mlp_out).astype(BF16)[None]
-
-    gate_up_wgrad = weight_grad(hidden_all, gate_up_grad)
-    down_wgrad = weight_grad(cot_all, activation)
+    mlp_wgrad = lax.psum_scatter(mlp_wgrad, CTX, scatter_dimension=0, tiled=True).astype(F32)
+    width = gate_weight.shape[1]
+
     o_wgrad = weight_grad(branch_all, attended)
     qkv_wgrad = weight_grad(normed_all, low)
-    gains = sum_all(jnp.concatenate([attn_gain_grad, q_gain_grad, k_gain_grad, mlp_gain_grad]))
+    gains = sum_all(jnp.concatenate([attn_gain_grad, q_gain_grad, k_gain_grad, mlp_gain_grad[0]]))
     d = attn_gain.shape[0]
     return (
         out_rows,
@@ -396,9 +628,9 @@
         gains[d + HD : d + 2 * HD],
         o_wgrad.T,
         gains[d + 2 * HD :],
-        gate_up_wgrad[:, :width],
-        gate_up_wgrad[:, width:],
-        down_wgrad.T,
+        mlp_wgrad[:, :width],
+        mlp_wgrad[:, width : 2 * width],
+        mlp_wgrad[:, 2 * width :].T,
     )
 
 

time: 788 us -> 543 us (0.69)
  waiting for transfers between devices: 252 us -> 127 us
  Pallas kernels: 18.7 us -> 127 us
  local copies, waits for them, and re-layouts: 189 us -> 93.8 us
  matrix products: 90 us -> 25.4 us
  other arithmetic: 92.9 us -> 44.8 us
  starting transfers between devices: 131 us -> 99.2 us
  between operations: 2.27 us -> 15.5 us
    ppermute x65 -> x45, waiting for transfers between devices: 223 us -> 96.1 us  [from_next(): lax.ppermute(value, axis, [((i + step) % size, i) for i in range(size)])]
    pallas_call x0 -> x1, Pallas kernels: none -> 109 us  [mlp(): pl.pallas_call(mlp_kernel, out_shape=(jax.ShapeDtypeStruct((rows, model),...]
    dot_general x16 -> x8, matrix products: 90 us -> 25.4 us  [dot(): lax.dot_general(left, right, (contract, ((), ())), preferred_element_type...]
    unnamed x208 -> x144, local copies, waits for them, and re-layouts: 61 us -> 41.7 us
    ppermute x65 -> x45, starting transfers between devices: 79.6 us -> 61 us  [from_next(): lax.ppermute(value, axis, [((i + step) % size, i) for i in range(size)])]
    dot_general x2 -> x1, local copies, waits for them, and re-layouts: 23.2 us -> 6.54 us  [dot(): lax.dot_general(left, right, (contract, ((), ())), preferred_element_type...]
    ppermute x19 -> x11, starting transfers between devices: 32.3 us -> 20.1 us  [along_z(): lax.ppermute(value, ('zl', 'zh'), [(place[source(z)], place[z]) for z in...]
    dynamic_slice x1 -> x0, local copies, waits for them, and re-layouts: 11.9 us -> none  [weight_grad(): lax.dynamic_index_in_dim(split, 1 - core, 2, keepdims=False)]
  transfers between devices with their start and end apart: 88 -> 61, of which waited for: 29 -> 27; matrix products, arithmetic and copies ran while one was open for 33% -> 26% of each run, Pallas kernels for 1% -> 4%
where the time goes in v2:
time: 543 us; the launch traced here: 533 us
  waiting for transfers between devices  127 us (23%)
  Pallas kernels  127 us (23%)
  starting transfers between devices  99.2 us (18%)
  local copies, waits for them, and re-layouts  93.8 us (17%)
  other arithmetic  44.8 us (8%)
  matrix products  25.4 us (5%)
  between operations  15.5 us (3%)
    pallas_call x1, Pallas kernels, mlp(): pl.pallas_call(mlp_kernel, out_shape=(jax.ShapeDtypeStruct((rows, model),...  109 us
    ppermute x45, waiting for transfers between devices, from_next(): lax.ppermute(value, axis, [((i + step) % size, i) for i in range(size)])  96.1 us
    ppermute x45, starting transfers between devices, from_next(): lax.ppermute(value, axis, [((i + step) % size, i) for i in range(size)])  61 us
    unnamed x144, local copies, waits for them, and re-layouts  41.7 us
    dot_general x8, matrix products, dot(): lax.dot_general(left, right, (contract, ((), ())), preferred_element_type...  25.4 us
    ppermute x11, starting transfers between devices, along_z(): lax.ppermute(value, ('zl', 'zh'), [(place[source(z)], place[z]) for z in...  20.1 us
    ppermute x11, waiting for transfers between devices, along_z(): lax.ppermute(value, ('zl', 'zh'), [(place[source(z)], place[z]) for z in...  17.4 us
  transfers between devices with their start and end apart: 61, of which 27 were waited for; matrix products, arithmetic and copies ran while one was open for 26% of the time, Pallas kernels for 4%

profile of v2, /device:TPU:0, one launch (start us, length us, event | category | flops | bytes accessed | tf_op | source)
XLA Modules:
  0.0 533.0 jit_solution(6771835897553650597)
XLA Ops:
  8.3 4.2 collective-permute-start.3
  12.7 6.1 %collective-permute-done.3 = bf16[256,512]{1,0:T(8,128)(2,1)S(1)} collective-permute-done((bf16[256,512]{1,0:T(8,128)(2,1)S(1)}, bf16[256,512]{1,0:T(8,128)(2,1)S(1)}, u32[]{:S(2)}, u32[]{:S(2)}) %collective-permute-start.3) | collective-permute-done | bytes 262176 | tf_op jit(solution)/shard_map/ppermute | solution.py:52
  43.9 6.5 %copy.106 = bf16[1024,2048]{1,0:T(8,128)(2,1)} copy(bf16[1024,2048]{0,1:T(8,128)(2,1)} %fusion.43) | data formatting | bytes 8388608 | tf_op jit(solution)/shard_map/dot_general | solution.py:42
  51.7 4.6 fusion.5
  98.9 8.4 %attend.1 = (bf16[2048,128]{1,0:T(8,128)(2,1)}, bf16[2048,128]{1,0:T(8,128)(2,1)S(1)}, bf16[2048,128]{1,0:T(8,128)(2,1)S(1)}, bf16[2048,128]{1,0:T(8,128)(2,1)S(1)}, f32[2048,1]{1,0:T(8,128)S(1)}) custom-call(s32[32]{0:T(128)S(1)} %copy-done.2, s32[4]{0:T(128)S(1)} %bitcast.287, s32[1]{0:T(128)} %bitcast.2.core, bf16[2048,128]{1,0:T(8,128)(2,1)S(1)} %bitcast.285, ...), custom_call_target="tpu_custom_call" | custom-call | flops 1073741824 | bytes 4194304 | tf_op jit(solution)/shard_map/attend/pallas_call | solution.py:231
  109.1 4.8 all-to-all-start.1
  115.9 8.9 %all-to-all-done.1 = bf16[16,128,128]{2,1,0:T(8,128)(2,1)S(1)} async-done(((bf16[16,128,128]{2,1,0:T(8,128)(2,1)}), bf16[16,128,128]{2,1,0:T(8,128)(2,1)S(1)}, u32[]{:S(2)}, u32[]{:S(2)}) %all-to-all-start.1) | async-done | bytes 524320 | tf_op jit(solution)/shard_map/all_to_all | solution.py:568
  133.9 10.4 %collective-permute-done.18 = bf16[2,128,2048]{2,1,0:T(8,128)(2,1)} collective-permute-done((bf16[2,128,2048]{2,1,0:T(8,128)(2,1)}, bf16[2,128,2048]{2,1,0:T(8,128)(2,1)}, u32[]{:S(2)}, u32[]{:S(2)}) %collective-permute-start.18) | collective-permute-done | bytes 1048608 | tf_op jit(solution)/shard_map/ppermute | solution.py:47
  148.6 6.3 %collective-permute-done.14 = bf16[128,2048]{1,0:T(8,128)(2,1)S(1)} collective-permute-done((bf16[128,2048]{1,0:T(8,128)(2,1)S(1)}, bf16[128,2048]{1,0:T(8,128)(2,1)S(1)}, u32[]{:S(2)}, u32[]{:S(2)}) %collective-permute-start.14) | collective-permute-done | bytes 524320 | tf_op jit(solution)/shard_map/ppermute | solution.py:47
  155.3 9.8 %collective-permute-done.15 = bf16[128,2048]{1,0:T(8,128)(2,1)S(1)} collective-permute-done((bf16[128,2048]{1,0:T(8,128)(2,1)S(1)}, bf16[128,2048]{1,0:T(8,128)(2,1)S(1)}, u32[]{:S(2)}, u32[]{:S(2)}) %collective-permute-start.15) | collective-permute-done | bytes 524320 | tf_op jit(solution)/shard_map/ppermute | solution.py:47
  166.5 108.6 %mlp.1 = (f32[128,2048]{1,0:T(8,128)}, bf16[128,2048]{1,0:T(8,128)(2,1)}, f32[1,2048]{1,0:T(1,128)}, bf16[1024,2048]{1,0:T(8,128)(2,1)}, bf16[2048,2304]{1,0:T(8,128)(2,1)}) custom-call(f32[128,2048]{1,0:T(8,128)} %fusion.11.middle, bf16[128,2048]{1,0:T(8,128)(2,1)} %bitcast.334, f32[1,2048]{1,0:T(1,128)} %bitcast.349, bf16[1024,2048]{1,0:T(8,128)(2,1)} %bitcast.300, ...), custom_call_target="tpu_custom_call" | custom-call | flops 28991029248 | bytes 41943040 | tf_op jit(solution)/shard_map/mlp/pallas_call | solution.py:471
  284.0 15.4 %collective-permute-done.27 = bf16[128,2048]{1,0:T(8,128)(2,1)} collective-permute-done((bf16[128,2048]{1,0:T(8,128)(2,1)}, bf16[128,2048]{1,0:T(8,128)(2,1)}, u32[]{:S(2)}, u32[]{:S(2)}) %collective-permute-start.27) | collective-permute-done | bytes 524320 | tf_op jit(solution)/shard_map/ppermute | solution.py:47
  317.7 4.5 reshape_reshape.7
  325.6 10.3 %attend_back.1 = (bf16[2048,128]{1,0:T(8,128)(2,1)S(1)}, f32[2048,128]{1,0:T(8,128)S(1)}, bf16[2048,128]{1,0:T(8,128)(2,1)S(1)}) custom-call(s32[32]{0:T(128)S(1)} %copy-done.2, s32[4]{0:T(128)S(1)} %bitcast.288, s32[1]{0:T(128)} %bitcast.2.core, bf16[2048,128]{1,0:T(8,128)(2,1)S(1)} %bitcast.282, bf16[2048,128]{1,0:T(8,128)(2,1)S(1)} %get-tuple-element.30.q_pos, ...), custom_call_target="tpu_custom_call" | custom-call | flops 2684354560 | bytes 5242880 | tf_op jit(solution)/shard_map/attend_back/pallas_call | solution.py:250
  336.5 9.9 %constant_dynamic-slice_fusion.1 = (bf16[512,8,1,128]{3,2,1,0:T(2,128)(2,1)}, bf16[512,8,1,128]{3,2,1,0:T(2,128)(2,1)}, bf16[512,8,1,128]{3,2,1,0:T(2,128)(2,1)}, bf16[512,8,1,128]{3,2,1,0:T(2,128)(2,1)}) fusion(bf16[512,8,2,128]{3,2,1,0:T(2,128)(2,1)S(1)} %copy-done.12, s32[]{:T(128)S(6)} %select_n.162, s32[]{:T(128)S(6)} %select_n.163, ...), kind=kLoop, calls=%fused_computation.166 | loop fusion | bytes 8388616 | tf_op jit(solution)/shard_map/jit(dynamic_index_in_dim)/dynamic_slice | solution.py:94
  346.3 5.8 %copy.152 = bf16[512,8,1,128]{0,3,1,2:T(8,128)(2,1)} copy(bf16[512,8,1,128]{3,2,1,0:T(2,128)(2,1)} %get-tuple-element.102) | data formatting | bytes 2097152
  352.2 5.8 %copy.153 = bf16[512,8,1,128]{0,3,1,2:T(8,128)(2,1)} copy(bf16[512,8,1,128]{3,2,1,0:T(2,128)(2,1)} %get-tuple-element.103) | data formatting | bytes 2097152
  358.0 5.8 %copy.149 = bf16[512,8,1,128]{0,3,1,2:T(8,128)(2,1)} copy(bf16[512,8,1,128]{3,2,1,0:T(2,128)(2,1)} %get-tuple-element.161) | data formatting | bytes 2097152
  363.8 5.9 %copy.150 = bf16[512,8,1,128]{0,3,1,2:T(8,128)(2,1)} copy(bf16[512,8,1,128]{3,2,1,0:T(2,128)(2,1)} %get-tuple-element.162) | data formatting | bytes 2097152
  374.0 5.7 %all-to-all-start.3 = ((bf16[16,2,128,128]{3,2,1,0:T(8,128)(2,1)}), bf16[16,2,128,128]{3,2,1,0:T(8,128)(2,1)S(1)}, u32[]{:S(2)}, u32[]{:S(2)}) async-start(bf16[16,2,128,128]{3,2,1,0:T(8,128)(2,1)} %pad_maximum_fusion.12), calls=%async_computation.3 | async-start | bytes 2097152 | tf_op jit(solution)/shard_map/all_to_all | solution.py:585
  412.6 6.4 %fusion.100 = (bf16[512,2048]{1,0:T(8,128)(2,1)S(1)}, f32[512,2048]{1,0:T(8,128)}) fusion(bf16[512,1024]{1,0:T(8,128)(2,1)} %reshape.368, bf16[2048,512]{1,0:T(8,128)(2,1)S(1)} %bitcast.295, bf16[2048,128]{1,0:T(8,128)(2,1)} %param.20, bf16[2048,128]{1,0:T(8,128)(2,1)} %param.19, bf16[2048,256]{1,0:T(8,128)(2,1)} %param.18), kind=kOutput, calls=%fused_computation.203 | convolution fusion | flops 2165309440 | bytes 11534336 | tf_op jit(solution)/shard_map/dot_general | solution.py:42
  430.7 19.2 %collective-permute-done.29 = bf16[128,2048]{1,0:T(8,128)(2,1)S(1)} collective-permute-done((bf16[128,2048]{1,0:T(8,128)(2,1)}, bf16[128,2048]{1,0:T(8,128)(2,1)S(1)}, u32[]{:S(2)}, u32[]{:S(2)}) %collective-permute-start.29) | collective-permute-done | bytes 524320 | tf_op jit(solution)/shard_map/ppermute | solution.py:47
  490.3 7.8 %collective-permute-done.43 = bf16[2,128,1024]{1,2,0:T(8,128)(2,1)S(1)} collective-permute-done((bf16[2,128,1024]{1,2,0:T(8,128)(2,1)}, bf16[2,128,1024]{1,2,0:T(8,128)(2,1)S(1)}, u32[]{:S(2)}, u32[]{:S(2)}) %collective-permute-start.43) | collective-permute-done | bytes 524320 | tf_op jit(solution)/shard_map/ppermute | solution.py:47
  498.1 10.9 %collective-permute-done.44 = bf16[2,128,1024]{1,2,0:T(8,128)(2,1)S(1)} collective-permute-done((bf16[2,128,1024]{1,2,0:T(8,128)(2,1)}, bf16[2,128,1024]{1,2,0:T(8,128)(2,1)S(1)}, u32[]{:S(2)}, u32[]{:S(2)}) %collective-permute-start.44) | collective-permute-done | bytes 524320 | tf_op jit(solution)/shard_map/ppermute | solution.py:47
  (361 shorter events, 225.4 us)
Async XLA Ops:
  25.4 25.0 %collective-permute-start.2 = (bf16[128,2048]{1,0:T(8,128)(2,1)}, bf16[128,2048]{1,0:T(8,128)(2,1)}, u32[]{:S(2)}, u32[]{:S(2)}) collective-permute-start(bf16[128,2048]{1,0:T(8,128)(2,1)} %fusion.17), channel_id=1, source_target_pairs={{3,0},{0,1},{1,2},{2,3},{7,4},{4,5},{5,6},{6,7},{11,8},{8,9},{9,10... | collective-permute-start | bytes 1572872 | tf_op jit(solution)/shard_map/ppermute | solution.py:47
  27.0 24.7 %collective-permute-start.1 = (bf16[128,2048]{1,0:T(8,128)(2,1)}, bf16[128,2048]{1,0:T(8,128)(2,1)}, u32[]{:S(2)}, u32[]{:S(2)}) collective-permute-start(bf16[128,2048]{1,0:T(8,128)(2,1)} %fusion.17), channel_id=1, source_target_pairs={{2,0},{3,1},{0,2},{1,3},{6,4},{7,5},{4,6},{5,7},{10,8},{11,9},{8,1... | collective-permute-start | bytes 1572872 | tf_op jit(solution)/shard_map/ppermute | solution.py:47
  87.5 26.5 %collective-permute-start.13 = (bf16[4,32,2048]{2,1,0:T(8,128)(2,1)S(1)}, bf16[4,32,2048]{2,1,0:T(8,128)(2,1)}, u32[]{:S(2)}, u32[]{:S(2)}) collective-permute-start(bf16[4,32,2048]{2,1,0:T(8,128)(2,1)S(1)} %pad_maximum_fusion.16), channel_id=1, source_target_pairs={{8,0},{0,8},{9,1},{1,9},{10,2},{2,10},{11,3},{3,11},{12,4},{4,12},... | collective-permute-start | bytes 1572872 | tf_op jit(solution)/shard_map/ppermute | solution.py:47
  93.5 39.7 %collective-permute-start.19 = (bf16[2,128,2048]{2,1,0:T(8,128)(2,1)}, bf16[2,128,2048]{2,1,0:T(8,128)(2,1)}, u32[]{:S(2)}, u32[]{:S(2)}) collective-permute-start(bf16[2,128,2048]{2,1,0:T(8,128)(2,1)} %get-tuple-element.128), channel_id=1, source_target_pairs={{2,0},{3,1},{0,2},{1,3},{6,4},{7,5},{4,6},{5,7},{10,8},{11,9},{8,1... | collective-permute-start | bytes 3145736 | tf_op jit(solution)/shard_map/ppermute | solution.py:47
  96.7 47.5 %collective-permute-start.18 = (bf16[2,128,2048]{2,1,0:T(8,128)(2,1)}, bf16[2,128,2048]{2,1,0:T(8,128)(2,1)}, u32[]{:S(2)}, u32[]{:S(2)}) collective-permute-start(bf16[2,128,2048]{2,1,0:T(8,128)(2,1)} %get-tuple-element.128), channel_id=1, source_target_pairs={{1,0},{2,1},{3,2},{0,3},{5,4},{6,5},{7,6},{4,7},{9,8},{10,9},{11,1... | collective-permute-start | bytes 3145736 | tf_op jit(solution)/shard_map/ppermute | solution.py:47
  97.9 46.3 %collective-permute-start.20 = (bf16[2,128,2048]{2,1,0:T(8,128)(2,1)}, bf16[2,128,2048]{2,1,0:T(8,128)(2,1)}, u32[]{:S(2)}, u32[]{:S(2)}) collective-permute-start(bf16[2,128,2048]{2,1,0:T(8,128)(2,1)} %get-tuple-element.128), channel_id=1, source_target_pairs={{3,0},{0,1},{1,2},{2,3},{7,4},{4,5},{5,6},{6,7},{11,8},{8,9},{9,10... | collective-permute-start | bytes 3145736 | tf_op jit(solution)/shard_map/ppermute | solution.py:47
  113.9 408.7 %reduce-scatter.2.cloned.1.call-start = ((), (), s32[]{:S(2)}) async-start(), calls=%async_computation.5 | async-start | bytes 10027008 | tf_op jit(solution)/shard_map/reduce_scatter | solution.py:613
  129.9 25.0 %collective-permute-start.14 = (bf16[128,2048]{1,0:T(8,128)(2,1)S(1)}, bf16[128,2048]{1,0:T(8,128)(2,1)S(1)}, u32[]{:S(2)}, u32[]{:S(2)}) collective-permute-start(bf16[128,2048]{1,0:T(8,128)(2,1)S(1)} %get-tuple-element.113), channel_id=1, source_target_pairs={{3,0},{0,1},{1,2},{2,3},{7,4},{4,5},{5,6},{6,7},{11,8},{8,9},{9,10... | collective-permute-start | bytes 1572872 | tf_op jit(solution)/shard_map/ppermute | solution.py:47
  130.6 24.7 %collective-permute-start.16 = (bf16[128,2048]{1,0:T(8,128)(2,1)S(1)}, bf16[128,2048]{1,0:T(8,128)(2,1)S(1)}, u32[]{:S(2)}, u32[]{:S(2)}) collective-permute-start(bf16[128,2048]{1,0:T(8,128)(2,1)S(1)} %get-tuple-element.114), channel_id=1, source_target_pairs={{1,0},{2,1},{3,2},{0,3},{5,4},{6,5},{7,6},{4,7},{9,8},{10,9},{11,1... | collective-permute-start | bytes 1572872 | tf_op jit(solution)/shard_map/ppermute | solution.py:47
  133.2 32.0 %collective-permute-start.15 = (bf16[128,2048]{1,0:T(8,128)(2,1)S(1)}, bf16[128,2048]{1,0:T(8,128)(2,1)S(1)}, u32[]{:S(2)}, u32[]{:S(2)}) collective-permute-start(bf16[128,2048]{1,0:T(8,128)(2,1)S(1)} %get-tuple-element.115), channel_id=1, source_target_pairs={{2,0},{3,1},{0,2},{1,3},{6,4},{7,5},{4,6},{5,7},{10,8},{11,9},{8,1... | collective-permute-start | bytes 1572872 | tf_op jit(solution)/shard_map/ppermute | solution.py:47
  275.2 24.2 %collective-permute-start.27 = (bf16[128,2048]{1,0:T(8,128)(2,1)}, bf16[128,2048]{1,0:T(8,128)(2,1)}, u32[]{:S(2)}, u32[]{:S(2)}) collective-permute-start(bf16[128,2048]{1,0:T(8,128)(2,1)} %get-tuple-element.29), channel_id=1, source_target_pairs={{3,0},{0,1},{1,2},{2,3},{7,4},{4,5},{5,6},{6,7},{11,8},{8,9},{9,10... | collective-permute-start | bytes 1572872 | tf_op jit(solution)/shard_map/ppermute | solution.py:47
  313.7 66.1 %collective-permute-start.21 = (bf16[2,128,2048]{2,1,0:T(8,128)(2,1)}, bf16[2,128,2048]{2,1,0:T(8,128)(2,1)}, u32[]{:S(2)}, u32[]{:S(2)}) collective-permute-start(bf16[2,128,2048]{2,1,0:T(8,128)(2,1)} %get-tuple-element.99), channel_id=1, source_target_pairs={{3,0},{0,1},{1,2},{2,3},{7,4},{4,5},{5,6},{6,7},{11,8},{8,9},{9,10... | collective-permute-start | bytes 3145736 | tf_op jit(solution)/shard_map/ppermute | solution.py:47
  314.3 65.5 %collective-permute-start.22 = (bf16[2,128,2048]{2,1,0:T(8,128)(2,1)}, bf16[2,128,2048]{2,1,0:T(8,128)(2,1)}, u32[]{:S(2)}, u32[]{:S(2)}) collective-permute-start(bf16[2,128,2048]{2,1,0:T(8,128)(2,1)} %get-tuple-element.100), channel_id=1, source_target_pairs={{2,0},{3,1},{0,2},{1,3},{6,4},{7,5},{4,6},{5,7},{10,8},{11,9},{8,1... | collective-permute-start | bytes 3145736 | tf_op jit(solution)/shard_map/ppermute | solution.py:47
  317.7 62.0 %collective-permute-start.23 = (bf16[2,128,2048]{2,1,0:T(8,128)(2,1)}, bf16[2,128,2048]{2,1,0:T(8,128)(2,1)}, u32[]{:S(2)}, u32[]{:S(2)}) collective-permute-start(bf16[2,128,2048]{2,1,0:T(8,128)(2,1)} %get-tuple-element.101), channel_id=1, source_target_pairs={{1,0},{2,1},{3,2},{0,3},{5,4},{6,5},{7,6},{4,7},{9,8},{10,9},{11,1... | collective-permute-start | bytes 3145736 | tf_op jit(solution)/shard_map/ppermute | solution.py:47
  335.8 37.0 %collective-permute-start.28 = (bf16[2048,128]{1,0:T(8,128)(2,1)S(1)}, bf16[2048,128]{1,0:T(8,128)(2,1)S(1)}, u32[]{:S(2)}, u32[]{:S(2)}) collective-permute-start(bf16[2048,128]{1,0:T(8,128)(2,1)S(1)} %get-tuple-element.36), channel_id=1, source_target_pairs={{8,0},{0,8},{9,1},{1,9},{10,2},{2,10},{11,3},{3,11},{12,4},{4,12},... | collective-permute-start | bytes 1572872 | tf_op jit(solution)/shard_map/ppermute | solution.py:47
  383.7 39.1 %collective-permute-start.24 = (bf16[128,2048]{1,0:T(8,128)(2,1)}, bf16[128,2048]{1,0:T(8,128)(2,1)}, u32[]{:S(2)}, u32[]{:S(2)}) collective-permute-start(bf16[128,2048]{1,0:T(8,128)(2,1)} %fusion.51), channel_id=1, source_target_pairs={{4,0},{0,4},{5,1},{1,5},{6,2},{2,6},{7,3},{3,7},{12,8},{8,12},{13,... | collective-permute-start | bytes 1572872 | tf_op jit(solution)/shard_map/ppermute | solution.py:47
  389.4 35.5 %collective-permute-start.50 = (bf16[2,128,512]{2,1,0:T(8,128)(2,1)}, bf16[2,128,512]{2,1,0:T(8,128)(2,1)}, u32[]{:S(2)}, u32[]{:S(2)}) collective-permute-start(bf16[2,128,512]{2,1,0:T(8,128)(2,1)} %get-tuple-element.120), channel_id=1, source_target_pairs={{48,0},{0,16},{16,32},{32,48},{49,1},{1,17},{17,33},{33,49},{50,2}... | collective-permute-start | bytes 786440 | tf_op jit(solution)/shard_map/ppermute | solution.py:47
  391.3 34.8 %collective-permute-start.52 = (bf16[2,128,512]{2,1,0:T(8,128)(2,1)}, bf16[2,128,512]{2,1,0:T(8,128)(2,1)}, u32[]{:S(2)}, u32[]{:S(2)}) collective-permute-start(bf16[2,128,512]{2,1,0:T(8,128)(2,1)} %get-tuple-element.121), channel_id=1, source_target_pairs={{16,0},{32,16},{48,32},{0,48},{17,1},{33,17},{49,33},{1,49},{18,2}... | collective-permute-start | bytes 786440 | tf_op jit(solution)/shard_map/ppermute | solution.py:47
  392.6 36.6 %collective-permute-start.51 = (bf16[2,128,512]{2,1,0:T(8,128)(2,1)}, bf16[2,128,512]{2,1,0:T(8,128)(2,1)}, u32[]{:S(2)}, u32[]{:S(2)}) collective-permute-start(bf16[2,128,512]{2,1,0:T(8,128)(2,1)} %get-tuple-element.122), channel_id=1, source_target_pairs={{32,0},{48,16},{0,32},{16,48},{33,1},{49,17},{1,33},{17,49},{34,2}... | collective-permute-start | bytes 786440 | tf_op jit(solution)/shard_map/ppermute | solution.py:47
  421.6 53.0 %collective-permute-start.42 = (bf16[1024,1024]{1,0:T(8,128)(2,1)}, bf16[1024,1024]{1,0:T(8,128)(2,1)}, u32[]{:S(2)}, u32[]{:S(2)}) collective-permute-start(bf16[1024,1024]{1,0:T(8,128)(2,1)} %convolution_convert_fusion), channel_id=1, source_target_pairs={{8,0},{0,8},{9,1},{1,9},{10,2},{2,10},{11,3},{3,11},{12,4},{4,12},... | collective-permute-start | bytes 6291464 | tf_op jit(solution)/shard_map/ppermute | solution.py:47
  422.8 27.0 %collective-permute-start.29 = (bf16[128,2048]{1,0:T(8,128)(2,1)}, bf16[128,2048]{1,0:T(8,128)(2,1)S(1)}, u32[]{:S(2)}, u32[]{:S(2)}) collective-permute-start(bf16[128,2048]{1,0:T(8,128)(2,1)} %get-tuple-element.110), channel_id=1, source_target_pairs={{3,0},{0,1},{1,2},{2,3},{7,4},{4,5},{5,6},{6,7},{11,8},{8,9},{9,10... | collective-permute-start | bytes 1572872 | tf_op jit(solution)/shard_map/ppermute | solution.py:47
  424.9 24.9 %collective-permute-start.31 = (bf16[128,2048]{1,0:T(8,128)(2,1)}, bf16[128,2048]{1,0:T(8,128)(2,1)}, u32[]{:S(2)}, u32[]{:S(2)}) collective-permute-start(bf16[128,2048]{1,0:T(8,128)(2,1)} %get-tuple-element.111), channel_id=1, source_target_pairs={{1,0},{2,1},{3,2},{0,3},{5,4},{6,5},{7,6},{4,7},{9,8},{10,9},{11,1... | collective-permute-start | bytes 1572872 | tf_op jit(solution)/shard_map/ppermute | solution.py:47
  426.1 23.7 %collective-permute-start.30 = (bf16[128,2048]{1,0:T(8,128)(2,1)}, bf16[128,2048]{1,0:T(8,128)(2,1)}, u32[]{:S(2)}, u32[]{:S(2)}) collective-permute-start(bf16[128,2048]{1,0:T(8,128)(2,1)} %get-tuple-element.112), channel_id=1, source_target_pairs={{2,0},{3,1},{0,2},{1,3},{6,4},{7,5},{4,6},{5,7},{10,8},{11,9},{8,1... | collective-permute-start | bytes 1572872 | tf_op jit(solution)/shard_map/ppermute | solution.py:47
  484.3 24.7 %collective-permute-start.44 = (bf16[2,128,1024]{1,2,0:T(8,128)(2,1)}, bf16[2,128,1024]{1,2,0:T(8,128)(2,1)S(1)}, u32[]{:S(2)}, u32[]{:S(2)}) collective-permute-start(bf16[2,128,1024]{1,2,0:T(8,128)(2,1)} %bitcast.333), channel_id=1, source_target_pairs={{32,0},{48,16},{0,32},{16,48},{33,1},{49,17},{1,33},{17,49},{34,2}... | collective-permute-start | bytes 1572872 | tf_op jit(solution)/shard_map/ppermute | solution.py:47
  (104 other events, 935.0 us)
Sparse Core Ops, SparseCore 0:
  275.3 79.2 reduce-scatter.1

commit v3 on v2

v3 whole, which is shorter than its diff:
```python
import functools

import jax
import jax.numpy as jnp
from jax import lax
from jax.experimental import pallas as pl
from jax.experimental.pallas import tpu as pltpu
from jax.sharding import Mesh, PartitionSpec as P

EPSILON = 1e-06
ROPE_BASE = 1000000.0
MASKED_SCORE = -1e30
HD = 128
BLK = 64
AXES = ("zl", "x", "core", "zh", "y")
SIZES = (2, 4, 2, 2, 4)
CTX = ("zl", "x", "core")
FSDP = ("zh", "y")
F32 = jnp.float32
BF16 = jnp.bfloat16


def tables(positions, head_dim):
    exponent_steps = jnp.arange(head_dim // 2, dtype=jnp.int32).astype(F32) * (2.0 / head_dim)
    frequency = ROPE_BASE ** (-exponent_steps)
    phases = positions.astype(F32)[:, None] * frequency[None, :]
    phases = jnp.concatenate([phases, phases], axis=-1)
    return (jnp.cos(phases), jnp.sin(phases))


def dot(left, right, contract=((1,), (0,))):
    return lax.dot_general(left, right, (contract, ((), ())), preferred_element_type=F32)


TILE = 256


def keep_mask(ends, first_row, rows, cols):
    place = first_row + lax.broadcasted_iota(jnp.int32, (rows, 1), 0)
    start = jnp.zeros((rows, 1), jnp.int32)
    for j in range(ends.shape[0]):
        start = jnp.where(place >= ends[j], ends[j], start)
    key = lax.broadcasted_iota(jnp.int32, (rows, cols), 1)
    return (key >= start) & (key <= place)


def attend_kernel(place, ends, core, q_in, mine, other, out, q_pos, k_pos, v_pos, log_total, out_pos):
    rows = q_in.shape[0]
    blocks = rows // BLK
    scale = HD ** (-0.5)

    @pl.when(core[0] == 0)
    def _():
        @pl.loop(0, blocks)
        def _(b):
            src = pl.ds(pl.multiple_of(b * BLK, BLK), BLK)
            dst = pl.ds(pl.multiple_of(place[b] * BLK, BLK), BLK)
            q_pos[dst, :] = q_in[src, :]
            k_pos[dst, :] = mine[src, :]
            v_pos[dst, :] = other[src, :]

    @pl.when(core[0] == 1)
    def _():
        @pl.loop(0, blocks)
        def _(b):
            src = pl.ds(pl.multiple_of(b * BLK, BLK), BLK)
            dst = pl.ds(pl.multiple_of(place[b] * BLK, BLK), BLK)
            q_pos[dst, :] = q_in[src, :]
            k_pos[dst, :] = other[src, :]
            v_pos[dst, :] = mine[src, :]

    for i in range(rows // TILE):
        span = pl.ds(i * TILE, TILE)
        n = (i + 1) * TILE
        scores = dot(q_pos[span, :], k_pos[:n, :], ((1,), (1,))) * scale
        scores = jnp.where(keep_mask(ends, i * TILE, TILE, n), scores, MASKED_SCORE)
        top = jnp.max(scores, axis=-1, keepdims=True)
        weights = jnp.exp(scores - top)
        total = jnp.sum(weights, axis=-1, keepdims=True)
        log_total[span, :] = top + jnp.log(total)
        probs = (weights * (1.0 / total)).astype(BF16)
        out_pos[span, :] = dot(probs, v_pos[:n, :]).astype(BF16)

    @pl.loop(0, blocks)
    def _(b):
        src = pl.ds(pl.multiple_of(b * BLK, BLK), BLK)
        dst = pl.ds(pl.multiple_of(place[b] * BLK, BLK), BLK)
        out[src, :] = out_pos[dst, :]


def attend_back_kernel(
    place, ends, core, grad_in, q_pos, k_pos, v_pos, log_total, q_grad, keep_grad, send_grad,
    grad_pos, q_acc, k_acc, v_acc,
):
    rows = grad_in.shape[0]
    blocks = rows // BLK
    scale = HD ** (-0.5)

    @pl.loop(0, blocks)
    def _(b):
        src = pl.ds(pl.multiple_of(b * BLK, BLK), BLK)
        dst = pl.ds(pl.multiple_of(place[b] * BLK, BLK), BLK)
        grad_pos[dst, :] = grad_in[src, :]

    k_acc[...] = jnp.zeros_like(k_acc)
    v_acc[...] = jnp.zeros_like(v_acc)
    for i in range(rows // TILE):
        span = pl.ds(i * TILE, TILE)
        n = (i + 1) * TILE
        queries = q_pos[span, :]
        grads = grad_pos[span, :]
        scores = dot(queries, k_pos[:n, :], ((1,), (1,))) * scale
        kept = keep_mask(ends, i * TILE, TILE, n)
        probs = jnp.where(kept, jnp.exp(scores - log_total[span, :]), 0.0)
        prob_grad = dot(grads, v_pos[:n, :], ((1,), (1,)))
        row_dot = jnp.sum(prob_grad * probs, axis=-1, keepdims=True)
        score_grad = (probs * (prob_grad - row_dot)).astype(BF16)
        q_acc[span, :] = (dot(score_grad, k_pos[:n, :]) * scale).astype(BF16)
        k_acc[:n, :] += dot(score_grad, queries, ((0,), (0,)))
        v_acc[:n, :] += dot(probs.astype(BF16), grads, ((0,), (0,)))

    @pl.loop(0, blocks)
    def _(b):
        src = pl.ds(pl.multiple_of(b * BLK, BLK), BLK)
        dst = pl.ds(pl.multiple_of(place[b] * BLK, BLK), BLK)
        q_grad[src, :] = q_acc[dst, :]
        k_rows = k_acc[dst, :] * scale
        v_rows = v_acc[dst, :]
        first = core[0] == 0
        keep_grad[src, :] = jnp.where(first, k_rows, v_rows)
        send_grad[src, :] = jnp.where(first, v_rows, k_rows).astype(BF16)


def attend(place, ends, core, q_in, mine, other):
    rows = q_in.shape[0]
    low = jax.ShapeDtypeStruct((rows, HD), BF16)
    smem = pl.BlockSpec(memory_space=pltpu.SMEM)
    vmem = pl.BlockSpec(memory_space=pltpu.VMEM)
    return pl.pallas_call(
        attend_kernel,
        out_shape=(low, low, low, low, jax.ShapeDtypeStruct((rows, 1), F32)),
        in_specs=[smem] * 3 + [vmem] * 3,
        out_specs=(vmem,) * 5,
        scratch_shapes=[pltpu.VMEM((rows, HD), BF16)],
        compiler_params=pltpu.CompilerParams(vmem_limit_bytes=40 * 2**20),
        cost_estimate=pl.CostEstimate(
            flops=2 * rows * rows * HD, bytes_accessed=rows * HD * 16, transcendentals=rows * rows // 2
        ),
        name="attend",
    )(place, ends, core, q_in, mine, other)


def attend_back(place, ends, core, grad_in, q_pos, k_pos, v_pos, log_total):
    rows = grad_in.shape[0]
    low = jax.ShapeDtypeStruct((rows, HD), BF16)
    smem = pl.BlockSpec(memory_space=pltpu.SMEM)
    vmem = pl.BlockSpec(memory_space=pltpu.VMEM)
    return pl.pallas_call(
        attend_back_kernel,
        out_shape=(low, jax.ShapeDtypeStruct((rows, HD), F32), low),
        in_specs=[smem] * 3 + [vmem] * 5,
        out_specs=(vmem,) * 3,
        scratch_shapes=[
            pltpu.VMEM((rows, HD), BF16),
            pltpu.VMEM((rows, HD), BF16),
            pltpu.VMEM((rows, HD), F32),
            pltpu.VMEM((rows, HD), F32),
        ],
        compiler_params=pltpu.CompilerParams(vmem_limit_bytes=48 * 2**20),
        cost_estimate=pl.CostEstimate(
            flops=5 * rows * rows * HD, bytes_accessed=rows * HD * 20, transcendentals=rows * rows // 2
        ),
        name="attend_back",
    )(place, ends, core, grad_in, q_pos, k_pos, v_pos, log_total)


def peers(pairs):
    barrier = pltpu.get_barrier_semaphore()
    for place in pairs:
        pl.semaphore_signal(barrier, inc=1, device_id=place, device_id_type=pl.DeviceIdType.MESH)
    pl.semaphore_wait(barrier, len(pairs))


def remote(src, dst, sent, landed, place):
    return pltpu.make_async_remote_copy(
        src_ref=src, dst_ref=dst, send_sem=sent, recv_sem=landed, device_id=place,
        device_id_type=pl.DeviceIdType.MESH,
    )


ROWS = 128
WIDE = 256


def ctx_at(index):
    return {"zl": index // 8, "x": lax.rem(index // 2, 4), "core": lax.rem(index, 2)}


def block(ref, index):
    return ref.at[pl.ds(pl.multiple_of(index * ROWS, ROWS), ROWS), :]


def inverse_rms(values):
    return lax.rsqrt(jnp.mean(values * values, axis=-1, keepdims=True) + EPSILON)


def rms_back(grad, values, gain):
    inverse = inverse_rms(values)
    scaled = grad * gain
    inner = jnp.mean(values * scaled, axis=-1, keepdims=True)
    back = inverse * scaled - values * (inverse * inverse * inverse * inner)
    return back, jnp.sum(grad * values * inverse, axis=0, keepdims=True)


def pre_kernel(
    tokens, cos, sin, attn_gain, q_gain, k_gain, cot_hbm, q_hbm, k_hbm, v_hbm, o_hbm,
    q_got, mine, other, raw_hbm, normed_hbm, own_hbm, par_hbm, o_par_hbm, cot_got,
    normed, w_own, w_par, o_own, o_par, raw, q_out, kv_out,
    load_sem, y_sent, y_land, cot_sent, cot_land, z_sent, z_land, x_sent, x_land, core_sent, core_land,
    q_sent, q_land, kv_sent, kv_land, swap_sem, local_sem, out_sem,
):
    zl, x, core = (lax.axis_index(a) for a in CTX)
    zh, y = (lax.axis_index(a) for a in FSDP)
    me = zl * 8 + x * 2 + core
    half = 4 * HD
    waits = []

    def along_y(k):
        return {"y": lax.rem(y + k, 4)}

    def along_x(k):
        return {"x": lax.rem(x + k, 4)}

    other_core = {"core": 1 - core}
    cross = {"zl": 1 - zl, "zh": 1 - zh}
    q_width, k_width = q_hbm.shape[1], k_hbm.shape[1]
    pieces = (
        (q_hbm, w_own.at[:, pl.ds(0, q_width)]),
        (k_hbm, w_own.at[:, pl.ds(q_width, k_width)]),
        (v_hbm, w_own.at[:, pl.ds(q_width + k_width, k_width)]),
        (o_hbm, o_own),
    )
    loads = [pltpu.make_async_copy(src, dst, load_sem.at[i]) for i, (src, dst) in enumerate(pieces)]
    for load in loads:
        load.start()
    own_cot = pltpu.make_async_copy(cot_hbm, cot_got.at[pl.ds(0, ROWS), :], local_sem.at[0])
    own_cot.start()
    rows_in = tokens[...].astype(F32)
    normed[:ROWS, :] = (rows_in * inverse_rms(rows_in) * attn_gain[...]).astype(BF16)
    peers([ctx_at(lax.rem(me + k, 16)) for k in range(1, 16)] + [along_y(k) for k in (1, 2, 3)] + [cross])

    y_copies = []
    for k in (1, 3, 2):
        copy = remote(
            normed.at[pl.ds(0, ROWS), :], normed.at[pl.ds((4 - k) * ROWS, ROWS), :], y_sent.at[k], y_land.at[4 - k],
            along_y(k),
        )
        copy.start()
        y_copies.append(copy)
    for load in loads:
        load.wait()

    def shard_stage(src, dst, first):
        eighth = src.shape[0] // 8

        def piece(ref, at_x, at_core):
            return ref.at[pl.ds(pl.multiple_of((at_x * 2 + at_core) * eighth, eighth), eighth), :]

        over_z = remote(piece(src, x, core), piece(dst, x, core), z_sent.at[first], z_land.at[first], cross)
        over_z.start()
        waits.append(over_z)

        def to_core(k):
            at_x = lax.rem(x + k, 4)
            copy = remote(
                piece(dst, at_x, core), piece(dst, at_x, core), core_sent.at[first * 4 + k],
                core_land.at[first * 4 + k], other_core,
            )
            copy.start()
            waits.append(copy)
            return copy

        def next_stage():
            over_z.wait_recv()
            copies = []
            for k in (1, 3, 2):
                copy = remote(
                    piece(dst, x, core), piece(dst, x, core), x_sent.at[first * 4 + k],
                    x_land.at[first * 4 + 4 - k], along_x(k),
                )
                copy.start()
                copies.append((4 - k, copy))
            waits.extend(copy for _, copy in copies)
            cores = [to_core(0)]

            def last_stage():
                for k, copy in copies:
                    copy.wait_recv()
                    cores.append(to_core(k))

                def finish():
                    for copy in cores:
                        copy.wait_recv()

                return finish

            return last_stage

        return next_stage

    qkv_stage = shard_stage(w_own, w_par, 0)
    o_stage = shard_stage(o_own, o_par, 1)
    qkv_stage = qkv_stage()
    o_stage = o_stage()
    qkv_stage = qkv_stage()
    o_stage = o_stage()

    for copy in y_copies:
        copy.wait_recv()
    waits.extend(y_copies)
    cot_copies = []
    for k in (1, 3, 2):
        copy = remote(
            cot_hbm, cot_got.at[pl.ds((4 - k) * ROWS, ROWS), :], cot_sent.at[k], cot_land.at[4 - k], along_y(k)
        )
        copy.start()
        cot_copies.append(copy)
    waits.extend(cot_copies)

    def prepared(value, gain):
        scaled = value * inverse_rms(value) * gain
        turned = jnp.concatenate([-scaled[:, HD // 2 :], scaled[:, : HD // 2]], axis=1)
        return (scaled * cos[...] + turned * sin[...]).astype(BF16)

    def unit_copy(src, dst, sent, landed, dest):
        return remote(block(src, dest), block(dst, me), sent.at[dest], landed.at[me], ctx_at(dest))

    def side_units(side):
        @pl.loop(0, 4)
        def _(s):
            rows = pl.ds(pl.multiple_of(s * ROWS, ROWS), ROWS)
            for g in range(2):
                at = side * half + g * HD
                unit = s * 4 + side * 2 + g
                q_out[pl.ds(pl.multiple_of(unit * ROWS, ROWS), ROWS), :] = prepared(raw[rows, at : at + HD], q_gain[...])
            at = side * half + 2 * HD
            unit = s * 4 + side * 2
            kv_out[pl.ds(pl.multiple_of(unit * ROWS, ROWS), ROWS), :] = prepared(raw[rows, at : at + HD], k_gain[...])
            kv_out[pl.ds(pl.multiple_of((unit + 1) * ROWS, ROWS), ROWS), :] = raw[rows, at + HD : at + 2 * HD].astype(BF16)

        @pl.loop(0, 8)
        def _(j):
            turn = lax.rem(me + j, 8)
            dest = (turn // 2) * 4 + side * 2 + lax.rem(turn, 2)

            @pl.when(dest != me)
            def _():
                unit_copy(kv_out, mine, kv_sent, kv_land, dest).start()
                unit_copy(q_out, q_got, q_sent, q_land, dest).start()

    raw[:, :half] = dot(normed[...], w_own[...])
    side_units(0)
    qkv_finish = qkv_stage
    qkv_finish()
    raw[:, half:] = dot(normed[...], w_par[...])
    side_units(1)
    local = [
        pltpu.make_async_copy(block(q_out, me), block(q_got, me), local_sem.at[1]),
        pltpu.make_async_copy(block(kv_out, me), block(mine, me), local_sem.at[2]),
    ]
    for copy in local:
        copy.start()
    o_finish = o_stage
    o_finish()
    outs = [
        pltpu.make_async_copy(src, dst, out_sem.at[i])
        for i, (src, dst) in enumerate(
            ((raw, raw_hbm), (normed, normed_hbm), (w_own, own_hbm), (w_par, par_hbm), (o_par, o_par_hbm))
        )
    ]
    for copy in outs:
        copy.start()

    def from_unit(src, dst, sent, landed, source):
        return remote(block(src, source), block(dst, source), sent.at[source], landed.at[source], ctx_at(source))

    local[1].wait()

    @pl.loop(0, 16)
    def _(source):
        @pl.when(source != me)
        def _():
            from_unit(kv_out, mine, kv_sent, kv_land, source).wait_recv()

    swap = remote(mine, other, swap_sem.at[0], swap_sem.at[1], other_core)
    swap.start()

    @pl.loop(0, 16)
    def _(source):
        @pl.when(source != me)
        def _():
            from_unit(q_out, q_got, q_sent, q_land, source).wait_recv()
            from_unit(q_out, q_got, q_sent, q_land, source).wait_send()
            from_unit(kv_out, mine, kv_sent, kv_land, source).wait_send()

    for copy in cot_copies:
        copy.wait_recv()
    swap.wait()
    local[0].wait()
    own_cot.wait()
    for copy in outs:
        copy.wait()
    for copy in waits:
        copy.wait_send()


def pre(tokens, cos, sin, attn_gain, q_gain, k_gain, cot, q_w, k_w, v_w, o_w):
    rows, model = tokens.shape
    wide = q_w.shape[1] + k_w.shape[1] + v_w.shape[1]
    anywhere = pl.BlockSpec(memory_space=pl.ANY)
    vmem = pl.BlockSpec(memory_space=pltpu.VMEM)
    dma = pltpu.SemaphoreType.DMA
    unit = jax.ShapeDtypeStruct((16 * rows, HD), BF16)
    return pl.pallas_call(
        pre_kernel,
        out_shape=(
            unit,
            unit,
            unit,
            jax.ShapeDtypeStruct((4 * rows, 2 * wide), F32),
            jax.ShapeDtypeStruct((4 * rows, model), BF16),
            jax.ShapeDtypeStruct((model, wide), BF16),
            jax.ShapeDtypeStruct((model, wide), BF16),
            jax.ShapeDtypeStruct(o_w.shape, BF16),
            jax.ShapeDtypeStruct((4 * rows, model), BF16),
        ),
        in_specs=[vmem] * 6 + [anywhere] * 5,
        out_specs=(anywhere,) * 9,
        scratch_shapes=[
            pltpu.VMEM((4 * rows, model), BF16),
            pltpu.VMEM((model, wide), BF16),
            pltpu.VMEM((model, wide), BF16),
            pltpu.VMEM(o_w.shape, BF16),
            pltpu.VMEM(o_w.shape, BF16),
            pltpu.VMEM((4 * rows, 2 * wide), F32),
            pltpu.VMEM((16 * rows, HD), BF16),
            pltpu.VMEM((16 * rows, HD), BF16),
            dma((4,)),
            dma((4,)),
            dma((4,)),
            dma((4,)),
            dma((4,)),
            dma((2,)),
            dma((2,)),
            dma((8,)),
            dma((8,)),
            dma((8,)),
            dma((8,)),
            dma((16,)),
            dma((16,)),
            dma((16,)),
            dma((16,)),
            dma((2,)),
            dma((3,)),
            dma((5,)),
        ],
        compiler_params=pltpu.CompilerParams(
            collective_id=3, has_side_effects=True, vmem_limit_bytes=58 * 2**20
        ),
        cost_estimate=pl.CostEstimate(
            flops=2 * 4 * rows * model * 2 * wide, bytes_accessed=24 * 2**20, transcendentals=0
        ),
        name="pre",
    )(tokens, cos, sin, attn_gain, q_gain, k_gain, cot, q_w, k_w, v_w, o_w)


def middle_kernel(
    tokens, cot, gain, att_hbm, o_own_hbm, o_par_hbm, cot_hbm, gate_hbm, up_hbm, down_hbm,
    middle, middle_grad, gain_grad, grad_got, att_out, branch_out, part_hbm, part_got, wgrad_hbm,
    att, o_own, o_par, o_parts, o_got, hid, cots, gate_w, up_w, down_w, act_grad, gu_grad, act, parts, got, z_out, z_got,
    part, stage, branch_all, att_grad,
    load_sem, att_sent, att_land, o_sent, o_land, sent, landed, sent_back, landed_back, cot_sent, cot_land,
    part_sent, part_land, branch_sent, branch_land, grad_sent, grad_land, stage_sem, out_sem, local_sem,
):
    zl, x, core = (lax.axis_index(a) for a in CTX)
    zh, y = (lax.axis_index(a) for a in FSDP)
    me = zl * 8 + x * 2 + core
    half = 4 * ROWS
    width = gate_w.shape[1]
    model = hid.shape[1]
    side = 2 * HD
    waits = []

    def along(k):
        return {"y": lax.rem(y + k, 4)}

    across = {"zh": 1 - zh}
    loads = [
        pltpu.make_async_copy(src, dst, load_sem.at[i])
        for i, (src, dst) in enumerate(
            (
                (o_own_hbm, o_own),
                (o_par_hbm, o_par),
                (cot_hbm, cots.at[pl.ds(0, half), :]),
                (down_hbm, down_w),
                (gate_hbm, gate_w),
                (up_hbm, up_w),
            )
        )
    ]
    for load in loads:
        load.start()
    peers([ctx_at(lax.rem(me + k, 16)) for k in range(1, 16)] + [along(1), along(2), along(3), across])

    def att_at(unit):
        return att.at[
            pl.ds(pl.multiple_of(unit // 4 * ROWS, ROWS), ROWS), pl.ds(pl.multiple_of(lax.rem(unit, 4) * HD, HD), HD)
        ]

    def att_copy(dest, source):
        return remote(block(att_hbm, dest), att_at(source), att_sent.at[dest], att_land.at[source], ctx_at(dest))

    @pl.loop(1, 16)
    def _(k):
        att_copy(lax.rem(me + k, 16), me).start()

    own_att = pltpu.make_async_copy(block(att_hbm, me), att_at(me), local_sem.at[0])
    own_att.start()
    cot_copy = remote(cot_hbm, cots.at[pl.ds(half, half), :], cot_sent, cot_land, across)
    cot_copy.start()
    waits.append(cot_copy)
    loads[0].wait()
    loads[1].wait()
    own_att.wait()

    @pl.loop(1, 16)
    def _(k):
        att_copy(lax.rem(me + k, 16), lax.rem(me + k, 16)).wait_recv()

    def rows_at(ref, r):
        return ref.at[pl.ds(r * ROWS, ROWS), :]

    @pl.loop(0, model // WIDE)
    def _(n):
        cols = pl.ds(pl.multiple_of(n * WIDE, WIDE), WIDE)
        total = dot(att[:, :side], o_own[:, cols]) + dot(att[:, side:], o_par[:, cols])
        o_parts[:, cols] = total.astype(BF16)

    o_copies = []
    for k in (1, 3, 2):
        copy = remote(rows_at(o_parts, k), rows_at(o_got, 4 - k), o_sent.at[k], o_land.at[4 - k], along(k))
        copy.start()
        o_copies.append(copy)
    waits.extend(o_copies)

    def grads_of_cot(first):
        rows = pl.ds(first, half)

        @pl.loop(0, width // WIDE)
        def _(n):
            cols = pl.ds(pl.multiple_of(n * WIDE, WIDE), WIDE)
            act_grad[rows, cols] = dot(cots[rows, :], down_w[cols, :], ((1,), (1,)))

    loads[2].wait()
    loads[3].wait()
    grads_of_cot(0)
    for copy in o_copies:
        copy.wait_recv()
    total = tokens[...].astype(F32) + o_parts[:ROWS, :].astype(F32)
    for k in (1, 2, 3):
        total += o_got[k * ROWS : (k + 1) * ROWS, :].astype(F32)
    middle[...] = total
    hid[:ROWS, :] = (total * inverse_rms(total) * gain[...]).astype(BF16)

    out = []
    for k in (1, 3, 2):
        out.append(remote(rows_at(hid, 0), rows_at(hid, 4 - k), sent.at[k], landed.at[4 - k], along(k)))
    out.append(remote(rows_at(hid, 0), rows_at(hid, 4), sent.at[4], landed.at[4], across))
    for copy in out:
        copy.start()
    loads[4].wait()
    loads[5].wait()
    cot_copy.wait_recv()
    grads_of_cot(half)

    out[3].wait_recv()
    on = []
    for k in (1, 3, 2):
        on.append(remote(rows_at(hid, 4), rows_at(hid, 8 - k), sent.at[4 + k], landed.at[8 - k], along(k)))
    for copy in on:
        copy.start()
    waits.extend(out + on)

    def forward(first):
        rows = pl.ds(first, half)

        @pl.loop(0, width // WIDE)
        def _(n):
            cols = pl.ds(pl.multiple_of(n * WIDE, WIDE), WIDE)
            gate = dot(hid[rows, :], gate_w[:, cols])
            up = dot(hid[rows, :], up_w[:, cols])
            sig = jax.nn.sigmoid(gate)
            silu = gate * sig
            grad = act_grad[rows, cols]
            act[rows, cols] = (silu * up).astype(BF16)
            gu_grad[rows, cols] = (grad * up * sig * (1.0 + gate * (1.0 - sig))).astype(BF16)
            gu_grad[rows, pl.ds(pl.multiple_of(width + n * WIDE, WIDE), WIDE)] = (grad * silu).astype(BF16)

    def backward(first):
        rows = pl.ds(first, half)

        @pl.loop(0, model // WIDE)
        def _(n):
            cols = pl.ds(pl.multiple_of(n * WIDE, WIDE), WIDE)
            total = dot(gu_grad[rows, :width], gate_w[cols, :], ((1,), (1,)))
            total += dot(gu_grad[rows, width:], up_w[cols, :], ((1,), (1,)))
            parts[rows, cols] = total.astype(BF16)

    for copy in out[:3]:
        copy.wait_recv()
    forward(0)
    backward(0)
    for copy in on:
        copy.wait_recv()
    forward(half)
    backward(half)
    back = {}
    for r in (4, 0):
        for k in (1, 3, 2):
            copy = remote(
                rows_at(parts, r + k), rows_at(got, r + 4 - k), sent_back.at[r + k], landed_back.at[r + 4 - k], along(k)
            )
            copy.start()
            back[r + 4 - k] = copy
    waits.extend(back.values())

    def down_part(first):
        rows = pl.ds(first, half)

        @pl.loop(0, model // WIDE)
        def _(n):
            cols = pl.ds(pl.multiple_of(n * WIDE, WIDE), WIDE)
            part[rows, cols] = dot(act[rows, :], down_w[:, cols]).astype(BF16)

    down_part(half)
    down_part(0)
    outs = [
        pltpu.make_async_copy(part.at[pl.ds(0, half), :], part_hbm, out_sem.at[0]),
        pltpu.make_async_copy(att, att_out, out_sem.at[1]),
    ]
    for copy in outs:
        copy.start()

    def stage_copy(b, n):
        rows = pl.ds(pl.multiple_of(n * WIDE, WIDE), WIDE)
        return pltpu.make_async_copy(stage.at[b], wgrad_hbm.at[rows, :], stage_sem.at[b])

    def weight_grads(begin, end):
        @pl.loop(begin, end)
        def _(m):
            for b in range(2):
                n = m * 2 + b
                cols = pl.ds(pl.multiple_of(n * WIDE, WIDE), WIDE)

                @pl.when(m > 0)
                def _():
                    stage_copy(b, n - 2).wait()

                stage[b, :, : 2 * width] = dot(hid[:, cols], gu_grad[...], ((0,), (0,))).astype(BF16)
                stage[b, :, 2 * width :] = dot(cots[:, cols], act[...], ((0,), (0,))).astype(BF16)
                stage_copy(b, n).start()

    steps = model // WIDE // 2
    weight_grads(0, steps // 2)
    for k in (1, 2, 3):
        back[4 + k].wait_recv()

    def summed(r):
        total = parts[r * ROWS : (r + 1) * ROWS, :].astype(F32)
        for k in (1, 2, 3):
            total += got[(r + k) * ROWS : (r + k + 1) * ROWS, :].astype(F32)
        return total

    z_out[...] = summed(4).astype(BF16)
    z_copy = remote(z_out, z_got, sent_back.at[0], landed_back.at[0], across)
    z_copy.start()
    waits.append(z_copy)
    weight_grads(steps // 2, steps)
    for k in (1, 2, 3):
        back[k].wait_recv()
    z_copy.wait_recv()

    rows_back, gain_sum = rms_back(summed(0) + z_got[...].astype(F32), middle[...], gain[...])
    gain_grad[...] = gain_sum
    total = cot[...].astype(F32) + rows_back
    middle_grad[...] = total
    branch_all[:ROWS, :] = total.astype(BF16)

    branch_copies = []
    for k in (1, 3, 2):
        copy = remote(
            rows_at(branch_all, 0), rows_at(branch_all, 4 - k), branch_sent.at[k], branch_land.at[4 - k], along(k)
        )
        copy.start()
        branch_copies.append(copy)
    waits.extend(branch_copies)
    part_copy = remote(part.at[pl.ds(half, half), :], part_got, part_sent, part_land, across)
    part_copy.start()
    for copy in branch_copies:
        copy.wait_recv()
    att_grad[:, :side] = dot(branch_all[...], o_own[...], ((1,), (1,))).astype(BF16)
    att_grad[:, side:] = dot(branch_all[...], o_par[...], ((1,), (1,))).astype(BF16)

    def unit_of(unit):
        return att_grad.at[
            pl.ds(pl.multiple_of(unit // 4 * ROWS, ROWS), ROWS), pl.ds(pl.multiple_of(lax.rem(unit, 4) * HD, HD), HD)
        ]

    def grad_copy(dest, source):
        return remote(unit_of(dest), block(grad_got, source), grad_sent.at[dest], grad_land.at[source], ctx_at(dest))

    @pl.loop(1, 16)
    def _(k):
        grad_copy(lax.rem(me + k, 16), me).start()

    own_grad = pltpu.make_async_copy(unit_of(me), block(grad_got, me), local_sem.at[1])
    own_grad.start()
    branch_copy = pltpu.make_async_copy(branch_all, branch_out, out_sem.at[2])
    branch_copy.start()
    outs.append(branch_copy)

    @pl.loop(1, 16)
    def _(k):
        peer = lax.rem(me + k, 16)
        grad_copy(peer, peer).wait_recv()
        grad_copy(peer, peer).wait_send()
        att_copy(peer, peer).wait_send()

    own_grad.wait()
    part_copy.wait()
    for copy in waits:
        copy.wait_send()
    for copy in outs:
        copy.wait()
    for b in range(2):
        stage_copy(b, 2 * steps - 2 + b).wait()


def middle_part(tokens, cot, gain, att, o_own, o_par, cot_half, gate_w, up_w, down_w):
    rows, model = tokens.shape
    width = gate_w.shape[1]
    anywhere = pl.BlockSpec(memory_space=pl.ANY)
    vmem = pl.BlockSpec(memory_space=pltpu.VMEM)
    dma = pltpu.SemaphoreType.DMA
    half = jax.ShapeDtypeStruct((4 * rows, model), BF16)
    low = functools.partial(pltpu.VMEM, dtype=BF16)
    return pl.pallas_call(
        middle_kernel,
        out_shape=(
            jax.ShapeDtypeStruct((rows, model), F32),
            jax.ShapeDtypeStruct((rows, model), F32),
            jax.ShapeDtypeStruct((1, model), F32),
            jax.ShapeDtypeStruct((16 * rows, HD), BF16),
            jax.ShapeDtypeStruct((4 * rows, 4 * HD), BF16),
            half,
            half,
            half,
            jax.ShapeDtypeStruct((model, 3 * width), BF16),
        ),
        in_specs=[vmem] * 3 + [anywhere] * 7,
        out_specs=(vmem,) * 3 + (anywhere,) * 6,
        scratch_shapes=[
            low((4 * rows, 4 * HD)),
            low((2 * HD, model)),
            low((2 * HD, model)),
            low((4 * rows, model)),
            low((4 * rows, model)),
            low((8 * rows, model)),
            low((8 * rows, model)),
            low((model, width)),
            low((model, width)),
            low((width, model)),
            pltpu.VMEM((8 * rows, width), F32),
            low((8 * rows, 2 * width)),
            low((8 * rows, width)),
            low((8 * rows, model)),
            low((8 * rows, model)),
            low((rows, model)),
            low((rows, model)),
            low((8 * rows, model)),
            low((2, WIDE, 3 * width)),
            low((4 * rows, model)),
            low((4 * rows, 4 * HD)),
            dma((6,)),
            dma((16,)),
            dma((16,)),
            dma((4,)),
            dma((4,)),
            dma((8,)),
            dma((8,)),
            dma((8,)),
            dma((8,)),
            dma,
            dma,
            dma,
            dma,
            dma((4,)),
            dma((4,)),
            dma((16,)),
            dma((16,)),
            dma((2,)),
            dma((3,)),
            dma((2,)),
        ],
        compiler_params=pltpu.CompilerParams(
            collective_id=1, has_side_effects=True, vmem_limit_bytes=60 * 2**20
        ),
        cost_estimate=pl.CostEstimate(
            flops=2 * 9 * 8 * rows * model * width, bytes_accessed=40 * 2**20, transcendentals=8 * rows * width
        ),
        name="middle",
    )(tokens, cot, gain, att, o_own, o_par, cot_half, gate_w, up_w, down_w)


def back_kernel(
    q_grad, keep, send, raw, cos, sin, q_gain, k_gain, tokens, middle_grad, attn_gain, mlp_gain_grad,
    middle, normed_hbm, own_hbm, par_hbm, branch_hbm, att_hbm, part_hbm, part_got_hbm,
    tokens_grad, wgrad, gains, out_rows, o_wgrad,
    normed, w_own, w_par, branch_all, att, part, part_across, out_got, swap_got, kv_out, q_got, kv_got, low, parts, y_got,
    core_out, core_got, red, x_got, z_out, z_low, z_got, o_core_out, o_core_got, o_red, o_x_got, o_z_out, o_z_low, o_z_got,
    g_out, g_got,
    load_sem, swap_sem, q_sent, q_land, kv_sent, kv_land, y_sent, y_land, out_sent, out_land,
    core_sent, core_land, x_sent, x_land, z_sent, z_land, g_sent, g_land,
):
    zl, x, core = (lax.axis_index(a) for a in CTX)
    zh, y = (lax.axis_index(a) for a in FSDP)
    me = zl * 8 + x * 2 + core
    half = 4 * HD

    def along_y(k):
        return {"y": lax.rem(y + k, 4)}

    def along_x(k):
        return {"x": lax.rem(x + k, 4)}

    def along_ctx(k):
        return ctx_at(lax.rem(me + k, 16))

    other_core = {"core": 1 - core}
    zs = {1: {"zl": 1 - zl}, 2: {"zh": 1 - zh}, 3: {"zl": 1 - zl, "zh": 1 - zh}}

    loads = [
        pltpu.make_async_copy(src, dst, load_sem.at[i])
        for i, (src, dst) in enumerate(
            (
                (part_hbm, part),
                (part_got_hbm, part_across),
                (branch_hbm, branch_all),
                (att_hbm, att),
                (normed_hbm, normed),
                (own_hbm, w_own),
                (par_hbm, w_par),
            )
        )
    ]
    for load in loads:
        load.start()
    peers([along_ctx(k) for k in range(1, 16)] + [along_y(k) for k in (1, 2, 3)] + [zs[2], zs[3]])

    swap = remote(send, swap_got, swap_sem.at[0], swap_sem.at[1], other_core)
    swap.start()

    waits = [swap]

    def to_rows(src, dst, sent, landed):
        copies = []
        for k in range(1, 16):
            copy = remote(block(src, lax.rem(me + k, 16)), block(dst, 16 - k), sent.at[k], landed.at[16 - k], along_ctx(k))
            copy.start()
            copies.append(copy)
        waits.extend(copies)
        return copies

    q_copies = to_rows(q_grad, q_got, q_sent, q_land)
    mine = pl.ds(pl.multiple_of(me * ROWS, ROWS), ROWS)
    q_got[:ROWS, :] = q_grad[mine, :]
    swap.wait_recv()
    kv_out[...] = (keep[...] + swap_got[...].astype(F32)).astype(BF16)
    kv_copies = to_rows(kv_out, kv_got, kv_sent, kv_land)
    kv_got[:ROWS, :] = kv_out[mine, :]

    loads[0].wait()
    loads[1].wait()
    part[...] = (part[...].astype(F32) + part_across[...].astype(F32)).astype(BF16)
    out_copies = []
    for k in (1, 3, 2):
        copy = remote(
            part.at[pl.ds(k * ROWS, ROWS), :], out_got.at[4 - k], out_sent.at[k], out_land.at[4 - k], along_y(k)
        )
        copy.start()
        out_copies.append(copy)
    waits.extend(out_copies)

    def grad_stages(first, tile, to_other, from_other, summed, from_x, total, total_low, from_z):
        n = total.shape[2] // 2

        def over_cores():
            @pl.loop(0, 8)
            def _(t):
                to_other[t] = tile(t * 2 + 1 - core).astype(BF16)

            copy = remote(to_other, from_other, core_sent.at[first], core_land.at[first], other_core)
            copy.start()
            waits.append(copy)
            return copy

        def over_x(core_copy):
            core_copy.wait_recv()

            @pl.loop(0, 8)
            def _(t):
                summed[t] = (tile(t * 2 + core) + from_other[t].astype(F32)).astype(BF16)

            copies = []
            for k in (1, 3, 2):
                for a in range(2):
                    copy = remote(
                        summed.at[a * 4 + lax.rem(x + k, 4)], from_x.at[4 - k, a],
                        x_sent.at[first * 8 + k * 2 + a], x_land.at[first * 8 + (4 - k) * 2 + a], along_x(k),
                    )
                    copy.start()
                    copies.append(copy)
            waits.extend(copies)
            return copies

        def over_z(x_copies):
            for copy in x_copies:
                copy.wait_recv()
            for a in range(2):
                value = summed[a * 4 + x].astype(F32)
                for k in (1, 2, 3):
                    value += from_x[k, a].astype(F32)
                total[a] = value
                total_low[a] = value.astype(BF16)
            copies = []
            for d in (1, 2, 3):
                rows_of = 1 - zl if d % 2 else zl
                copy = remote(
                    total_low.at[rows_of, :, pl.ds(n if d >= 2 else 0, n)], from_z.at[d - 1],
                    z_sent.at[first * 3 + d - 1], z_land.at[first * 3 + d - 1], zs[d],
                )
                copy.start()
                copies.append(copy)
            waits.extend(copies)
            return copies

        def finish(z_copies):
            for copy in z_copies:
                copy.wait_recv()
            value = total[zl, :, :n]
            for d in range(3):
                value = value + from_z[d].astype(F32)
            return value

        return over_cores, over_x, over_z, finish

    def tile_of(left, right):
        def tile(t):
            cols = pl.ds(pl.multiple_of(t * ROWS, ROWS), ROWS)
            return dot(left[:, cols], right[...], ((0,), (0,)))

        return tile

    qkv_cores, qkv_x, qkv_z, qkv_finish = grad_stages(
        0, tile_of(normed, low), core_out, core_got, red, x_got, z_out, z_low, z_got
    )
    o_cores, o_x, o_z, o_finish = grad_stages(
        1, tile_of(branch_all, att), o_core_out, o_core_got, o_red, o_x_got, o_z_out, o_z_low, o_z_got
    )
    loads[2].wait()
    loads[3].wait()
    o_x_copies = o_x(o_cores())
    for load in loads[4:]:
        load.wait()
    for copy in q_copies:
        copy.wait_recv()
    for copy in kv_copies:
        copy.wait_recv()

    g_out[0] = jnp.zeros_like(g_out[0])

    def from_unit(ref, unit):
        return ref[pl.ds(pl.multiple_of(lax.rem(unit - me + 16, 16) * ROWS, ROWS), ROWS), :]

    def head_back(grad, value, gain):
        turned = grad * sin[...]
        turned = jnp.concatenate([turned[:, HD // 2 :], -turned[:, : HD // 2]], axis=1)
        back, gain_sum = rms_back(grad * cos[...] + turned, value, gain)
        return back.astype(BF16), gain_sum

    @pl.loop(0, 4)
    def _(s):
        rows = pl.ds(pl.multiple_of(s * ROWS, ROWS), ROWS)
        for h in range(4):
            at = (h // 2) * half + (h % 2) * HD
            cols = slice(at, at + HD)
            grad = from_unit(q_got, s * 4 + h).astype(F32)
            back, gain_sum = head_back(grad, raw[rows, cols], q_gain[...])
            low[rows, cols] = back
            g_out[0, 32:33, :] += gain_sum
        for kv in range(2):
            at = kv * half + 2 * HD
            cols = slice(at, at + HD)
            grad = from_unit(kv_got, s * 4 + kv * 2).astype(F32)
            back, gain_sum = head_back(grad, raw[rows, cols], k_gain[...])
            low[rows, cols] = back
            g_out[0, 33:34, :] += gain_sum
            low[rows, at + HD : at + 2 * HD] = from_unit(kv_got, s * 4 + kv * 2 + 1)

    core_copy = qkv_cores()

    @pl.loop(0, parts.shape[1] // WIDE)
    def _(n):
        cols = pl.ds(pl.multiple_of(n * WIDE, WIDE), WIDE)
        total = dot(low[:, :half], w_own[cols, :], ((1,), (1,)))
        total += dot(low[:, half:], w_par[cols, :], ((1,), (1,)))
        parts[:, cols] = total.astype(BF16)

    y_copies = []
    for k in (1, 3, 2):
        copy = remote(
            parts.at[pl.ds(k * ROWS, ROWS), :], y_got.at[4 - k], y_sent.at[k], y_land.at[4 - k], along_y(k)
        )
        copy.start()
        y_copies.append(copy)
    waits.extend(y_copies)

    x_copies = qkv_x(core_copy)
    for copy in out_copies:
        copy.wait_recv()
    total = middle[...] + part[:ROWS, :].astype(F32)
    for k in (1, 2, 3):
        total += out_got[k].astype(F32)
    out_rows[...] = total.astype(BF16)
    o_z_copies = o_z(o_x_copies)

    for copy in y_copies:
        copy.wait_recv()
    grad = parts[:ROWS, :].astype(F32)
    for k in (1, 2, 3):
        grad += y_got[k].astype(F32)
    rows_back, gain_sum = rms_back(grad, tokens[...].astype(F32), attn_gain[...])
    tokens_grad[...] = (middle_grad[...] + rows_back).astype(BF16)
    for i in range(16):
        g_out[0, i : i + 1, :] = gain_sum[:, i * HD : (i + 1) * HD]
        g_out[0, 16 + i : 17 + i, :] = mlp_gain_grad[:, i * HD : (i + 1) * HD]

    def gain_stage(stage, places):
        copies = []
        for i, (place, back_slot) in enumerate(places):
            copy = remote(
                g_out.at[stage], g_got.at[stage, back_slot], g_sent.at[stage * 3 + i],
                g_land.at[stage * 3 + back_slot], place,
            )
            copy.start()
            copies.append(copy)
        waits.extend(copies)
        return copies

    def gain_sum_of(stage, copies):
        for copy in copies:
            copy.wait_recv()
        total = g_out[stage]
        for i in range(len(copies)):
            total = total + g_got[stage, i]
        return total

    copies = gain_stage(0, [(along_y(k), 3 - k) for k in (1, 2, 3)])

    z_copies = qkv_z(x_copies)
    o_wgrad[...] = o_finish(o_z_copies)
    g_out[1] = gain_sum_of(0, copies)
    copies = gain_stage(1, [(along_x(k), 3 - k) for k in (1, 2, 3)])
    g_out[2] = gain_sum_of(1, copies)
    copies = gain_stage(2, [(zs[d], d - 1) for d in (1, 2, 3)])
    wgrad[...] = qkv_finish(z_copies)
    g_out[3] = gain_sum_of(2, copies)
    copies = gain_stage(3, [(other_core, 0)])
    gains[...] = gain_sum_of(3, copies)
    for copy in waits:
        copy.wait_send()


def back(q_grad, keep, send, raw, cos, sin, q_gain, k_gain, tokens, middle_grad, attn_gain, mlp_gain_grad,
         middle, normed, w_own, w_par, branch_all, att, part, part_across):
    rows, model = tokens.shape
    wide = raw.shape[1]
    anywhere = pl.BlockSpec(memory_space=pl.ANY)
    vmem = pl.BlockSpec(memory_space=pltpu.VMEM)
    dma = pltpu.SemaphoreType.DMA
    return pl.pallas_call(
        back_kernel,
        out_shape=(
            jax.ShapeDtypeStruct((rows, model), BF16),
            jax.ShapeDtypeStruct((rows, wide // 2), F32),
            jax.ShapeDtypeStruct((40, HD), F32),
            jax.ShapeDtypeStruct((rows, model), BF16),
            jax.ShapeDtypeStruct((rows, 2 * HD), F32),
        ),
        in_specs=[vmem] * 13 + [anywhere] * 7,
        out_specs=(vmem,) * 5,
        scratch_shapes=[
            pltpu.VMEM((4 * rows, model), BF16),
            pltpu.VMEM((model, wide // 2), BF16),
            pltpu.VMEM((model, wide // 2), BF16),
            pltpu.VMEM((4 * rows, model), BF16),
            pltpu.VMEM((4 * rows, 4 * HD), BF16),
            pltpu.VMEM((4 * rows, model), BF16),
            pltpu.VMEM((4 * rows, model), BF16),
            pltpu.VMEM((4, rows, model), BF16),
            pltpu.VMEM((16 * rows, HD), BF16),
            pltpu.VMEM((16 * rows, HD), BF16),
            pltpu.VMEM((16 * rows, HD), BF16),
            pltpu.VMEM((16 * rows, HD), BF16),
            pltpu.VMEM((4 * rows, wide), BF16),
            pltpu.VMEM((4 * rows, model), BF16),
            pltpu.VMEM((4, rows, model), BF16),
            pltpu.VMEM((8, rows, wide), BF16),
            pltpu.VMEM((8, rows, wide), BF16),
            pltpu.VMEM((8, rows, wide), BF16),
            pltpu.VMEM((4, 2, rows, wide), BF16),
            pltpu.VMEM((2, rows, wide), F32),
            pltpu.VMEM((2, rows, wide), BF16),
            pltpu.VMEM((3, rows, wide // 2), BF16),
            pltpu.VMEM((8, rows, 4 * HD), BF16),
            pltpu.VMEM((8, rows, 4 * HD), BF16),
            pltpu.VMEM((8, rows, 4 * HD), BF16),
            pltpu.VMEM((4, 2, rows, 4 * HD), BF16),
            pltpu.VMEM((2, rows, 4 * HD), F32),
            pltpu.VMEM((2, rows, 4 * HD), BF16),
            pltpu.VMEM((3, rows, 2 * HD), BF16),
            pltpu.VMEM((4, 40, HD), F32),
            pltpu.VMEM((4, 3, 40, HD), F32),
            dma((7,)),
            dma((2,)),
            dma((16,)),
            dma((16,)),
            dma((16,)),
            dma((16,)),
            dma((4,)),
            dma((4,)),
            dma((4,)),
            dma((4,)),
            dma((2,)),
            dma((2,)),
            dma((16,)),
            dma((16,)),
            dma((6,)),
            dma((6,)),
            dma((12,)),
            dma((12,)),
        ],
        compiler_params=pltpu.CompilerParams(
            collective_id=2, has_side_effects=True, vmem_limit_bytes=58 * 2**20
        ),
        cost_estimate=pl.CostEstimate(
            flops=4 * 4 * rows * model * wide, bytes_accessed=24 * 2**20, transcendentals=0
        ),
        name="back",
    )(
        q_grad, keep, send, raw, cos, sin, q_gain, k_gain, tokens, middle_grad, attn_gain, mlp_gain_grad,
        middle, normed, w_own, w_par, branch_all, att, part, part_across,
    )


def per_device(
    tokens,
    cotangent,
    attn_gain,
    q_weight,
    k_weight,
    v_weight,
    q_gain,
    k_gain,
    o_weight,
    mlp_gain,
    gate_weight,
    up_weight,
    down_weight,
    doc_lengths,
    block_place,
):
    rows = tokens.shape[1]
    zl, x, core = (lax.axis_index(a) for a in CTX)
    zh, y = (lax.axis_index(a) for a in FSDP)
    ctx_place = zl * 8 + x * 2 + core
    sequence = zh * 4 + lax.rem(y + ctx_place // 4, 4)
    ends = jnp.cumsum(lax.dynamic_index_in_dim(doc_lengths, sequence, 0, keepdims=False))
    ends = ends.astype(jnp.int32)
    core_flag = core.astype(jnp.int32).reshape(1)
    own_blocks = lax.dynamic_slice_in_dim(block_place, ctx_place * (rows // BLK), rows // BLK)
    own_positions = (own_blocks[:, None] * BLK + jnp.arange(BLK, dtype=jnp.int32)[None, :]).reshape(-1)
    cos_rows, sin_rows = tables(own_positions, HD)
    q_gain, k_gain = q_gain.reshape(1, HD), k_gain.reshape(1, HD)
    attn_gain, mlp_gain = attn_gain.reshape(1, -1), mlp_gain.reshape(1, -1)
    cot = cotangent[0]

    q_in, mine, other, raw, normed, w_own, w_par, o_par, cot_half = pre(
        tokens[0], cos_rows, sin_rows, attn_gain, q_gain, k_gain, cot, q_weight, k_weight, v_weight, o_weight
    )
    out, q_pos, k_pos, v_pos, log_total = attend(block_place, ends, core_flag, q_in, mine, other)
    middle, middle_grad, mlp_gain_grad, grad_in, att, branch_all, part, part_across, mlp_wgrad = middle_part(
        tokens[0], cot, mlp_gain, out, o_weight, o_par, cot_half, gate_weight, up_weight, down_weight
    )
    mlp_wgrad = lax.psum_scatter(mlp_wgrad, CTX, scatter_dimension=0, tiled=True).astype(F32)
    width = gate_weight.shape[1]
    q_grad, keep_grad, send_grad = attend_back(
        block_place, ends, core_flag, grad_in, q_pos, k_pos, v_pos, log_total
    )
    tokens_grad, qkv_wgrad, gains, out_rows, o_wgrad = back(
        q_grad, keep_grad, send_grad, raw, cos_rows, sin_rows, q_gain, k_gain, tokens[0], middle_grad, attn_gain,
        mlp_gain_grad, middle, normed, w_own, w_par, branch_all, att, part, part_across,
    )
    return (
        out_rows[None],
        tokens_grad[None],
        gains[:16].reshape(-1),
        qkv_wgrad[:, : 2 * HD],
        qkv_wgrad[:, 2 * HD : 3 * HD],
        qkv_wgrad[:, 3 * HD :],
        gains[32],
        gains[33],
        o_wgrad.T,
        gains[16:32].reshape(-1),
        mlp_wgrad[:, :width],
        mlp_wgrad[:, width : 2 * width],
        mlp_wgrad[:, 2 * width :].T,
    )


def solution(mesh):
    fine = Mesh(mesh.devices.reshape(SIZES), AXES)
    rows = P(FSDP, CTX, None)
    in_specs = (
        rows,
        rows,
        P(),
        P(None, FSDP),
        P(None, FSDP),
        P(None, FSDP),
        P(),
        P(),
        P(FSDP, None),
        P(),
        P(None, FSDP),
        P(None, FSDP),
        P(FSDP, None),
        P(),
        P(),
    )
    out_specs = (
        rows,
        rows,
        P(),
        P(CTX, FSDP),
        P(CTX, FSDP),
        P(CTX, FSDP),
        P(),
        P(),
        P(FSDP, CTX),
        P(),
        P(CTX, FSDP),
        P(CTX, FSDP),
        P(FSDP, CTX),
    )
    return jax.shard_map(
        per_device, mesh=fine, in_specs=in_specs, out_specs=out_specs, check_vma=False
    )
```

time: 543 us -> 431 us (0.79)
  Pallas kernels: 127 us -> 386 us
  waiting for transfers between devices: 127 us -> 0.02 us
  starting transfers between devices: 99.2 us -> 0.04 us
  local copies, waits for them, and re-layouts: 93.8 us -> 19.2 us
  other arithmetic: 44.8 us -> 3.28 us
  matrix products: 25.4 us -> 0 us
    pallas_call x1 -> x3, Pallas kernels: 109 us -> 367 us  [the longest x1 204 us: middle_part(): pl.pallas_call(middle_kernel, out_shape=(jax.ShapeDtypeStruct((rows, mode...]
    ppermute x56 -> x0, waiting for transfers between devices: 114 us -> none  [the longest x45 96.1 us: from_next(): lax.ppermute(value, axis, [((i + step) % size, i) for i in range(size)])]
    ppermute x56 -> x0, starting transfers between devices: 81.1 us -> none  [the longest x45 61 us: from_next(): lax.ppermute(value, axis, [((i + step) % size, i) for i in range(size)])]
    unnamed x144 -> x30, local copies, waits for them, and re-layouts: 41.7 us -> 12.3 us
    dot_general x8 -> x0, matrix products: 25.4 us -> none  [dot(): lax.dot_general(left, right, (contract, ((), ())), preferred_element_type...]
    all_to_all x4 -> x0, starting transfers between devices: 18 us -> none  [the longest x1 5.69 us: per_device(): back = lax.all_to_all(back, CTX, 0, 0, tiled=True)]
    dynamic_slice x7 -> x0, local copies, waits for them, and re-layouts: 15.9 us -> none  [the longest x1 9.89 us: weight_grad(): lax.dynamic_index_in_dim(split, core, 2, keepdims=False)]
    all_to_all x4 -> x0, waiting for transfers between devices: 13.4 us -> none  [the longest x1 8.87 us: per_device(): attended = lax.all_to_all(out.reshape(16, rows, HD), CTX, 0, 0, tiled=True)]
  transfers between devices with their start and end apart: 61 -> 1, of which waited for: 27 -> 0; matrix products, arithmetic and copies ran while one was open for 26% -> 2% of each run, Pallas kernels for 4% -> 27%
where the time goes in v3:
time: 431 us; the launch traced here: 423 us
  Pallas kernels  386 us (90%)
  local copies, waits for them, and re-layouts  19.2 us (4%)
  between operations  14.4 us (3%)
    pallas_call x1, Pallas kernels, middle_part(): pl.pallas_call(middle_kernel, out_shape=(jax.ShapeDtypeStruct((rows, mode...  204 us
    pallas_call x1, Pallas kernels, back(): pl.pallas_call(back_kernel, out_shape=(jax.ShapeDtypeStruct((rows, model)...  104 us
    pallas_call x1, Pallas kernels, pre(): pl.pallas_call(pre_kernel, out_shape=(unit, unit, unit, jax.ShapeDtypeStr...  59.2 us
    unnamed x30, local copies, waits for them, and re-layouts  12.3 us
    pallas_call x1, Pallas kernels, attend_back(): pl.pallas_call(attend_back_kernel, out_shape=(low, jax.ShapeDtypeStruct((...  10.4 us
  transfers between devices with their start and end apart: 1, of which 0 were waited for; matrix products, arithmetic and copies ran while one was open for 2% of the time, Pallas kernels for 27%

profile of v3, /device:TPU:0, one launch (start us, length us, event | category | flops | bytes accessed | tf_op | source)
XLA Modules:
  0.0 422.9 jit_solution(119296024048959128)
XLA Ops:
  9.2 1.0 fusion
  10.2 59.2 %pre.1 = (bf16[2048,128]{1,0:T(8,128)(2,1)}, bf16[2048,128]{1,0:T(8,128)(2,1)}, bf16[2048,128]{1,0:T(8,128)(2,1)}, f32[512,1024]{1,0:T(8,128)}, bf16[512,2048]{1...) custom-call(bf16[128,2048]{1,0:T(8,128)(2,1)} %bitcast.24, ...), custom_call_target="tpu_custom_call" | custom-call | flops 2147483648 | bytes 25165824 | tf_op jit(solution)/shard_map/pre/pallas_call | solution.py:424
  69.4 1.0 copy-done.6
  70.4 1.0 copy-done.7
  71.5 1.0 copy-done.8
  72.5 8.2 %attend.1 = (bf16[2048,128]{1,0:T(8,128)(2,1)S(1)}, bf16[2048,128]{1,0:T(8,128)(2,1)S(1)}, bf16[2048,128]{1,0:T(8,128)(2,1)S(1)}, bf16[2048,128]{1,0:T(8,128)(2,1)S(1)}, f32[2048,1]{1,0:T(8,128)S(1)}) custom-call(s32[32]{0:T(128)S(1)} %copy-done.4, s32[4]{0:T(128)S(1)} %bitcast.22, s32[1]{0:T(128)} %bitcast.1.core, bf16[2048,128]{1,0:T(8,128)(2,1)S(1)} %copy-done.6, ...), custom_call_target="tpu_custom_call" | custom-call | flops 1073741824 | bytes 4194304 | tf_op jit(solution)/shard_map/attend/pallas_call | solution.py:139
  80.7 0.8 copy-done.5
  81.5 204.3 %middle.1 = (f32[128,2048]{1,0:T(8,128)}, f32[128,2048]{1,0:T(8,128)}, f32[1,2048]{1,0:T(1,128)}, bf16[2048,128]{1,0:T(8,128)(2,1)}, bf16[512,512]{1,0:T(8,128)(...) custom-call(bf16[128,2048]{1,0:T(8,128)(2,1)} %bitcast.25, ...), custom_call_target="tpu_custom_call" | custom-call | flops 28991029248 | bytes 41943040 | tf_op jit(solution)/shard_map/middle/pallas_call | solution.py:757
  285.8 1.0 copy-done.9
  286.8 10.4 %attend_back.1 = (bf16[2048,128]{1,0:T(8,128)(2,1)S(1)}, f32[2048,128]{1,0:T(8,128)S(1)}, bf16[2048,128]{1,0:T(8,128)(2,1)S(1)}) custom-call(s32[32]{0:T(128)S(1)} %copy-done.4, s32[4]{0:T(128)S(1)} %bitcast.23, s32[1]{0:T(128)} %bitcast.1.core, bf16[2048,128]{1,0:T(8,128)(2,1)S(1)} %copy-done.9, bf16[2048,128]{1,0:T(8,128)(2,1)S(1)} %get-tuple-element.51.q_pos, ...), custom_call_target="tpu_custom_call" | custom-call | flops 2684354560 | bytes 5242880 | tf_op jit(solution)/shard_map/attend_back/pallas_call | solution.py:158
  297.2 1.0 copy-done.1
  298.3 0.8 copy-done.2
  299.1 0.8 copy-done.3
  299.9 103.9 %back.1 = (bf16[128,2048]{1,0:T(8,128)(2,1)}, f32[128,512]{1,0:T(8,128)}, f32[40,128]{1,0:T(8,128)}, bf16[128,2048]{1,0:T(8,128)(2,1)}, f32[128,256]{1,0:T(8,128)}) custom-call(bf16[2048,128]{1,0:T(8,128)(2,1)} %copy-done.2, f32[2048,128]{1,0:T(8,128)} %copy-done.1, bf16[2048,128]{1,0:T(8,128)(2,1)} %copy-done.3, f32[512,1024]{1,0:T(8,128)} %get-tuple-element.58.raw, ...), custom_call_target="tpu_custom_call" | custom-call | flops 4294967296 | bytes 25165824 | tf_op jit(solution)/shard_map/back/pallas_call | solution.py:1101
  403.7 1.7 copy.28
  405.4 1.6 slice.31
  407.0 1.3 slice_bitcast_fusion.3
  408.2 1.3 slice_bitcast_fusion.1
  409.5 1.5 fusion.3
  411.1 1.2 convert_element_type.23
  412.4 0.9 copy.29
  413.3 0.9 fusion.2
  414.2 0.8 copy.32
  415.0 0.8 copy.33
  (29 shorter events, 2.0 us)
Async XLA Ops:
  7.2 0.7 copy-start
  7.2 403.9 %reduce-scatter.2.cloned.1.call-start = ((), (), s32[]{:S(2)}) async-start(), calls=%async_computation.1 | async-start | bytes 10027008 | tf_op jit(solution)/shard_map/reduce_scatter | solution.py:1215
  10.2 59.2 %copy-start.4 = (s32[32]{0:T(128)S(1)}, s32[32]{0:T(128)}, u32[]{:S(2)}) copy-start(s32[32]{0:T(128)} %place.3) | copy-start | bytes 388
  69.4 1.0 copy-start.6
  70.4 1.0 copy-start.7
  71.5 1.0 copy-start.8
  80.7 0.8 copy-start.5
  285.8 1.0 copy-start.9
  297.2 1.0 copy-start.1
  298.3 0.8 copy-start.2
  299.1 0.8 copy-start.3
  411.1 3.1 copy-start.12
  411.1 2.2 copy-start.10
  412.3 2.7 copy-start.11
Sparse Core Ops, SparseCore 0:
  285.9 112.7 reduce-scatter.1

commit v4 on v3

--- a/solution.py
+++ b/solution.py
@@ -212,6 +212,62 @@
     return back, jnp.sum(grad * values * inverse, axis=0, keepdims=True)
 
 
+def gather_ring(slot, along, sent, landed, waits, own=None):
+    def move(src, dst, i, k):
+        copy = remote(src, dst, sent.at[i], landed.at[i], along(k))
+        copy.start()
+        waits.append(copy)
+        return copy
+
+    own = slot(0) if own is None else own
+    near = [move(own, slot(1), 0, 3), move(own, slot(3), 1, 1)]
+    far = []
+
+    def pass_on():
+        for h, k in ((0, 3), (1, 1)):
+            near[h].wait_recv()
+            far.append(move(slot(1 + 2 * h, h), slot(2, h), 2 + h, k))
+
+    def finish():
+        for copy in far:
+            copy.wait_recv()
+
+    return pass_on, finish
+
+
+def scatter_ring(part, relay, got, along, sent, landed, waits):
+    def move(src, dst, i, k):
+        copy = remote(src, dst, sent.at[i], landed.at[i], along(k))
+        copy.start()
+        waits.append(copy)
+        return copy
+
+    first = [move(part(2, 0), relay(0), 0, 1), move(part(2, 1), relay(1), 1, 3)]
+    last = [move(part(1, 1), got(0, 1), 2, 1), move(part(3, 0), got(1, 0), 3, 3)]
+
+    def pass_on():
+        for h, k in ((0, 1), (1, 3)):
+            first[h].wait_recv()
+            ref = part(k, h)
+            ref[...] = (ref[...].astype(F32) + relay(h)[...].astype(F32)).astype(BF16)
+            last.append(move(ref, got(h, h), 4 + h, k))
+
+    def finish():
+        for copy in last:
+            copy.wait_recv()
+
+    return pass_on, finish
+
+
+def row_slots(ref, base=0):
+    def slot(r, h=None):
+        if h is None:
+            return ref.at[pl.ds((base + r) * ROWS, ROWS), :]
+        return ref.at[pl.ds((base + r) * ROWS + h * (ROWS // 2), ROWS // 2), :]
+
+    return slot
+
+
 def pre_kernel(
     tokens, cos, sin, attn_gain, q_gain, k_gain, cot_hbm, q_hbm, k_hbm, v_hbm, o_hbm,
     q_got, mine, other, raw_hbm, normed_hbm, own_hbm, par_hbm, o_par_hbm, cot_got,
@@ -249,14 +305,7 @@
     normed[:ROWS, :] = (rows_in * inverse_rms(rows_in) * attn_gain[...]).astype(BF16)
     peers([ctx_at(lax.rem(me + k, 16)) for k in range(1, 16)] + [along_y(k) for k in (1, 2, 3)] + [cross])
 
-    y_copies = []
-    for k in (1, 3, 2):
-        copy = remote(
-            normed.at[pl.ds(0, ROWS), :], normed.at[pl.ds((4 - k) * ROWS, ROWS), :], y_sent.at[k], y_land.at[4 - k],
-            along_y(k),
-        )
-        copy.start()
-        y_copies.append(copy)
+    normed_pass, normed_finish = gather_ring(row_slots(normed), along_y, y_sent, y_land, waits)
     for load in loads:
         load.wait()
 
@@ -308,25 +357,6 @@
 
         return next_stage
 
-    qkv_stage = shard_stage(w_own, w_par, 0)
-    o_stage = shard_stage(o_own, o_par, 1)
-    qkv_stage = qkv_stage()
-    o_stage = o_stage()
-    qkv_stage = qkv_stage()
-    o_stage = o_stage()
-
-    for copy in y_copies:
-        copy.wait_recv()
-    waits.extend(y_copies)
-    cot_copies = []
-    for k in (1, 3, 2):
-        copy = remote(
-            cot_hbm, cot_got.at[pl.ds((4 - k) * ROWS, ROWS), :], cot_sent.at[k], cot_land.at[4 - k], along_y(k)
-        )
-        copy.start()
-        cot_copies.append(copy)
-    waits.extend(cot_copies)
-
     def prepared(value, gain):
         scaled = value * inverse_rms(value) * gain
         turned = jnp.concatenate([-scaled[:, HD // 2 :], scaled[:, : HD // 2]], axis=1)
@@ -335,42 +365,52 @@
     def unit_copy(src, dst, sent, landed, dest):
         return remote(block(src, dest), block(dst, me), sent.at[dest], landed.at[me], ctx_at(dest))
 
-    def side_units(side):
-        @pl.loop(0, 4)
-        def _(s):
-            rows = pl.ds(pl.multiple_of(s * ROWS, ROWS), ROWS)
-            for g in range(2):
-                at = side * half + g * HD
-                unit = s * 4 + side * 2 + g
-                q_out[pl.ds(pl.multiple_of(unit * ROWS, ROWS), ROWS), :] = prepared(raw[rows, at : at + HD], q_gain[...])
-            at = side * half + 2 * HD
-            unit = s * 4 + side * 2
-            kv_out[pl.ds(pl.multiple_of(unit * ROWS, ROWS), ROWS), :] = prepared(raw[rows, at : at + HD], k_gain[...])
-            kv_out[pl.ds(pl.multiple_of((unit + 1) * ROWS, ROWS), ROWS), :] = raw[rows, at + HD : at + 2 * HD].astype(BF16)
-
-        @pl.loop(0, 8)
-        def _(j):
-            turn = lax.rem(me + j, 8)
-            dest = (turn // 2) * 4 + side * 2 + lax.rem(turn, 2)
+    def units(s, side):
+        rows = slice(s * ROWS, (s + 1) * ROWS)
+        unit = s * 4 + side * 2
+        for g in range(2):
+            at = side * half + g * HD
+            q_out[(unit + g) * ROWS : (unit + g + 1) * ROWS, :] = prepared(raw[rows, at : at + HD], q_gain[...])
+        at = side * half + 2 * HD
+        kv_out[unit * ROWS : (unit + 1) * ROWS, :] = prepared(raw[rows, at : at + HD], k_gain[...])
+        kv_out[(unit + 1) * ROWS : (unit + 2) * ROWS, :] = raw[rows, at + HD : at + 2 * HD].astype(BF16)
+        for g in range(2):
+            dest = unit + lax.rem(me + g, 2)
 
             @pl.when(dest != me)
             def _():
                 unit_copy(kv_out, mine, kv_sent, kv_land, dest).start()
                 unit_copy(q_out, q_got, q_sent, q_land, dest).start()
 
-    raw[:, :half] = dot(normed[...], w_own[...])
-    side_units(0)
-    qkv_finish = qkv_stage
+    def own_side(s):
+        rows = slice(s * ROWS, (s + 1) * ROWS)
+        raw[rows, :half] = dot(normed[rows, :], w_own[...])
+        units(s, 0)
+
+    qkv_stage = shard_stage(w_own, w_par, 0)
+    o_stage = shard_stage(o_own, o_par, 1)
+    own_side(0)
+    qkv_stage = qkv_stage()
+    o_stage = o_stage()
+    normed_pass()
+    cot_pass, cot_finish = gather_ring(row_slots(cot_got), along_y, cot_sent, cot_land, waits, cot_hbm)
+    own_side(1)
+    own_side(3)
+    qkv_finish = qkv_stage()
+    normed_finish()
+    own_side(2)
     qkv_finish()
     raw[:, half:] = dot(normed[...], w_par[...])
-    side_units(1)
+    for s in (2, 3, 1, 0):
+        units(s, 1)
+    o_finish = o_stage()
+    cot_pass()
     local = [
         pltpu.make_async_copy(block(q_out, me), block(q_got, me), local_sem.at[1]),
         pltpu.make_async_copy(block(kv_out, me), block(mine, me), local_sem.at[2]),
     ]
     for copy in local:
         copy.start()
-    o_finish = o_stage
     o_finish()
     outs = [
         pltpu.make_async_copy(src, dst, out_sem.at[i])
@@ -403,8 +443,7 @@
             from_unit(q_out, q_got, q_sent, q_land, source).wait_send()
             from_unit(kv_out, mine, kv_sent, kv_land, source).wait_send()
 
-    for copy in cot_copies:
-        copy.wait_recv()
+    cot_finish()
     swap.wait()
     local[0].wait()
     own_cot.wait()
@@ -476,11 +515,13 @@
 
 def middle_kernel(
     tokens, cot, gain, att_hbm, o_own_hbm, o_par_hbm, cot_hbm, gate_hbm, up_hbm, down_hbm,
-    middle, middle_grad, gain_grad, grad_got, att_out, branch_out, part_hbm, part_got, wgrad_hbm,
-    att, o_own, o_par, o_parts, o_got, hid, cots, gate_w, up_w, down_w, act_grad, gu_grad, act, parts, got, z_out, z_got,
-    part, stage, branch_all, att_grad,
-    load_sem, att_sent, att_land, o_sent, o_land, sent, landed, sent_back, landed_back, cot_sent, cot_land,
-    part_sent, part_land, branch_sent, branch_land, grad_sent, grad_land, stage_sem, out_sem, local_sem,
+    middle, middle_grad, gain_grad, gate_wgrad, up_wgrad, down_wgrad, grad_got, att_out, branch_out, part_hbm,
+    att, o_own, o_par, relay, o_got, hid, cots, gate_w, up_w, down_w, act_grad, gu_grad, act, parts, got, z_out, z_got,
+    part, stage, tiles, tile_relay, tile_got, tile_z, down_sum, branch_all, att_grad,
+    load_sem, att_sent, att_land, o_sent, o_land, hid_sent, hid_land, far_sent, far_land, across_sent, across_land,
+    near_back_sent, near_back_land, far_back_sent, far_back_land, cot_sent, cot_land, part_sent, part_land,
+    branch_sent, branch_land, grad_sent, grad_land, core_sent, core_land, x_sent, x_land, zl_sent, zl_land,
+    out_sem, local_sem,
 ):
     zl, x, core = (lax.axis_index(a) for a in CTX)
     zh, y = (lax.axis_index(a) for a in FSDP)
@@ -494,7 +535,11 @@
     def along(k):
         return {"y": lax.rem(y + k, 4)}
 
+    def along_x(k):
+        return {"x": lax.rem(x + k, 4)}
+
     across = {"zh": 1 - zh}
+    other_core = {"core": 1 - core}
     loads = [
         pltpu.make_async_copy(src, dst, load_sem.at[i])
         for i, (src, dst) in enumerate(
@@ -526,9 +571,12 @@
 
     own_att = pltpu.make_async_copy(block(att_hbm, me), att_at(me), local_sem.at[0])
     own_att.start()
-    cot_copy = remote(cot_hbm, cots.at[pl.ds(half, half), :], cot_sent, cot_land, across)
-    cot_copy.start()
-    waits.append(cot_copy)
+    cot_copies = {
+        r: remote(row_slots(cot_hbm)(r), row_slots(cots)(4 + r), cot_sent.at[r], cot_land.at[r], across) for r in range(4)
+    }
+    for r in (0, 1, 3):
+        cot_copies[r].start()
+    waits.extend(cot_copies.values())
     loads[0].wait()
     loads[1].wait()
     own_att.wait()
@@ -537,62 +585,71 @@
     def _(k):
         att_copy(lax.rem(me + k, 16), lax.rem(me + k, 16)).wait_recv()
 
-    def rows_at(ref, r):
-        return ref.at[pl.ds(r * ROWS, ROWS), :]
+    def scattered(base, got_base, relay_at, sent, landed):
+        slots = row_slots(parts, base)
+
+        def halves(ref, first):
+            return lambda r, h: row_slots(ref, first)(r, h)
+
+        def relay_half(h):
+            return relay.at[pl.ds(relay_at * ROWS + h * (ROWS // 2), ROWS // 2), :]
+
+        return scatter_ring(slots, relay_half, halves(got, got_base), along, sent, landed, waits)
+
+    def summed(base, got_base):
+        value = parts[base * ROWS : (base + 1) * ROWS, :].astype(F32)
+        for i in range(2):
+            value += got[(got_base + i) * ROWS : (got_base + i + 1) * ROWS, :].astype(F32)
+        return value
 
     @pl.loop(0, model // WIDE)
     def _(n):
         cols = pl.ds(pl.multiple_of(n * WIDE, WIDE), WIDE)
-        total = dot(att[:, :side], o_own[:, cols]) + dot(att[:, side:], o_par[:, cols])
-        o_parts[:, cols] = total.astype(BF16)
-
-    o_copies = []
-    for k in (1, 3, 2):
-        copy = remote(rows_at(o_parts, k), rows_at(o_got, 4 - k), o_sent.at[k], o_land.at[4 - k], along(k))
-        copy.start()
-        o_copies.append(copy)
-    waits.extend(o_copies)
-
-    def grads_of_cot(first):
-        rows = pl.ds(first, half)
+        value = dot(att[:, :side], o_own[:, cols]) + dot(att[:, side:], o_par[:, cols])
+        parts[pl.ds(0, half), cols] = value.astype(BF16)
+
+    o_waits = []
+    o_pass, o_finish = scatter_ring(
+        row_slots(parts),
+        lambda h: relay.at[pl.ds(h * (ROWS // 2), ROWS // 2), :],
+        lambda r, h: row_slots(o_got)(r, h),
+        along, o_sent, o_land, o_waits,
+    )
+
+    def grads_of_cot(first, count):
+        rows = pl.ds(first, count)
 
         @pl.loop(0, width // WIDE)
         def _(n):
             cols = pl.ds(pl.multiple_of(n * WIDE, WIDE), WIDE)
-            act_grad[rows, cols] = dot(cots[rows, :], down_w[cols, :], ((1,), (1,)))
+            act_grad[rows, cols] = dot(cots[rows, :], down_w[cols, :], ((1,), (1,))).astype(BF16)
 
     loads[2].wait()
     loads[3].wait()
-    grads_of_cot(0)
-    for copy in o_copies:
-        copy.wait_recv()
-    total = tokens[...].astype(F32) + o_parts[:ROWS, :].astype(F32)
-    for k in (1, 2, 3):
-        total += o_got[k * ROWS : (k + 1) * ROWS, :].astype(F32)
-    middle[...] = total
-    hid[:ROWS, :] = (total * inverse_rms(total) * gain[...]).astype(BF16)
-
-    out = []
-    for k in (1, 3, 2):
-        out.append(remote(rows_at(hid, 0), rows_at(hid, 4 - k), sent.at[k], landed.at[4 - k], along(k)))
-    out.append(remote(rows_at(hid, 0), rows_at(hid, 4), sent.at[4], landed.at[4], across))
-    for copy in out:
-        copy.start()
+    grads_of_cot(0, half)
+    o_pass()
+    o_finish()
+    value = tokens[...].astype(F32) + parts[:ROWS, :].astype(F32)
+    for i in range(2):
+        value += o_got[i * ROWS : (i + 1) * ROWS, :].astype(F32)
+    middle[...] = value
+    hid[:ROWS, :] = (value * inverse_rms(value) * gain[...]).astype(BF16)
+
+    hid_pass, hid_finish = gather_ring(row_slots(hid), along, hid_sent, hid_land, waits)
+    hid_across = remote(row_slots(hid)(0), row_slots(hid)(4), across_sent.at[0], across_land.at[0], across)
+    hid_across.start()
+    waits.append(hid_across)
     loads[4].wait()
     loads[5].wait()
-    cot_copy.wait_recv()
-    grads_of_cot(half)
-
-    out[3].wait_recv()
-    on = []
-    for k in (1, 3, 2):
-        on.append(remote(rows_at(hid, 4), rows_at(hid, 8 - k), sent.at[4 + k], landed.at[8 - k], along(k)))
-    for copy in on:
-        copy.start()
-    waits.extend(out + on)
-
-    def forward(first):
-        rows = pl.ds(first, half)
+    for copy in o_waits:
+        copy.wait_send()
+    hid_pass()
+    hid_across.wait_recv()
+    far_pass, far_finish = gather_ring(row_slots(hid, 4), along, far_sent, far_land, waits)
+    cot_copies[2].start()
+
+    def forward(first, count):
+        rows = pl.ds(first, count)
 
         @pl.loop(0, width // WIDE)
         def _(n):
@@ -601,38 +658,98 @@
             up = dot(hid[rows, :], up_w[:, cols])
             sig = jax.nn.sigmoid(gate)
             silu = gate * sig
-            grad = act_grad[rows, cols]
+            grad = act_grad[rows, cols].astype(F32)
             act[rows, cols] = (silu * up).astype(BF16)
             gu_grad[rows, cols] = (grad * up * sig * (1.0 + gate * (1.0 - sig))).astype(BF16)
             gu_grad[rows, pl.ds(pl.multiple_of(width + n * WIDE, WIDE), WIDE)] = (grad * silu).astype(BF16)
 
-    def backward(first):
-        rows = pl.ds(first, half)
+    def backward(first, count):
+        rows = pl.ds(first, count)
 
         @pl.loop(0, model // WIDE)
         def _(n):
             cols = pl.ds(pl.multiple_of(n * WIDE, WIDE), WIDE)
-            total = dot(gu_grad[rows, :width], gate_w[cols, :], ((1,), (1,)))
-            total += dot(gu_grad[rows, width:], up_w[cols, :], ((1,), (1,)))
-            parts[rows, cols] = total.astype(BF16)
-
-    for copy in out[:3]:
-        copy.wait_recv()
-    forward(0)
-    backward(0)
-    for copy in on:
-        copy.wait_recv()
-    forward(half)
-    backward(half)
-    back = {}
-    for r in (4, 0):
-        for k in (1, 3, 2):
-            copy = remote(
-                rows_at(parts, r + k), rows_at(got, r + 4 - k), sent_back.at[r + k], landed_back.at[r + 4 - k], along(k)
+            value = dot(gu_grad[rows, :width], gate_w[cols, :], ((1,), (1,)))
+            value += dot(gu_grad[rows, width:], up_w[cols, :], ((1,), (1,)))
+            parts[rows, cols] = value.astype(BF16)
+
+    forward(0, 2 * ROWS)
+    forward(3 * ROWS, ROWS)
+    hid_finish()
+    forward(2 * ROWS, ROWS)
+    cot_copies[0].wait_recv()
+    cot_copies[1].wait_recv()
+    grads_of_cot(half, 2 * ROWS)
+    cot_copies[3].wait_recv()
+    grads_of_cot(7 * ROWS, ROWS)
+    far_pass()
+    backward(0, half)
+    forward(half, 2 * ROWS)
+    forward(7 * ROWS, ROWS)
+    backward(half, 2 * ROWS)
+    backward(7 * ROWS, ROWS)
+    cot_copies[2].wait_recv()
+    grads_of_cot(6 * ROWS, ROWS)
+    far_finish()
+    forward(6 * ROWS, ROWS)
+    backward(6 * ROWS, ROWS)
+    far_back_pass, far_back_finish = scattered(4, 2, 0, far_back_sent, far_back_land)
+    near_back_pass, near_back_finish = scattered(0, 0, 1, near_back_sent, near_back_land)
+
+    def tile_pair(p, which):
+        def columns(ref):
+            return jnp.concatenate(
+                [ref[:, pl.ds(pl.multiple_of(((2 * p + i) * 2 + which) * ROWS, ROWS), ROWS)] for i in range(2)], axis=1
             )
-            copy.start()
-            back[r + 4 - k] = copy
-    waits.extend(back.values())
+
+        return dot(columns(hid), gu_grad[...], ((0,), (0,))), dot(columns(cots), act[...], ((0,), (0,)))
+
+    def pair_copy(b, p):
+        return remote(stage.at[b], tiles.at[pl.ds(2 * p, 2)], core_sent.at[p], core_land.at[p], other_core)
+
+    @pl.loop(0, 2)
+    def _(m):
+        for b in range(2):
+            p = m * 2 + b
+
+            @pl.when(m > 0)
+            def _():
+                pair_copy(b, p - 2).wait_send()
+
+            gate_up, down = tile_pair(p, 1 - core)
+            for i in range(2):
+                stage[b, i, :, : 2 * width] = gate_up[i * ROWS : (i + 1) * ROWS].astype(BF16)
+                stage[b, i, :, 2 * width :] = down[i * ROWS : (i + 1) * ROWS].astype(BF16)
+            pair_copy(b, p).start()
+
+    far_back_pass()
+
+    @pl.loop(0, 2)
+    def _(m):
+        for b in range(2):
+            p = m * 2 + b
+            gate_up, down = tile_pair(p, core)
+            pair_copy(b, p).wait_recv()
+            for i in range(2):
+                at = 2 * p + i
+                near = tiles[at]
+                value = gate_up[i * ROWS : (i + 1) * ROWS] + near[:, : 2 * width].astype(F32)
+                tiles[at, :, : 2 * width] = value.astype(BF16)
+                value = down[i * ROWS : (i + 1) * ROWS] + near[:, 2 * width :].astype(F32)
+                tiles[at, :, 2 * width :] = value.astype(BF16)
+
+    tile_pass, tile_finish = scatter_ring(
+        lambda k, h: tiles.at[h * 4 + lax.rem(x + k, 4)],
+        lambda h: tile_relay.at[h],
+        lambda r, h: tile_got.at[r, h],
+        along_x, x_sent, x_land, waits,
+    )
+    near_back_pass()
+    far_back_finish()
+    z_out[...] = summed(4, 2).astype(BF16)
+    z_copy = remote(z_out, z_got, across_sent.at[1], across_land.at[1], across)
+    z_copy.start()
+    waits.append(z_copy)
 
     def down_part(first):
         rows = pl.ds(first, half)
@@ -645,71 +762,22 @@
     down_part(half)
     down_part(0)
     outs = [
-        pltpu.make_async_copy(part.at[pl.ds(0, half), :], part_hbm, out_sem.at[0]),
+        pltpu.make_async_copy(part.at[pl.ds(half, half), :], part_hbm, out_sem.at[0]),
         pltpu.make_async_copy(att, att_out, out_sem.at[1]),
     ]
     for copy in outs:
         copy.start()
-
-    def stage_copy(b, n):
-        rows = pl.ds(pl.multiple_of(n * WIDE, WIDE), WIDE)
-        return pltpu.make_async_copy(stage.at[b], wgrad_hbm.at[rows, :], stage_sem.at[b])
-
-    def weight_grads(begin, end):
-        @pl.loop(begin, end)
-        def _(m):
-            for b in range(2):
-                n = m * 2 + b
-                cols = pl.ds(pl.multiple_of(n * WIDE, WIDE), WIDE)
-
-                @pl.when(m > 0)
-                def _():
-                    stage_copy(b, n - 2).wait()
-
-                stage[b, :, : 2 * width] = dot(hid[:, cols], gu_grad[...], ((0,), (0,))).astype(BF16)
-                stage[b, :, 2 * width :] = dot(cots[:, cols], act[...], ((0,), (0,))).astype(BF16)
-                stage_copy(b, n).start()
-
-    steps = model // WIDE // 2
-    weight_grads(0, steps // 2)
-    for k in (1, 2, 3):
-        back[4 + k].wait_recv()
-
-    def summed(r):
-        total = parts[r * ROWS : (r + 1) * ROWS, :].astype(F32)
-        for k in (1, 2, 3):
-            total += got[(r + k) * ROWS : (r + k + 1) * ROWS, :].astype(F32)
-        return total
-
-    z_out[...] = summed(4).astype(BF16)
-    z_copy = remote(z_out, z_got, sent_back.at[0], landed_back.at[0], across)
-    z_copy.start()
-    waits.append(z_copy)
-    weight_grads(steps // 2, steps)
-    for k in (1, 2, 3):
-        back[k].wait_recv()
+    tile_pass()
+    near_back_finish()
     z_copy.wait_recv()
 
-    rows_back, gain_sum = rms_back(summed(0) + z_got[...].astype(F32), middle[...], gain[...])
+    rows_back, gain_sum = rms_back(summed(0, 0) + z_got[...].astype(F32), middle[...], gain[...])
     gain_grad[...] = gain_sum
-    total = cot[...].astype(F32) + rows_back
-    middle_grad[...] = total
-    branch_all[:ROWS, :] = total.astype(BF16)
-
-    branch_copies = []
-    for k in (1, 3, 2):
-        copy = remote(
-            rows_at(branch_all, 0), rows_at(branch_all, 4 - k), branch_sent.at[k], branch_land.at[4 - k], along(k)
-        )
-        copy.start()
-        branch_copies.append(copy)
-    waits.extend(branch_copies)
-    part_copy = remote(part.at[pl.ds(half, half), :], part_got, part_sent, part_land, across)
-    part_copy.start()
-    for copy in branch_copies:
-        copy.wait_recv()
-    att_grad[:, :side] = dot(branch_all[...], o_own[...], ((1,), (1,))).astype(BF16)
-    att_grad[:, side:] = dot(branch_all[...], o_par[...], ((1,), (1,))).astype(BF16)
+    value = cot[...].astype(F32) + rows_back
+    middle_grad[...] = value
+    branch_all[:ROWS, :] = value.astype(BF16)
+
+    branch_pass, branch_finish = gather_ring(row_slots(branch_all), along, branch_sent, branch_land, waits)
 
     def unit_of(unit):
         return att_grad.at[
@@ -719,15 +787,56 @@
     def grad_copy(dest, source):
         return remote(unit_of(dest), block(grad_got, source), grad_sent.at[dest], grad_land.at[source], ctx_at(dest))
 
-    @pl.loop(1, 16)
-    def _(k):
-        grad_copy(lax.rem(me + k, 16), me).start()
-
+    def to_units(s):
+        rows = slice(s * ROWS, (s + 1) * ROWS)
+        att_grad[rows, :side] = dot(branch_all[rows, :], o_own[...], ((1,), (1,))).astype(BF16)
+        att_grad[rows, side:] = dot(branch_all[rows, :], o_par[...], ((1,), (1,))).astype(BF16)
+
+        @pl.loop(0, 4)
+        def _(j):
+            dest = s * 4 + lax.rem(me + j, 4)
+
+            @pl.when(dest != me)
+            def _():
+                grad_copy(dest, me).start()
+
+    to_units(0)
+    branch_pass()
+    to_units(1)
+    to_units(3)
+    branch_finish()
+    to_units(2)
     own_grad = pltpu.make_async_copy(unit_of(me), block(grad_got, me), local_sem.at[1])
     own_grad.start()
+    part_pass, part_finish = scatter_ring(
+        row_slots(part),
+        lambda h: relay.at[pl.ds(h * (ROWS // 2), ROWS // 2), :],
+        lambda r, h: row_slots(o_got)(r, h),
+        along, part_sent, part_land, waits,
+    )
     branch_copy = pltpu.make_async_copy(branch_all, branch_out, out_sem.at[2])
     branch_copy.start()
     outs.append(branch_copy)
+
+    tile_finish()
+
+    def tile_sum(a):
+        value = tiles[a * 4 + x].astype(F32)
+        for i in range(2):
+            value += tile_got[i, a].astype(F32)
+        return value
+
+    for b in range(2):
+        pair_copy(b, 2 + b).wait_send()
+    stage[0, 0] = tile_sum(1 - zl).astype(BF16)
+    tile_copy = remote(stage.at[0, 0], tile_z, zl_sent, zl_land, {"zl": 1 - zl})
+    tile_copy.start()
+    waits.append(tile_copy)
+    value = tile_sum(zl)
+    gate_wgrad[...] = value[:, :width]
+    up_wgrad[...] = value[:, width : 2 * width]
+    down_sum[...] = value[:, 2 * width :]
+    part_pass()
 
     @pl.loop(1, 16)
     def _(k):
@@ -736,14 +845,22 @@
         grad_copy(peer, peer).wait_send()
         att_copy(peer, peer).wait_send()
 
+    tile_copy.wait_recv()
+    gate_wgrad[...] += tile_z[:, :width].astype(F32)
+    up_wgrad[...] += tile_z[:, width : 2 * width].astype(F32)
+    down = down_sum[...] + tile_z[:, 2 * width :].astype(F32)
+    for i in range(width // HD):
+        down_wgrad[i * HD : (i + 1) * HD, :] = down[:, i * HD : (i + 1) * HD].T
     own_grad.wait()
-    part_copy.wait()
+    part_finish()
+    value = middle[...] + part[:ROWS, :].astype(F32)
+    for i in range(2):
+        value += o_got[i * ROWS : (i + 1) * ROWS, :].astype(F32)
+    middle[...] = value
     for copy in waits:
         copy.wait_send()
     for copy in outs:
         copy.wait()
-    for b in range(2):
-        stage_copy(b, 2 * steps - 2 + b).wait()
 
 
 def middle_part(tokens, cot, gain, att, o_own, o_par, cot_half, gate_w, up_w, down_w):
@@ -760,60 +877,77 @@
             jax.ShapeDtypeStruct((rows, model), F32),
             jax.ShapeDtypeStruct((rows, model), F32),
             jax.ShapeDtypeStruct((1, model), F32),
+            jax.ShapeDtypeStruct((rows, width), F32),
+            jax.ShapeDtypeStruct((rows, width), F32),
+            jax.ShapeDtypeStruct((width, rows), F32),
             jax.ShapeDtypeStruct((16 * rows, HD), BF16),
             jax.ShapeDtypeStruct((4 * rows, 4 * HD), BF16),
             half,
             half,
-            half,
-            jax.ShapeDtypeStruct((model, 3 * width), BF16),
         ),
         in_specs=[vmem] * 3 + [anywhere] * 7,
-        out_specs=(vmem,) * 3 + (anywhere,) * 6,
+        out_specs=(vmem,) * 6 + (anywhere,) * 4,
         scratch_shapes=[
             low((4 * rows, 4 * HD)),
             low((2 * HD, model)),
             low((2 * HD, model)),
-            low((4 * rows, model)),
-            low((4 * rows, model)),
+            low((2 * rows, model)),
+            low((2 * rows, model)),
             low((8 * rows, model)),
             low((8 * rows, model)),
             low((model, width)),
             low((model, width)),
             low((width, model)),
-            pltpu.VMEM((8 * rows, width), F32),
+            low((8 * rows, width)),
             low((8 * rows, 2 * width)),
             low((8 * rows, width)),
             low((8 * rows, model)),
-            low((8 * rows, model)),
+            low((4 * rows, model)),
             low((rows, model)),
             low((rows, model)),
             low((8 * rows, model)),
-            low((2, WIDE, 3 * width)),
+            low((2, 2, rows, 3 * width)),
+            low((8, rows, 3 * width)),
+            low((2, rows, 3 * width)),
+            low((2, 2, rows, 3 * width)),
+            low((rows, 3 * width)),
+            pltpu.VMEM((rows, width), F32),
             low((4 * rows, model)),
             low((4 * rows, 4 * HD)),
             dma((6,)),
+            dma((16,)),
+            dma((16,)),
+            dma((6,)),
+            dma((6,)),
+            dma((4,)),
+            dma((4,)),
+            dma((4,)),
+            dma((4,)),
+            dma((2,)),
+            dma((2,)),
+            dma((6,)),
+            dma((6,)),
+            dma((6,)),
+            dma((6,)),
+            dma((4,)),
+            dma((4,)),
+            dma((6,)),
+            dma((6,)),
+            dma((4,)),
+            dma((4,)),
             dma((16,)),
             dma((16,)),
             dma((4,)),
             dma((4,)),
-            dma((8,)),
-            dma((8,)),
-            dma((8,)),
-            dma((8,)),
+            dma((6,)),
+            dma((6,)),
             dma,
             dma,
-            dma,
-            dma,
-            dma((4,)),
-            dma((4,)),
-            dma((16,)),
-            dma((16,)),
-            dma((2,)),
             dma((3,)),
             dma((2,)),
         ],
         compiler_params=pltpu.CompilerParams(
-            collective_id=1, has_side_effects=True, vmem_limit_bytes=60 * 2**20
+            collective_id=1, has_side_effects=True, vmem_limit_bytes=63 * 2**20
         ),
         cost_estimate=pl.CostEstimate(
             flops=2 * 9 * 8 * rows * model * width, bytes_accessed=40 * 2**20, transcendentals=8 * rows * width
@@ -824,12 +958,12 @@
 
 def back_kernel(
     q_grad, keep, send, raw, cos, sin, q_gain, k_gain, tokens, middle_grad, attn_gain, mlp_gain_grad,
-    middle, normed_hbm, own_hbm, par_hbm, branch_hbm, att_hbm, part_hbm, part_got_hbm,
-    tokens_grad, wgrad, gains, out_rows, o_wgrad,
-    normed, w_own, w_par, branch_all, att, part, part_across, out_got, swap_got, kv_out, q_got, kv_got, low, parts, y_got,
-    core_out, core_got, red, x_got, z_out, z_low, z_got, o_core_out, o_core_got, o_red, o_x_got, o_z_out, o_z_low, o_z_got,
+    middle, normed_hbm, own_hbm, par_hbm, branch_hbm, att_hbm, part_hbm,
+    tokens_grad, out_rows, q_wgrad, k_wgrad, v_wgrad, o_wgrad, attn_total, mlp_total, q_total, k_total,
+    normed, w_own, w_par, branch_all, att, part, out_got, relay, out_across, swap_got, kv_out, q_got, kv_got, low, parts, y_got,
+    core_out, core_got, red, x_relay, x_got, z_out, z_low, z_got, o_core_out, o_core_got, o_red, o_x_relay, o_x_got, o_z_out, o_z_low, o_z_got,
     g_out, g_got,
-    load_sem, swap_sem, q_sent, q_land, kv_sent, kv_land, y_sent, y_land, out_sent, out_land,
+    load_sem, swap_sem, across_sem, q_sent, q_land, kv_sent, kv_land, y_sent, y_land, out_sent, out_land,
     core_sent, core_land, x_sent, x_land, z_sent, z_land, g_sent, g_land,
 ):
     zl, x, core = (lax.axis_index(a) for a in CTX)
@@ -854,7 +988,6 @@
         for i, (src, dst) in enumerate(
             (
                 (part_hbm, part),
-                (part_got_hbm, part_across),
                 (branch_hbm, branch_all),
                 (att_hbm, att),
                 (normed_hbm, normed),
@@ -890,18 +1023,14 @@
     kv_got[:ROWS, :] = kv_out[mine, :]
 
     loads[0].wait()
-    loads[1].wait()
-    part[...] = (part[...].astype(F32) + part_across[...].astype(F32)).astype(BF16)
-    out_copies = []
-    for k in (1, 3, 2):
-        copy = remote(
-            part.at[pl.ds(k * ROWS, ROWS), :], out_got.at[4 - k], out_sent.at[k], out_land.at[4 - k], along_y(k)
-        )
-        copy.start()
-        out_copies.append(copy)
-    waits.extend(out_copies)
-
-    def grad_stages(first, tile, to_other, from_other, summed, from_x, total, total_low, from_z):
+    out_pass, out_finish = scatter_ring(
+        row_slots(part),
+        lambda h: relay.at[pl.ds(h * (ROWS // 2), ROWS // 2), :],
+        lambda r, h: row_slots(out_got)(r, h),
+        along_y, out_sent, out_land, waits,
+    )
+
+    def grad_stages(first, tile, to_other, from_other, summed, x_relay, from_x, total, total_low, from_z):
         n = total.shape[2] // 2
 
         def over_cores():
@@ -921,25 +1050,19 @@
             def _(t):
                 summed[t] = (tile(t * 2 + core) + from_other[t].astype(F32)).astype(BF16)
 
-            copies = []
-            for k in (1, 3, 2):
-                for a in range(2):
-                    copy = remote(
-                        summed.at[a * 4 + lax.rem(x + k, 4)], from_x.at[4 - k, a],
-                        x_sent.at[first * 8 + k * 2 + a], x_land.at[first * 8 + (4 - k) * 2 + a], along_x(k),
-                    )
-                    copy.start()
-                    copies.append(copy)
-            waits.extend(copies)
-            return copies
-
-        def over_z(x_copies):
-            for copy in x_copies:
-                copy.wait_recv()
+            return scatter_ring(
+                lambda k, h: summed.at[h * 4 + lax.rem(x + k, 4)],
+                lambda h: x_relay.at[h],
+                lambda r, h: from_x.at[r, h],
+                along_x, x_sent.at[first], x_land.at[first], waits,
+            )
+
+        def over_z(x_finish):
+            x_finish()
             for a in range(2):
                 value = summed[a * 4 + x].astype(F32)
-                for k in (1, 2, 3):
-                    value += from_x[k, a].astype(F32)
+                for i in range(2):
+                    value += from_x[i, a].astype(F32)
                 total[a] = value
                 total_low[a] = value.astype(BF16)
             copies = []
@@ -972,15 +1095,16 @@
         return tile
 
     qkv_cores, qkv_x, qkv_z, qkv_finish = grad_stages(
-        0, tile_of(normed, low), core_out, core_got, red, x_got, z_out, z_low, z_got
+        0, tile_of(normed, low), core_out, core_got, red, x_relay, x_got, z_out, z_low, z_got
     )
     o_cores, o_x, o_z, o_finish = grad_stages(
-        1, tile_of(branch_all, att), o_core_out, o_core_got, o_red, o_x_got, o_z_out, o_z_low, o_z_got
-    )
+        1, tile_of(branch_all, att), o_core_out, o_core_got, o_red, o_x_relay, o_x_got, o_z_out, o_z_low, o_z_got
+    )
+    loads[1].wait()
     loads[2].wait()
-    loads[3].wait()
-    o_x_copies = o_x(o_cores())
-    for load in loads[4:]:
+    o_x_pass, o_x_finish = o_x(o_cores())
+    out_pass()
+    for load in loads[3:]:
         load.wait()
     for copy in q_copies:
         copy.wait_recv()
@@ -1018,6 +1142,14 @@
             low[rows, at + HD : at + 2 * HD] = from_unit(kv_got, s * 4 + kv * 2 + 1)
 
     core_copy = qkv_cores()
+    out_finish()
+    value = part[:ROWS, :].astype(F32)
+    for i in range(2):
+        value += out_got[i * ROWS : (i + 1) * ROWS, :].astype(F32)
+    part[:ROWS, :] = value.astype(BF16)
+    across_copy = remote(part.at[pl.ds(0, ROWS), :], out_across, across_sem.at[0], across_sem.at[1], zs[2])
+    across_copy.start()
+    waits.append(across_copy)
 
     @pl.loop(0, parts.shape[1] // WIDE)
     def _(n):
@@ -1026,29 +1158,25 @@
         total += dot(low[:, half:], w_par[cols, :], ((1,), (1,)))
         parts[:, cols] = total.astype(BF16)
 
-    y_copies = []
-    for k in (1, 3, 2):
-        copy = remote(
-            parts.at[pl.ds(k * ROWS, ROWS), :], y_got.at[4 - k], y_sent.at[k], y_land.at[4 - k], along_y(k)
-        )
-        copy.start()
-        y_copies.append(copy)
-    waits.extend(y_copies)
-
-    x_copies = qkv_x(core_copy)
-    for copy in out_copies:
-        copy.wait_recv()
-    total = middle[...] + part[:ROWS, :].astype(F32)
-    for k in (1, 2, 3):
-        total += out_got[k].astype(F32)
-    out_rows[...] = total.astype(BF16)
-    o_z_copies = o_z(o_x_copies)
-
-    for copy in y_copies:
-        copy.wait_recv()
+    o_x_pass()
+    y_pass, y_finish = scatter_ring(
+        row_slots(parts),
+        lambda h: relay.at[pl.ds(ROWS + h * (ROWS // 2), ROWS // 2), :],
+        lambda r, h: row_slots(y_got)(r, h),
+        along_y, y_sent, y_land, waits,
+    )
+
+    x_pass, x_finish = qkv_x(core_copy)
+    y_pass()
+    x_pass()
+    o_z_copies = o_z(o_x_finish)
+
+    across_copy.wait_recv()
+    out_rows[...] = (middle[...] + out_across[...].astype(F32)).astype(BF16)
+    y_finish()
     grad = parts[:ROWS, :].astype(F32)
-    for k in (1, 2, 3):
-        grad += y_got[k].astype(F32)
+    for i in range(2):
+        grad += y_got[i * ROWS : (i + 1) * ROWS, :].astype(F32)
     rows_back, gain_sum = rms_back(grad, tokens[...].astype(F32), attn_gain[...])
     tokens_grad[...] = (middle_grad[...] + rows_back).astype(BF16)
     for i in range(16):
@@ -1077,22 +1205,32 @@
 
     copies = gain_stage(0, [(along_y(k), 3 - k) for k in (1, 2, 3)])
 
-    z_copies = qkv_z(x_copies)
-    o_wgrad[...] = o_finish(o_z_copies)
+    z_copies = qkv_z(x_finish)
+    value = o_finish(o_z_copies)
+    for i in range(2):
+        o_wgrad[i * HD : (i + 1) * HD, :] = value[:, i * HD : (i + 1) * HD].T
     g_out[1] = gain_sum_of(0, copies)
     copies = gain_stage(1, [(along_x(k), 3 - k) for k in (1, 2, 3)])
     g_out[2] = gain_sum_of(1, copies)
     copies = gain_stage(2, [(zs[d], d - 1) for d in (1, 2, 3)])
-    wgrad[...] = qkv_finish(z_copies)
+    value = qkv_finish(z_copies)
+    q_wgrad[...] = value[:, : 2 * HD]
+    k_wgrad[...] = value[:, 2 * HD : 3 * HD]
+    v_wgrad[...] = value[:, 3 * HD :]
     g_out[3] = gain_sum_of(2, copies)
     copies = gain_stage(3, [(other_core, 0)])
-    gains[...] = gain_sum_of(3, copies)
+    gains = gain_sum_of(3, copies)
+    for i in range(16):
+        attn_total[:, i * HD : (i + 1) * HD] = gains[i : i + 1, :]
+        mlp_total[:, i * HD : (i + 1) * HD] = gains[16 + i : 17 + i, :]
+    q_total[...] = gains[32:33, :]
+    k_total[...] = gains[33:34, :]
     for copy in waits:
         copy.wait_send()
 
 
 def back(q_grad, keep, send, raw, cos, sin, q_gain, k_gain, tokens, middle_grad, attn_gain, mlp_gain_grad,
-         middle, normed, w_own, w_par, branch_all, att, part, part_across):
+         middle, normed, w_own, w_par, branch_all, att, part):
     rows, model = tokens.shape
     wide = raw.shape[1]
     anywhere = pl.BlockSpec(memory_space=pl.ANY)
@@ -1102,13 +1240,18 @@
         back_kernel,
         out_shape=(
             jax.ShapeDtypeStruct((rows, model), BF16),
-            jax.ShapeDtypeStruct((rows, wide // 2), F32),
-            jax.ShapeDtypeStruct((40, HD), F32),
             jax.ShapeDtypeStruct((rows, model), BF16),
             jax.ShapeDtypeStruct((rows, 2 * HD), F32),
+            jax.ShapeDtypeStruct((rows, HD), F32),
+            jax.ShapeDtypeStruct((rows, HD), F32),
+            jax.ShapeDtypeStruct((2 * HD, rows), F32),
+            jax.ShapeDtypeStruct((1, model), F32),
+            jax.ShapeDtypeStruct((1, model), F32),
+            jax.ShapeDtypeStruct((1, HD), F32),
+            jax.ShapeDtypeStruct((1, HD), F32),
         ),
-        in_specs=[vmem] * 13 + [anywhere] * 7,
-        out_specs=(vmem,) * 5,
+        in_specs=[vmem] * 13 + [anywhere] * 6,
+        out_specs=(vmem,) * 10,
         scratch_shapes=[
             pltpu.VMEM((4 * rows, model), BF16),
             pltpu.VMEM((model, wide // 2), BF16),
@@ -1116,45 +1259,49 @@
             pltpu.VMEM((4 * rows, model), BF16),
             pltpu.VMEM((4 * rows, 4 * HD), BF16),
             pltpu.VMEM((4 * rows, model), BF16),
-            pltpu.VMEM((4 * rows, model), BF16),
-            pltpu.VMEM((4, rows, model), BF16),
+            pltpu.VMEM((2 * rows, model), BF16),
+            pltpu.VMEM((2 * rows, model), BF16),
+            pltpu.VMEM((rows, model), BF16),
             pltpu.VMEM((16 * rows, HD), BF16),
             pltpu.VMEM((16 * rows, HD), BF16),
             pltpu.VMEM((16 * rows, HD), BF16),
             pltpu.VMEM((16 * rows, HD), BF16),
             pltpu.VMEM((4 * rows, wide), BF16),
             pltpu.VMEM((4 * rows, model), BF16),
-            pltpu.VMEM((4, rows, model), BF16),
+            pltpu.VMEM((2 * rows, model), BF16),
             pltpu.VMEM((8, rows, wide), BF16),
             pltpu.VMEM((8, rows, wide), BF16),
             pltpu.VMEM((8, rows, wide), BF16),
-            pltpu.VMEM((4, 2, rows, wide), BF16),
+            pltpu.VMEM((2, rows, wide), BF16),
+            pltpu.VMEM((2, 2, rows, wide), BF16),
             pltpu.VMEM((2, rows, wide), F32),
             pltpu.VMEM((2, rows, wide), BF16),
             pltpu.VMEM((3, rows, wide // 2), BF16),
             pltpu.VMEM((8, rows, 4 * HD), BF16),
             pltpu.VMEM((8, rows, 4 * HD), BF16),
             pltpu.VMEM((8, rows, 4 * HD), BF16),
-            pltpu.VMEM((4, 2, rows, 4 * HD), BF16),
+            pltpu.VMEM((2, rows, 4 * HD), BF16),
+            pltpu.VMEM((2, 2, rows, 4 * HD), BF16),
             pltpu.VMEM((2, rows, 4 * HD), F32),
             pltpu.VMEM((2, rows, 4 * HD), BF16),
             pltpu.VMEM((3, rows, 2 * HD), BF16),
             pltpu.VMEM((4, 40, HD), F32),
             pltpu.VMEM((4, 3, 40, HD), F32),
-            dma((7,)),
+            dma((6,)),
+            dma((2,)),
             dma((2,)),
             dma((16,)),
             dma((16,)),
             dma((16,)),
             dma((16,)),
-            dma((4,)),
-            dma((4,)),
-            dma((4,)),
-            dma((4,)),
+            dma((6,)),
+            dma((6,)),
+            dma((6,)),
+            dma((6,)),
             dma((2,)),
             dma((2,)),
-            dma((16,)),
-            dma((16,)),
+            dma((2, 6)),
+            dma((2, 6)),
             dma((6,)),
             dma((6,)),
             dma((12,)),
@@ -1169,7 +1316,7 @@
         name="back",
     )(
         q_grad, keep, send, raw, cos, sin, q_gain, k_gain, tokens, middle_grad, attn_gain, mlp_gain_grad,
-        middle, normed, w_own, w_par, branch_all, att, part, part_across,
+        middle, normed, w_own, w_par, branch_all, att, part,
     )
 
 
@@ -1209,32 +1356,32 @@
         tokens[0], cos_rows, sin_rows, attn_gain, q_gain, k_gain, cot, q_weight, k_weight, v_weight, o_weight
     )
     out, q_pos, k_pos, v_pos, log_total = attend(block_place, ends, core_flag, q_in, mine, other)
-    middle, middle_grad, mlp_gain_grad, grad_in, att, branch_all, part, part_across, mlp_wgrad = middle_part(
-        tokens[0], cot, mlp_gain, out, o_weight, o_par, cot_half, gate_weight, up_weight, down_weight
-    )
-    mlp_wgrad = lax.psum_scatter(mlp_wgrad, CTX, scatter_dimension=0, tiled=True).astype(F32)
-    width = gate_weight.shape[1]
+    (
+        middle, middle_grad, mlp_gain_grad, gate_wgrad, up_wgrad, down_wgrad, grad_in, att, branch_all, part,
+    ) = middle_part(tokens[0], cot, mlp_gain, out, o_weight, o_par, cot_half, gate_weight, up_weight, down_weight)
     q_grad, keep_grad, send_grad = attend_back(
         block_place, ends, core_flag, grad_in, q_pos, k_pos, v_pos, log_total
     )
-    tokens_grad, qkv_wgrad, gains, out_rows, o_wgrad = back(
+    (
+        tokens_grad, out_rows, q_wgrad, k_wgrad, v_wgrad, o_wgrad, attn_gain_grad, mlp_gain_grad, q_gain_grad, k_gain_grad,
+    ) = back(
         q_grad, keep_grad, send_grad, raw, cos_rows, sin_rows, q_gain, k_gain, tokens[0], middle_grad, attn_gain,
-        mlp_gain_grad, middle, normed, w_own, w_par, branch_all, att, part, part_across,
+        mlp_gain_grad, middle, normed, w_own, w_par, branch_all, att, part,
     )
     return (
         out_rows[None],
         tokens_grad[None],
-        gains[:16].reshape(-1),
-        qkv_wgrad[:, : 2 * HD],
-        qkv_wgrad[:, 2 * HD : 3 * HD],
-        qkv_wgrad[:, 3 * HD :],
-        gains[32],
-        gains[33],
-        o_wgrad.T,
-        gains[16:32].reshape(-1),
-        mlp_wgrad[:, :width],
-        mlp_wgrad[:, width : 2 * width],
-        mlp_wgrad[:, 2 * width :].T,
+        attn_gain_grad[0],
+        q_wgrad,
+        k_wgrad,
+        v_wgrad,
+        q_gain_grad[0],
+        k_gain_grad[0],
+        o_wgrad,
+        mlp_gain_grad[0],
+        gate_wgrad,
+        up_wgrad,
+        down_wgrad,
     )
 
 

time: 431 us -> 349 us (0.81)
  the two profiles are of different devices: /device:TPU:0 before, /device:TPU:1 now
where the time goes in v4:
time: 349 us; the launch traced here: 343 us
  Pallas kernels  315 us (90%)
  local copies, waits for them, and re-layouts  24.6 us (7%)
    pallas_call x1, Pallas kernels, middle_part(): pl.pallas_call(middle_kernel, out_shape=(jax.ShapeDtypeStruct((rows, mode...  178 us
    pallas_call x1, Pallas kernels, back(): pl.pallas_call(back_kernel, out_shape=(jax.ShapeDtypeStruct((rows, model)...  69.8 us
    pallas_call x1, Pallas kernels, pre(): pl.pallas_call(pre_kernel, out_shape=(unit, unit, unit, jax.ShapeDtypeStr...  49.6 us
    unnamed x67, local copies, waits for them, and re-layouts  24.4 us
    pallas_call x1, Pallas kernels, attend_back(): pl.pallas_call(attend_back_kernel, out_shape=(low, jax.ShapeDtypeStruct((...  10.2 us
    pallas_call x1, Pallas kernels, attend(): pl.pallas_call(attend_kernel, out_shape=(low, low, low, low, jax.ShapeDty...  7.88 us

profile of v4, /device:TPU:1, one launch (start us, length us, event | category | flops | bytes accessed | tf_op | source)
XLA Modules:
  0.0 343.3 jit_solution(1441410230162642335)
XLA Ops:
  2.1 1.0 fusion
  3.0 49.6 %pre.1 = (bf16[2048,128]{1,0:T(8,128)(2,1)}, bf16[2048,128]{1,0:T(8,128)(2,1)}, bf16[2048,128]{1,0:T(8,128)(2,1)}, f32[512,1024]{1,0:T(8,128)}, bf16[512,2048]{1...) custom-call(bf16[128,2048]{1,0:T(8,128)(2,1)} %bitcast.19, ...), custom_call_target="tpu_custom_call" | custom-call | flops 2147483648 | bytes 25165824 | tf_op jit(solution)/shard_map/pre/pallas_call | solution.py:463
  52.7 1.0 copy-done.12
  53.7 1.0 copy-done.13
  54.8 1.0 copy-done.14
  55.8 7.9 %attend.1 = (bf16[2048,128]{1,0:T(8,128)(2,1)S(1)}, bf16[2048,128]{1,0:T(8,128)(2,1)S(1)}, bf16[2048,128]{1,0:T(8,128)(2,1)S(1)}, bf16[2048,128]{1,0:T(8,128)(2,1)S(1)}, f32[2048,1]{1,0:T(8,128)S(1)}) custom-call(s32[32]{0:T(128)S(1)} %copy-done.4, s32[4]{0:T(128)S(1)} %bitcast.15, s32[1]{0:T(128)} %bitcast.1.core, bf16[2048,128]{1,0:T(8,128)(2,1)S(1)} %copy-done.12, ...), custom_call_target="tpu_custom_call" | custom-call | flops 1073741824 | bytes 4194304 | tf_op jit(solution)/shard_map/attend/pallas_call | solution.py:139
  63.7 0.9 copy-done.5
  64.7 0.8 copy-done.7
  65.5 0.8 copy-done.9
  66.3 0.8 copy-done.11
  67.0 177.9 %middle.1 = (f32[128,2048]{1,0:T(8,128)}, f32[128,2048]{1,0:T(8,128)}, f32[1,2048]{1,0:T(1,128)}, f32[128,768]{1,0:T(8,128)}, f32[128,768]{1,0:T(8,128)}, /*inde...) custom-call(bf16[128,2048]{1,0:T(8,128)(2,1)} %bitcast.20, ...), custom_call_target="tpu_custom_call" | custom-call | flops 28991029248 | bytes 41943040 | tf_op jit(solution)/shard_map/middle/pallas_call | solution.py:874
  244.9 1.2 copy-done.6
  246.2 1.0 copy-done.8
  247.2 1.0 copy-done.10
  248.2 1.0 copy-done.15
  249.3 10.2 %attend_back.1 = (bf16[2048,128]{1,0:T(8,128)(2,1)S(1)}, f32[2048,128]{1,0:T(8,128)S(1)}, bf16[2048,128]{1,0:T(8,128)(2,1)S(1)}) custom-call(s32[32]{0:T(128)S(1)} %copy-done.4, s32[4]{0:T(128)S(1)} %bitcast.16, s32[1]{0:T(128)} %bitcast.1.core, bf16[2048,128]{1,0:T(8,128)(2,1)S(1)} %copy-done.15, bf16[2048,128]{1,0:T(8,128)(2,1)S(1)} %get-tuple-element.57.q_pos, ...), custom_call_target="tpu_custom_call" | custom-call | flops 2684354560 | bytes 5242880 | tf_op jit(solution)/shard_map/attend_back/pallas_call | solution.py:158
  259.5 1.0 copy-done.1
  260.5 0.8 copy-done.2
  261.3 0.8 copy-done.3
  262.1 69.8 %back.1 = (bf16[128,2048]{1,0:T(8,128)(2,1)}, bf16[128,2048]{1,0:T(8,128)(2,1)}, f32[128,256]{1,0:T(8,128)}, f32[128,128]{1,0:T(8,128)}, f32[128,128]{1,0:T(8,12...) custom-call(bf16[2048,128]{1,0:T(8,128)(2,1)} %copy-done.2, ...), custom_call_target="tpu_custom_call" | custom-call | flops 4294967296 | bytes 25165824 | tf_op jit(solution)/shard_map/back/pallas_call | solution.py:1239
  332.1 2.0 copy.41
  334.1 1.9 copy.42
  340.8 0.7 copy.51
  342.3 0.7 copy.53
  (56 shorter events, 7.0 us)
Async XLA Ops:
  3.0 49.7 %copy-start.4 = (s32[32]{0:T(128)S(1)}, s32[32]{0:T(128)}, u32[]{:S(2)}) copy-start(s32[32]{0:T(128)} %place.3) | copy-start | bytes 388
  52.7 1.0 copy-start.12
  53.7 1.0 copy-start.13
  54.8 1.0 copy-start.14
  63.7 1.0 copy-start.5
  64.7 0.8 copy-start.7
  65.5 0.8 copy-start.9
  66.2 0.8 copy-start.11
  244.9 1.2 copy-start.6
  246.2 1.0 copy-start.8
  247.2 1.0 copy-start.10
  248.2 1.0 copy-start.15
  259.5 1.0 copy-start.1
  332.0 4.0 %copy-start.24 = (f32[1,2048]{1,0:T(1,128)S(1)}, f32[1,2048]{1,0:T(1,128)}, u32[]{:S(2)}) copy-start(f32[1,2048]{1,0:T(1,128)} %get-tuple-element.76) | copy-start | bytes 24580
  332.0 4.6 %copy-start.20 = (f32[128,256]{1,0:T(8,128)S(1)}, f32[128,256]{1,0:T(8,128)}, u32[]{:S(2)}) copy-start(f32[128,256]{1,0:T(8,128)} %get-tuple-element.105) | copy-start | bytes 393220
  332.0 5.3 %copy-start.22 = (f32[128,128]{1,0:T(8,128)S(1)}, f32[128,128]{1,0:T(8,128)}, u32[]{:S(2)}) copy-start(f32[128,128]{1,0:T(8,128)} %get-tuple-element.106) | copy-start | bytes 196612
  332.0 5.9 %copy-start.21 = (f32[128,128]{1,0:T(8,128)S(1)}, f32[128,128]{1,0:T(8,128)}, u32[]{:S(2)}) copy-start(f32[128,128]{1,0:T(8,128)} %get-tuple-element.107) | copy-start | bytes 196612
  332.0 6.5 %copy-start.26 = (f32[1,128]{1,0:T(1,128)S(1)}, f32[1,128]{1,0:T(1,128)}, u32[]{:S(2)}) copy-start(f32[1,128]{1,0:T(1,128)} %get-tuple-element.80) | copy-start | bytes 1540
  332.0 7.0 %copy-start.25 = (f32[1,128]{1,0:T(1,128)S(1)}, f32[1,128]{1,0:T(1,128)}, u32[]{:S(2)}) copy-start(f32[1,128]{1,0:T(1,128)} %get-tuple-element.81) | copy-start | bytes 1540
  332.0 7.5 %copy-start.19 = (f32[256,128]{1,0:T(8,128)S(1)}, f32[256,128]{1,0:T(8,128)}, u32[]{:S(2)}) copy-start(f32[256,128]{1,0:T(8,128)} %get-tuple-element.110) | copy-start | bytes 393220
  332.1 8.2 %copy-start.23 = (f32[1,2048]{1,0:T(1,128)S(1)}, f32[1,2048]{1,0:T(1,128)}, u32[]{:S(2)}) copy-start(f32[1,2048]{1,0:T(1,128)} %get-tuple-element.83) | copy-start | bytes 24580
  332.1 8.8 %copy-start.18 = (f32[128,768]{1,0:T(8,128)S(1)}, f32[128,768]{1,0:T(8,128)}, u32[]{:S(2)}) copy-start(f32[128,768]{1,0:T(8,128)} %get-tuple-element.112) | copy-start | bytes 1179652
  332.1 9.5 %copy-start.17 = (f32[128,768]{1,0:T(8,128)S(1)}, f32[128,768]{1,0:T(8,128)}, u32[]{:S(2)}) copy-start(f32[128,768]{1,0:T(8,128)} %get-tuple-element.113) | copy-start | bytes 1179652
  332.1 10.2 %copy-start.16 = (f32[768,128]{1,0:T(8,128)S(1)}, f32[768,128]{1,0:T(8,128)}, u32[]{:S(2)}) copy-start(f32[768,128]{1,0:T(8,128)} %get-tuple-element.114) | copy-start | bytes 1179652
  (3 other events, 2.4 us)

commit v5 on v4

--- a/solution.py
+++ b/solution.py
@@ -38,73 +38,39 @@
 def keep_mask(ends, first_row, rows, cols):
     place = first_row + lax.broadcasted_iota(jnp.int32, (rows, 1), 0)
     start = jnp.zeros((rows, 1), jnp.int32)
-    for j in range(ends.shape[0]):
-        start = jnp.where(place >= ends[j], ends[j], start)
+    for end in ends:
+        start = jnp.where(place >= end, end, start)
     key = lax.broadcasted_iota(jnp.int32, (rows, cols), 1)
     return (key >= start) & (key <= place)
 
 
-def attend_kernel(place, ends, core, q_in, mine, other, out, q_pos, k_pos, v_pos, log_total, out_pos):
-    rows = q_in.shape[0]
-    blocks = rows // BLK
-    scale = HD ** (-0.5)
-
-    @pl.when(core[0] == 0)
-    def _():
-        @pl.loop(0, blocks)
-        def _(b):
-            src = pl.ds(pl.multiple_of(b * BLK, BLK), BLK)
-            dst = pl.ds(pl.multiple_of(place[b] * BLK, BLK), BLK)
-            q_pos[dst, :] = q_in[src, :]
-            k_pos[dst, :] = mine[src, :]
-            v_pos[dst, :] = other[src, :]
-
-    @pl.when(core[0] == 1)
-    def _():
-        @pl.loop(0, blocks)
-        def _(b):
-            src = pl.ds(pl.multiple_of(b * BLK, BLK), BLK)
-            dst = pl.ds(pl.multiple_of(place[b] * BLK, BLK), BLK)
-            q_pos[dst, :] = q_in[src, :]
-            k_pos[dst, :] = other[src, :]
-            v_pos[dst, :] = mine[src, :]
-
-    for i in range(rows // TILE):
+def ordered(order, blocks, pairs):
+    @pl.loop(0, blocks)
+    def _(b):
+        rows = pl.ds(pl.multiple_of(b * BLK, BLK), BLK)
+        for src, dst in pairs:
+            dst[rows, :] = src[order[b]]
+
+
+def attend(ends, q_pos, k_pos, v_pos, out_pos, log_total):
+    for i in range(q_pos.shape[0] // TILE):
         span = pl.ds(i * TILE, TILE)
         n = (i + 1) * TILE
-        scores = dot(q_pos[span, :], k_pos[:n, :], ((1,), (1,))) * scale
+        scores = dot(q_pos[span, :], k_pos[:n, :], ((1,), (1,))) * HD ** (-0.5)
         scores = jnp.where(keep_mask(ends, i * TILE, TILE, n), scores, MASKED_SCORE)
         top = jnp.max(scores, axis=-1, keepdims=True)
         weights = jnp.exp(scores - top)
         total = jnp.sum(weights, axis=-1, keepdims=True)
         log_total[span, :] = top + jnp.log(total)
         probs = (weights * (1.0 / total)).astype(BF16)
-        out_pos[span, :] = dot(probs, v_pos[:n, :]).astype(BF16)
-
-    @pl.loop(0, blocks)
-    def _(b):
-        src = pl.ds(pl.multiple_of(b * BLK, BLK), BLK)
-        dst = pl.ds(pl.multiple_of(place[b] * BLK, BLK), BLK)
-        out[src, :] = out_pos[dst, :]
-
-
-def attend_back_kernel(
-    place, ends, core, grad_in, q_pos, k_pos, v_pos, log_total, q_grad, keep_grad, send_grad,
-    grad_pos, q_acc, k_acc, v_acc,
-):
-    rows = grad_in.shape[0]
-    blocks = rows // BLK
+        out_pos[i * TILE // BLK : n // BLK] = dot(probs, v_pos[:n, :]).astype(BF16).reshape(TILE // BLK, BLK, HD)
+
+
+def attend_back(ends, q_pos, k_pos, v_pos, log_total, grad_pos, q_acc, k_acc, v_acc):
     scale = HD ** (-0.5)
-
-    @pl.loop(0, blocks)
-    def _(b):
-        src = pl.ds(pl.multiple_of(b * BLK, BLK), BLK)
-        dst = pl.ds(pl.multiple_of(place[b] * BLK, BLK), BLK)
-        grad_pos[dst, :] = grad_in[src, :]
-
     k_acc[...] = jnp.zeros_like(k_acc)
     v_acc[...] = jnp.zeros_like(v_acc)
-    for i in range(rows // TILE):
+    for i in range(q_pos.shape[0] // TILE):
         span = pl.ds(i * TILE, TILE)
         n = (i + 1) * TILE
         queries = q_pos[span, :]
@@ -115,63 +81,17 @@
         prob_grad = dot(grads, v_pos[:n, :], ((1,), (1,)))
         row_dot = jnp.sum(prob_grad * probs, axis=-1, keepdims=True)
         score_grad = (probs * (prob_grad - row_dot)).astype(BF16)
-        q_acc[span, :] = (dot(score_grad, k_pos[:n, :]) * scale).astype(BF16)
-        k_acc[:n, :] += dot(score_grad, queries, ((0,), (0,)))
-        v_acc[:n, :] += dot(probs.astype(BF16), grads, ((0,), (0,)))
-
-    @pl.loop(0, blocks)
-    def _(b):
-        src = pl.ds(pl.multiple_of(b * BLK, BLK), BLK)
-        dst = pl.ds(pl.multiple_of(place[b] * BLK, BLK), BLK)
-        q_grad[src, :] = q_acc[dst, :]
-        k_rows = k_acc[dst, :] * scale
-        v_rows = v_acc[dst, :]
-        first = core[0] == 0
-        keep_grad[src, :] = jnp.where(first, k_rows, v_rows)
-        send_grad[src, :] = jnp.where(first, v_rows, k_rows).astype(BF16)
-
-
-def attend(place, ends, core, q_in, mine, other):
-    rows = q_in.shape[0]
-    low = jax.ShapeDtypeStruct((rows, HD), BF16)
-    smem = pl.BlockSpec(memory_space=pltpu.SMEM)
-    vmem = pl.BlockSpec(memory_space=pltpu.VMEM)
-    return pl.pallas_call(
-        attend_kernel,
-        out_shape=(low, low, low, low, jax.ShapeDtypeStruct((rows, 1), F32)),
-        in_specs=[smem] * 3 + [vmem] * 3,
-        out_specs=(vmem,) * 5,
-        scratch_shapes=[pltpu.VMEM((rows, HD), BF16)],
-        compiler_params=pltpu.CompilerParams(vmem_limit_bytes=40 * 2**20),
-        cost_estimate=pl.CostEstimate(
-            flops=2 * rows * rows * HD, bytes_accessed=rows * HD * 16, transcendentals=rows * rows // 2
-        ),
-        name="attend",
-    )(place, ends, core, q_in, mine, other)
-
-
-def attend_back(place, ends, core, grad_in, q_pos, k_pos, v_pos, log_total):
-    rows = grad_in.shape[0]
-    low = jax.ShapeDtypeStruct((rows, HD), BF16)
-    smem = pl.BlockSpec(memory_space=pltpu.SMEM)
-    vmem = pl.BlockSpec(memory_space=pltpu.VMEM)
-    return pl.pallas_call(
-        attend_back_kernel,
-        out_shape=(low, jax.ShapeDtypeStruct((rows, HD), F32), low),
-        in_specs=[smem] * 3 + [vmem] * 5,
-        out_specs=(vmem,) * 3,
-        scratch_shapes=[
-            pltpu.VMEM((rows, HD), BF16),
-            pltpu.VMEM((rows, HD), BF16),
-            pltpu.VMEM((rows, HD), F32),
-            pltpu.VMEM((rows, HD), F32),
-        ],
-        compiler_params=pltpu.CompilerParams(vmem_limit_bytes=48 * 2**20),
-        cost_estimate=pl.CostEstimate(
-            flops=5 * rows * rows * HD, bytes_accessed=rows * HD * 20, transcendentals=rows * rows // 2
-        ),
-        name="attend_back",
-    )(place, ends, core, grad_in, q_pos, k_pos, v_pos, log_total)
+        q_rows = (dot(score_grad, k_pos[:n, :]) * scale).astype(BF16)
+        q_acc[i * TILE // BLK : n // BLK] = q_rows.reshape(TILE // BLK, BLK, HD)
+        k_acc[: n // BLK] += dot(score_grad, queries, ((0,), (0,))).reshape(n // BLK, BLK, HD)
+        v_acc[: n // BLK] += dot(probs.astype(BF16), grads, ((0,), (0,))).reshape(n // BLK, BLK, HD)
+
+
+def document_ends(doc_lengths, sequence):
+    ends = [doc_lengths[sequence, 0]]
+    for j in range(1, doc_lengths.shape[1]):
+        ends.append(ends[-1] + doc_lengths[sequence, j])
+    return ends
 
 
 def peers(pairs):
@@ -198,6 +118,10 @@
 
 def block(ref, index):
     return ref.at[pl.ds(pl.multiple_of(index * ROWS, ROWS), ROWS), :]
+
+
+def pair(ref, index):
+    return ref.at[pl.ds(index * 2, 2)]
 
 
 def inverse_rms(values):
@@ -269,9 +193,9 @@
 
 
 def pre_kernel(
-    tokens, cos, sin, attn_gain, q_gain, k_gain, cot_hbm, q_hbm, k_hbm, v_hbm, o_hbm,
-    q_got, mine, other, raw_hbm, normed_hbm, own_hbm, par_hbm, o_par_hbm, cot_got,
-    normed, w_own, w_par, o_own, o_par, raw, q_out, kv_out,
+    place, stored, doc_lengths, tokens, cos, sin, attn_gain, q_gain, k_gain, cot_hbm, q_hbm, k_hbm, v_hbm, o_hbm,
+    log_total, out_hbm, q_hbm_out, k_hbm_out, v_hbm_out, raw_hbm, normed_hbm, own_hbm, par_hbm, o_par_hbm, cot_got,
+    q_got, mine, other, q_pos, k_pos, v_pos, out_pos, out, normed, w_own, w_par, o_own, o_par, raw, q_out, kv_out,
     load_sem, y_sent, y_land, cot_sent, cot_land, z_sent, z_land, x_sent, x_land, core_sent, core_land,
     q_sent, q_land, kv_sent, kv_land, swap_sem, local_sem, out_sem,
 ):
@@ -363,17 +287,20 @@
         return (scaled * cos[...] + turned * sin[...]).astype(BF16)
 
     def unit_copy(src, dst, sent, landed, dest):
-        return remote(block(src, dest), block(dst, me), sent.at[dest], landed.at[me], ctx_at(dest))
+        return remote(pair(src, dest), pair(dst, me), sent.at[dest], landed.at[me], ctx_at(dest))
+
+    def put(ref, unit, value):
+        ref[unit * 2 : unit * 2 + 2] = value.reshape(2, BLK, HD)
 
     def units(s, side):
         rows = slice(s * ROWS, (s + 1) * ROWS)
         unit = s * 4 + side * 2
         for g in range(2):
             at = side * half + g * HD
-            q_out[(unit + g) * ROWS : (unit + g + 1) * ROWS, :] = prepared(raw[rows, at : at + HD], q_gain[...])
+            put(q_out, unit + g, prepared(raw[rows, at : at + HD], q_gain[...]))
         at = side * half + 2 * HD
-        kv_out[unit * ROWS : (unit + 1) * ROWS, :] = prepared(raw[rows, at : at + HD], k_gain[...])
-        kv_out[(unit + 1) * ROWS : (unit + 2) * ROWS, :] = raw[rows, at + HD : at + 2 * HD].astype(BF16)
+        put(kv_out, unit, prepared(raw[rows, at : at + HD], k_gain[...]))
+        put(kv_out, unit + 1, raw[rows, at + HD : at + 2 * HD].astype(BF16))
         for g in range(2):
             dest = unit + lax.rem(me + g, 2)
 
@@ -404,10 +331,9 @@
     for s in (2, 3, 1, 0):
         units(s, 1)
     o_finish = o_stage()
-    cot_pass()
     local = [
-        pltpu.make_async_copy(block(q_out, me), block(q_got, me), local_sem.at[1]),
-        pltpu.make_async_copy(block(kv_out, me), block(mine, me), local_sem.at[2]),
+        pltpu.make_async_copy(pair(q_out, me), pair(q_got, me), local_sem.at[1]),
+        pltpu.make_async_copy(pair(kv_out, me), pair(mine, me), local_sem.at[2]),
     ]
     for copy in local:
         copy.start()
@@ -422,7 +348,7 @@
         copy.start()
 
     def from_unit(src, dst, sent, landed, source):
-        return remote(block(src, source), block(dst, source), sent.at[source], landed.at[source], ctx_at(source))
+        return remote(pair(src, source), pair(dst, source), sent.at[source], landed.at[source], ctx_at(source))
 
     local[1].wait()
 
@@ -443,9 +369,34 @@
             from_unit(q_out, q_got, q_sent, q_land, source).wait_send()
             from_unit(kv_out, mine, kv_sent, kv_land, source).wait_send()
 
-    cot_finish()
     swap.wait()
     local[0].wait()
+    cot_pass()
+
+    blocks = q_pos.shape[0] // BLK
+
+    @pl.when(core == 0)
+    def _():
+        ordered(stored, blocks, ((q_got, q_pos), (mine, k_pos), (other, v_pos)))
+
+    @pl.when(core == 1)
+    def _():
+        ordered(stored, blocks, ((q_got, q_pos), (other, k_pos), (mine, v_pos)))
+
+    more = [
+        pltpu.make_async_copy(src, dst, out_sem.at[5 + i])
+        for i, (src, dst) in enumerate(((q_pos, q_hbm_out), (k_pos, k_hbm_out), (v_pos, v_hbm_out)))
+    ]
+    for copy in more:
+        copy.start()
+    outs.extend(more)
+    ends = document_ends(doc_lengths, zh * 4 + lax.rem(y + me // 4, 4))
+    attend(ends, q_pos, k_pos, v_pos, out_pos, log_total)
+    ordered(place, blocks, ((out_pos, out),))
+    out_copy = pltpu.make_async_copy(out, out_hbm, out_sem.at[8])
+    out_copy.start()
+    outs.append(out_copy)
+    cot_finish()
     own_cot.wait()
     for copy in outs:
         copy.wait()
@@ -453,7 +404,7 @@
         copy.wait_send()
 
 
-def pre(tokens, cos, sin, attn_gain, q_gain, k_gain, cot, q_w, k_w, v_w, o_w):
+def pre(place, stored, doc_lengths, tokens, cos, sin, attn_gain, q_gain, k_gain, cot, q_w, k_w, v_w, o_w):
     rows, model = tokens.shape
     wide = q_w.shape[1] + k_w.shape[1] + v_w.shape[1]
     anywhere = pl.BlockSpec(memory_space=pl.ANY)
@@ -463,6 +414,8 @@
     return pl.pallas_call(
         pre_kernel,
         out_shape=(
+            jax.ShapeDtypeStruct((16 * rows, 1), F32),
+            unit,
             unit,
             unit,
             unit,
@@ -473,17 +426,20 @@
             jax.ShapeDtypeStruct(o_w.shape, BF16),
             jax.ShapeDtypeStruct((4 * rows, model), BF16),
         ),
-        in_specs=[vmem] * 6 + [anywhere] * 5,
-        out_specs=(anywhere,) * 9,
-        scratch_shapes=[
+        in_specs=[pl.BlockSpec(memory_space=pltpu.SMEM)] * 3 + [vmem] * 6 + [anywhere] * 5,
+        out_specs=(vmem,) + (anywhere,) * 10,
+        scratch_shapes=[pltpu.VMEM((16 * rows // BLK, BLK, HD), BF16)] * 3
+        + [pltpu.VMEM((16 * rows, HD), BF16)] * 3
+        + [pltpu.VMEM((16 * rows // BLK, BLK, HD), BF16), pltpu.VMEM((16 * rows, HD), BF16)]
+        + [
             pltpu.VMEM((4 * rows, model), BF16),
             pltpu.VMEM((model, wide), BF16),
             pltpu.VMEM((model, wide), BF16),
             pltpu.VMEM(o_w.shape, BF16),
             pltpu.VMEM(o_w.shape, BF16),
             pltpu.VMEM((4 * rows, 2 * wide), F32),
-            pltpu.VMEM((16 * rows, HD), BF16),
-            pltpu.VMEM((16 * rows, HD), BF16),
+            pltpu.VMEM((16 * rows // BLK, BLK, HD), BF16),
+            pltpu.VMEM((16 * rows // BLK, BLK, HD), BF16),
             dma((4,)),
             dma((4,)),
             dma((4,)),
@@ -501,7 +457,7 @@
             dma((16,)),
             dma((2,)),
             dma((3,)),
-            dma((5,)),
+            dma((9,)),
         ],
         compiler_params=pltpu.CompilerParams(
             collective_id=3, has_side_effects=True, vmem_limit_bytes=58 * 2**20
@@ -510,18 +466,18 @@
             flops=2 * 4 * rows * model * 2 * wide, bytes_accessed=24 * 2**20, transcendentals=0
         ),
         name="pre",
-    )(tokens, cos, sin, attn_gain, q_gain, k_gain, cot, q_w, k_w, v_w, o_w)
+    )(place, stored, doc_lengths, tokens, cos, sin, attn_gain, q_gain, k_gain, cot, q_w, k_w, v_w, o_w)
 
 
 def middle_kernel(
     tokens, cot, gain, att_hbm, o_own_hbm, o_par_hbm, cot_hbm, gate_hbm, up_hbm, down_hbm,
-    middle, middle_grad, gain_grad, gate_wgrad, up_wgrad, down_wgrad, grad_got, att_out, branch_out, part_hbm,
+    middle, middle_grad, gain_grad, gate_wgrad, up_wgrad, down_wgrad, grad_got, att_out, branch, part_hbm, o_full,
     att, o_own, o_par, relay, o_got, hid, cots, gate_w, up_w, down_w, act_grad, gu_grad, act, parts, got, z_out, z_got,
-    part, stage, tiles, tile_relay, tile_got, tile_z, down_sum, branch_all, att_grad,
+    part, stage, tiles, tile_relay, tile_got, tile_z, down_sum, att_grad,
     load_sem, att_sent, att_land, o_sent, o_land, hid_sent, hid_land, far_sent, far_land, across_sent, across_land,
     near_back_sent, near_back_land, far_back_sent, far_back_land, cot_sent, cot_land, part_sent, part_land,
-    branch_sent, branch_land, grad_sent, grad_land, core_sent, core_land, x_sent, x_land, zl_sent, zl_land,
-    out_sem, local_sem,
+    oy_sent, oy_land, ox_sent, ox_land, oc_sent, oc_land, grad_sent, grad_land, core_sent, core_land, x_sent, x_land, zl_sent, zl_land,
+    out_sem, local_sem, oload_sem,
 ):
     zl, x, core = (lax.axis_index(a) for a in CTX)
     zh, y = (lax.axis_index(a) for a in FSDP)
@@ -555,7 +511,19 @@
     ]
     for load in loads:
         load.start()
-    peers([ctx_at(lax.rem(me + k, 16)) for k in range(1, 16)] + [along(1), along(2), along(3), across])
+    barrier = pltpu.get_barrier_semaphore()
+    places = [ctx_at(lax.rem(me + k, 16)) for k in range(1, 16)] + [along(1), along(2), along(3), across]
+    for place in places:
+        pl.semaphore_signal(barrier, inc=1, device_id=place, device_id_type=pl.DeviceIdType.MESH)
+
+    @pl.when(me >= 4)
+    def _():
+        @pl.loop(0, 16)
+        def _(k):
+            place = dict(ctx_at(lax.rem(me + k, 16)), **along(me // 4))
+            pl.semaphore_signal(barrier, inc=1, device_id=place, device_id_type=pl.DeviceIdType.MESH)
+
+    pl.semaphore_wait(barrier, len(places) + 12)
 
     def att_at(unit):
         return att.at[
@@ -571,12 +539,57 @@
 
     own_att = pltpu.make_async_copy(block(att_hbm, me), att_at(me), local_sem.at[0])
     own_att.start()
-    cot_copies = {
-        r: remote(row_slots(cot_hbm)(r), row_slots(cots)(4 + r), cot_sent.at[r], cot_land.at[r], across) for r in range(4)
-    }
-    for r in (0, 1, 3):
-        cot_copies[r].start()
-    waits.extend(cot_copies.values())
+    cot_copies = [
+        remote(row_slots(cot_hbm)(r), row_slots(cots)(4 + r), cot_sent.at[r], cot_land.at[r], across) for r in range(4)
+    ]
+    cot_copies[0].start()
+    cot_copies[1].start()
+    waits.extend(cot_copies)
+
+    def o_rows(k, h, at, count):
+        return o_full.at[pl.ds(pl.multiple_of(k * half + h * side + at, 16), count), :]
+
+    piece = core * HD + x * (ROWS // 4)
+    oy_rings = []
+    for h, src in ((0, o_own_hbm), (1, o_par_hbm)):
+
+        def slot(k, part_of=None, h=h):
+            if part_of is None:
+                return o_rows(k, h, piece, ROWS // 4)
+            return o_rows(k, h, piece + part_of * (ROWS // 8), ROWS // 8)
+
+        own_piece = src.at[pl.ds(pl.multiple_of(piece, ROWS // 4), ROWS // 4), :]
+        oy_rings.append(gather_ring(slot, along, oy_sent.at[h], oy_land.at[h], waits, own_piece))
+
+    def ox_move(k, h, at_x, i, to):
+        ref = o_rows(k, h, core * HD + at_x * (ROWS // 4), ROWS // 4)
+        copy = remote(ref, ref, ox_sent.at[i, k - 1, h], ox_land.at[i, k - 1, h], along_x(to))
+        copy.start()
+        waits.append(copy)
+        return copy
+
+    def ox_start():
+        return [ox_move(k, h, x, i, to) for k in (1, 2, 3) for h in (0, 1) for i, to in ((0, 3), (1, 1))]
+
+    def ox_pass(near):
+        for copy in near:
+            copy.wait_recv()
+        far = [ox_move(k, 0, lax.rem(x + 1, 4), 2, 3) for k in (1, 2, 3)]
+        return far + [ox_move(k, 1, lax.rem(x + 3, 4), 2, 1) for k in (1, 2, 3)]
+
+    def o_cores(far):
+        for copy in far:
+            copy.wait_recv()
+        copies = []
+        for k in (1, 2, 3):
+            for h in (0, 1):
+                ref = o_rows(k, h, core * HD, HD)
+                copy = remote(ref, ref, oc_sent.at[k - 1, h], oc_land.at[k - 1, h], other_core)
+                copy.start()
+                copies.append(copy)
+        waits.extend(copies)
+        return copies
+
     loads[0].wait()
     loads[1].wait()
     own_att.wait()
@@ -584,6 +597,9 @@
     @pl.loop(1, 16)
     def _(k):
         att_copy(lax.rem(me + k, 16), lax.rem(me + k, 16)).wait_recv()
+
+    for ring_pass, _ in oy_rings:
+        ring_pass()
 
     def scattered(base, got_base, relay_at, sent, landed):
         slots = row_slots(parts, base)
@@ -624,6 +640,9 @@
             cols = pl.ds(pl.multiple_of(n * WIDE, WIDE), WIDE)
             act_grad[rows, cols] = dot(cots[rows, :], down_w[cols, :], ((1,), (1,))).astype(BF16)
 
+    for _, ring_finish in oy_rings:
+        ring_finish()
+    o_near = ox_start()
     loads[2].wait()
     loads[3].wait()
     grads_of_cot(0, half)
@@ -635,17 +654,19 @@
     middle[...] = value
     hid[:ROWS, :] = (value * inverse_rms(value) * gain[...]).astype(BF16)
 
-    hid_pass, hid_finish = gather_ring(row_slots(hid), along, hid_sent, hid_land, waits)
+    hid_waits = []
+    hid_pass, hid_finish = gather_ring(row_slots(hid), along, hid_sent, hid_land, hid_waits)
     hid_across = remote(row_slots(hid)(0), row_slots(hid)(4), across_sent.at[0], across_land.at[0], across)
     hid_across.start()
-    waits.append(hid_across)
+    hid_waits.append(hid_across)
     loads[4].wait()
     loads[5].wait()
     for copy in o_waits:
         copy.wait_send()
     hid_pass()
     hid_across.wait_recv()
-    far_pass, far_finish = gather_ring(row_slots(hid, 4), along, far_sent, far_land, waits)
+    far_pass, far_finish = gather_ring(row_slots(hid, 4), along, far_sent, far_land, hid_waits)
+    cot_copies[3].start()
     cot_copies[2].start()
 
     def forward(first, count):
@@ -677,17 +698,19 @@
     forward(3 * ROWS, ROWS)
     hid_finish()
     forward(2 * ROWS, ROWS)
+    o_far = ox_pass(o_near)
     cot_copies[0].wait_recv()
     cot_copies[1].wait_recv()
     grads_of_cot(half, 2 * ROWS)
-    cot_copies[3].wait_recv()
-    grads_of_cot(7 * ROWS, ROWS)
     far_pass()
     backward(0, half)
     forward(half, 2 * ROWS)
+    cot_copies[3].wait_recv()
+    grads_of_cot(7 * ROWS, ROWS)
     forward(7 * ROWS, ROWS)
     backward(half, 2 * ROWS)
     backward(7 * ROWS, ROWS)
+    o_core_copies = o_cores(o_far)
     cot_copies[2].wait_recv()
     grads_of_cot(6 * ROWS, ROWS)
     far_finish()
@@ -759,14 +782,30 @@
             cols = pl.ds(pl.multiple_of(n * WIDE, WIDE), WIDE)
             part[rows, cols] = dot(act[rows, :], down_w[:, cols]).astype(BF16)
 
+    for copy in o_core_copies:
+        copy.wait_recv()
+    for copy in hid_waits:
+        copy.wait_send()
+    o_loads = [
+        pltpu.make_async_copy(o_full.at[pl.ds(k * half, half), :], ref.at[pl.ds(first, half), :], oload_sem.at[k - 1])
+        for k, ref, first in ((1, cots, 0), (2, cots, half), (3, hid, 0))
+    ]
+    for load in o_loads:
+        load.start()
+    down_part(0)
     down_part(half)
-    down_part(0)
     outs = [
         pltpu.make_async_copy(part.at[pl.ds(half, half), :], part_hbm, out_sem.at[0]),
         pltpu.make_async_copy(att, att_out, out_sem.at[1]),
     ]
     for copy in outs:
         copy.start()
+    part_pass, part_finish = scatter_ring(
+        row_slots(part),
+        lambda h: relay.at[pl.ds(2 * ROWS + h * (ROWS // 2), ROWS // 2), :],
+        lambda r, h: row_slots(o_got)(r, h),
+        along, part_sent, part_land, waits,
+    )
     tile_pass()
     near_back_finish()
     z_copy.wait_recv()
@@ -775,48 +814,39 @@
     gain_grad[...] = gain_sum
     value = cot[...].astype(F32) + rows_back
     middle_grad[...] = value
-    branch_all[:ROWS, :] = value.astype(BF16)
-
-    branch_pass, branch_finish = gather_ring(row_slots(branch_all), along, branch_sent, branch_land, waits)
-
-    def unit_of(unit):
-        return att_grad.at[
-            pl.ds(pl.multiple_of(unit // 4 * ROWS, ROWS), ROWS), pl.ds(pl.multiple_of(lax.rem(unit, 4) * HD, HD), HD)
-        ]
-
-    def grad_copy(dest, source):
-        return remote(unit_of(dest), block(grad_got, source), grad_sent.at[dest], grad_land.at[source], ctx_at(dest))
-
-    def to_units(s):
-        rows = slice(s * ROWS, (s + 1) * ROWS)
-        att_grad[rows, :side] = dot(branch_all[rows, :], o_own[...], ((1,), (1,))).astype(BF16)
-        att_grad[rows, side:] = dot(branch_all[rows, :], o_par[...], ((1,), (1,))).astype(BF16)
+    branch[...] = value.astype(BF16)
+
+    def unit_copy(k, h):
+        unit = (4 - k) % 4 * 4 + h
+        place = dict(ctx_at(unit), **along(k))
+        cols = pl.ds(pl.multiple_of((k * 4 + h) * HD, HD), HD)
+        return remote(att_grad.at[:, cols], block(grad_got, me), grad_sent.at[k * 4 + h], grad_land.at[me], place)
+
+    for k in range(4):
+        at = k * 4 * HD
+        if k == 0:
+            att_grad[:, :side] = dot(branch[...], o_own[...], ((1,), (1,))).astype(BF16)
+            att_grad[:, side : 2 * side] = dot(branch[...], o_par[...], ((1,), (1,))).astype(BF16)
+        else:
+            o_loads[k - 1].wait()
+            rows_of = (cots[:half, :], cots[half:, :], hid[:half, :])[k - 1]
+            att_grad[:, at : at + 4 * HD] = dot(branch[...], rows_of, ((1,), (1,))).astype(BF16)
 
         @pl.loop(0, 4)
         def _(j):
-            dest = s * 4 + lax.rem(me + j, 4)
-
-            @pl.when(dest != me)
+            h = lax.rem(me + j, 4)
+
+            @pl.when((k > 0) | (h != me))
             def _():
-                grad_copy(dest, me).start()
-
-    to_units(0)
-    branch_pass()
-    to_units(1)
-    to_units(3)
-    branch_finish()
-    to_units(2)
-    own_grad = pltpu.make_async_copy(unit_of(me), block(grad_got, me), local_sem.at[1])
-    own_grad.start()
-    part_pass, part_finish = scatter_ring(
-        row_slots(part),
-        lambda h: relay.at[pl.ds(h * (ROWS // 2), ROWS // 2), :],
-        lambda r, h: row_slots(o_got)(r, h),
-        along, part_sent, part_land, waits,
-    )
-    branch_copy = pltpu.make_async_copy(branch_all, branch_out, out_sem.at[2])
-    branch_copy.start()
-    outs.append(branch_copy)
+                unit_copy(k, h).start()
+
+    def own_grad():
+        cols = pl.ds(pl.multiple_of(lax.rem(me, 4) * HD, HD), HD)
+        return pltpu.make_async_copy(att_grad.at[:, cols], block(grad_got, me), local_sem.at[1])
+
+    @pl.when(me < 4)
+    def _():
+        own_grad().start()
 
     tile_finish()
 
@@ -841,9 +871,28 @@
     @pl.loop(1, 16)
     def _(k):
         peer = lax.rem(me + k, 16)
-        grad_copy(peer, peer).wait_recv()
-        grad_copy(peer, peer).wait_send()
         att_copy(peer, peer).wait_send()
+
+    @pl.loop(0, 16)
+    def _(source):
+        @pl.when((me >= 4) | (source != me))
+        def _():
+            remote(
+                att_grad.at[:, pl.ds(0, HD)], block(grad_got, source), grad_sent.at[0], grad_land.at[source], other_core
+            ).wait_recv()
+
+    for k in range(4):
+
+        @pl.loop(0, 4)
+        def _(h):
+            @pl.when((k > 0) | (h != me))
+            def _():
+                unit_copy(k, h).wait_send()
+
+    @pl.when(me < 4)
+    def _():
+        own_grad().wait()
+
 
     tile_copy.wait_recv()
     gate_wgrad[...] += tile_z[:, :width].astype(F32)
@@ -851,7 +900,6 @@
     down = down_sum[...] + tile_z[:, 2 * width :].astype(F32)
     for i in range(width // HD):
         down_wgrad[i * HD : (i + 1) * HD, :] = down[:, i * HD : (i + 1) * HD].T
-    own_grad.wait()
     part_finish()
     value = middle[...] + part[:ROWS, :].astype(F32)
     for i in range(2):
@@ -882,16 +930,17 @@
             jax.ShapeDtypeStruct((width, rows), F32),
             jax.ShapeDtypeStruct((16 * rows, HD), BF16),
             jax.ShapeDtypeStruct((4 * rows, 4 * HD), BF16),
+            jax.ShapeDtypeStruct((rows, model), BF16),
             half,
-            half,
+            jax.ShapeDtypeStruct((16 * HD, model), BF16),
         ),
         in_specs=[vmem] * 3 + [anywhere] * 7,
-        out_specs=(vmem,) * 6 + (anywhere,) * 4,
+        out_specs=(vmem,) * 6 + (anywhere,) * 2 + (vmem,) + (anywhere,) * 2,
         scratch_shapes=[
             low((4 * rows, 4 * HD)),
             low((2 * HD, model)),
             low((2 * HD, model)),
-            low((2 * rows, model)),
+            low((3 * rows, model)),
             low((2 * rows, model)),
             low((8 * rows, model)),
             low((8 * rows, model)),
@@ -912,8 +961,7 @@
             low((2, 2, rows, 3 * width)),
             low((rows, 3 * width)),
             pltpu.VMEM((rows, width), F32),
-            low((4 * rows, model)),
-            low((4 * rows, 4 * HD)),
+            low((rows, 16 * HD)),
             dma((6,)),
             dma((16,)),
             dma((16,)),
@@ -933,8 +981,12 @@
             dma((4,)),
             dma((6,)),
             dma((6,)),
-            dma((4,)),
-            dma((4,)),
+            dma((2, 4)),
+            dma((2, 4)),
+            dma((3, 3, 2)),
+            dma((3, 3, 2)),
+            dma((3, 2)),
+            dma((3, 2)),
             dma((16,)),
             dma((16,)),
             dma((4,)),
@@ -945,6 +997,7 @@
             dma,
             dma((3,)),
             dma((2,)),
+            dma((3,)),
         ],
         compiler_params=pltpu.CompilerParams(
             collective_id=1, has_side_effects=True, vmem_limit_bytes=63 * 2**20
@@ -957,13 +1010,15 @@
 
 
 def back_kernel(
-    q_grad, keep, send, raw, cos, sin, q_gain, k_gain, tokens, middle_grad, attn_gain, mlp_gain_grad,
-    middle, normed_hbm, own_hbm, par_hbm, branch_hbm, att_hbm, part_hbm,
+    place, stored, doc_lengths, log_total, cos, sin, q_gain, k_gain, attn_gain, mlp_gain_grad,
+    grad_hbm, q_pos_hbm, k_pos_hbm, v_pos_hbm, part_hbm, branch_hbm, att_hbm, raw_hbm, normed_hbm, own_hbm, par_hbm,
+    middle_hbm, tokens_hbm, middle_grad_hbm,
     tokens_grad, out_rows, q_wgrad, k_wgrad, v_wgrad, o_wgrad, attn_total, mlp_total, q_total, k_total,
+    grad_in, q_pos, k_pos, v_pos, grad_pos, q_acc, q_grad, send, k_acc, v_acc, keep, raw, middle, tokens, middle_grad,
     normed, w_own, w_par, branch_all, att, part, out_got, relay, out_across, swap_got, kv_out, q_got, kv_got, low, parts, y_got,
     core_out, core_got, red, x_relay, x_got, z_out, z_low, z_got, o_core_out, o_core_got, o_red, o_x_relay, o_x_got, o_z_out, o_z_low, o_z_got,
-    g_out, g_got,
-    load_sem, swap_sem, across_sem, q_sent, q_land, kv_sent, kv_land, y_sent, y_land, out_sent, out_land,
+    g_out, g_got, by_gain,
+    load_sem, swap_sem, across_sem, q_sent, q_land, kv_sent, kv_land, y_sent, y_land, out_sent, out_land, branch_sent, branch_land,
     core_sent, core_land, x_sent, x_land, z_sent, z_land, g_sent, g_land,
 ):
     zl, x, core = (lax.axis_index(a) for a in CTX)
@@ -988,47 +1043,29 @@
         for i, (src, dst) in enumerate(
             (
                 (part_hbm, part),
-                (branch_hbm, branch_all),
+                (grad_hbm, grad_in),
+                (q_pos_hbm, q_pos),
+                (k_pos_hbm, k_pos),
+                (v_pos_hbm, v_pos),
+                (branch_hbm, branch_all.at[pl.ds(0, ROWS), :]),
                 (att_hbm, att),
                 (normed_hbm, normed),
+                (raw_hbm, raw),
                 (own_hbm, w_own),
                 (par_hbm, w_par),
+                (middle_hbm, middle),
+                (tokens_hbm, tokens),
+                (middle_grad_hbm, middle_grad),
             )
         )
     ]
     for load in loads:
         load.start()
     peers([along_ctx(k) for k in range(1, 16)] + [along_y(k) for k in (1, 2, 3)] + [zs[2], zs[3]])
-
-    swap = remote(send, swap_got, swap_sem.at[0], swap_sem.at[1], other_core)
-    swap.start()
-
-    waits = [swap]
-
-    def to_rows(src, dst, sent, landed):
-        copies = []
-        for k in range(1, 16):
-            copy = remote(block(src, lax.rem(me + k, 16)), block(dst, 16 - k), sent.at[k], landed.at[16 - k], along_ctx(k))
-            copy.start()
-            copies.append(copy)
-        waits.extend(copies)
-        return copies
-
-    q_copies = to_rows(q_grad, q_got, q_sent, q_land)
-    mine = pl.ds(pl.multiple_of(me * ROWS, ROWS), ROWS)
-    q_got[:ROWS, :] = q_grad[mine, :]
-    swap.wait_recv()
-    kv_out[...] = (keep[...] + swap_got[...].astype(F32)).astype(BF16)
-    kv_copies = to_rows(kv_out, kv_got, kv_sent, kv_land)
-    kv_got[:ROWS, :] = kv_out[mine, :]
-
-    loads[0].wait()
-    out_pass, out_finish = scatter_ring(
-        row_slots(part),
-        lambda h: relay.at[pl.ds(h * (ROWS // 2), ROWS // 2), :],
-        lambda r, h: row_slots(out_got)(r, h),
-        along_y, out_sent, out_land, waits,
-    )
+    waits = []
+
+    loads[5].wait()
+    branch_pass, branch_finish = gather_ring(row_slots(branch_all), along_y, branch_sent, branch_land, waits)
 
     def grad_stages(first, tile, to_other, from_other, summed, x_relay, from_x, total, total_low, from_z):
         n = total.shape[2] // 2
@@ -1100,16 +1137,61 @@
     o_cores, o_x, o_z, o_finish = grad_stages(
         1, tile_of(branch_all, att), o_core_out, o_core_got, o_red, o_x_relay, o_x_got, o_z_out, o_z_low, o_z_got
     )
-    loads[1].wait()
-    loads[2].wait()
+    for load in loads[:5] + loads[6:7]:
+        load.wait()
+
+    blocks = q_pos.shape[0] // BLK
+    ordered(stored, blocks, ((grad_in, grad_pos),))
+    ends = document_ends(doc_lengths, zh * 4 + lax.rem(y + me // 4, 4))
+    attend_back(ends, q_pos, k_pos, v_pos, log_total, grad_pos, q_acc, k_acc, v_acc)
+    ordered(place, blocks, ((q_acc, q_grad),))
+
+    @pl.loop(0, blocks)
+    def _(b):
+        dst_rows = pl.ds(pl.multiple_of(b * BLK, BLK), BLK)
+        k_rows = k_acc[place[b]] * HD ** (-0.5)
+        v_rows = v_acc[place[b]]
+        keep[dst_rows, :] = jnp.where(core == 0, k_rows, v_rows)
+        send[dst_rows, :] = jnp.where(core == 0, v_rows, k_rows).astype(BF16)
+
+    swap = remote(send, swap_got, swap_sem.at[0], swap_sem.at[1], other_core)
+    swap.start()
+
+    waits.append(swap)
+
+    def to_rows(src, dst, sent, landed):
+        copies = []
+        for k in range(1, 16):
+            copy = remote(block(src, lax.rem(me + k, 16)), block(dst, 16 - k), sent.at[k], landed.at[16 - k], along_ctx(k))
+            copy.start()
+            copies.append(copy)
+        waits.extend(copies)
+        return copies
+
+    q_copies = to_rows(q_grad, q_got, q_sent, q_land)
+    mine = pl.ds(pl.multiple_of(me * ROWS, ROWS), ROWS)
+    q_got[:ROWS, :] = q_grad[mine, :]
+    branch_pass()
+    out_pass, out_finish = scatter_ring(
+        row_slots(part),
+        lambda h: relay.at[pl.ds(h * (ROWS // 2), ROWS // 2), :],
+        lambda r, h: row_slots(out_got)(r, h),
+        along_y, out_sent, out_land, waits,
+    )
+    swap.wait_recv()
+    kv_out[...] = (keep[...] + swap_got[...].astype(F32)).astype(BF16)
+    kv_copies = to_rows(kv_out, kv_got, kv_sent, kv_land)
+    kv_got[:ROWS, :] = kv_out[mine, :]
+
+    branch_finish()
     o_x_pass, o_x_finish = o_x(o_cores())
-    out_pass()
-    for load in loads[3:]:
+    for load in loads[7:]:
         load.wait()
     for copy in q_copies:
         copy.wait_recv()
     for copy in kv_copies:
         copy.wait_recv()
+    out_pass()
 
     g_out[0] = jnp.zeros_like(g_out[0])
 
@@ -1157,7 +1239,11 @@
         total = dot(low[:, :half], w_own[cols, :], ((1,), (1,)))
         total += dot(low[:, half:], w_par[cols, :], ((1,), (1,)))
         parts[:, cols] = total.astype(BF16)
-
+        by_gain[:, cols] = jnp.sum(total * normed[:, cols].astype(F32), axis=0, keepdims=True) / attn_gain[:, cols]
+
+    for i in range(16):
+        g_out[0, i : i + 1, :] = by_gain[:, i * HD : (i + 1) * HD]
+        g_out[0, 16 + i : 17 + i, :] = mlp_gain_grad[:, i * HD : (i + 1) * HD]
     o_x_pass()
     y_pass, y_finish = scatter_ring(
         row_slots(parts),
@@ -1165,23 +1251,6 @@
         lambda r, h: row_slots(y_got)(r, h),
         along_y, y_sent, y_land, waits,
     )
-
-    x_pass, x_finish = qkv_x(core_copy)
-    y_pass()
-    x_pass()
-    o_z_copies = o_z(o_x_finish)
-
-    across_copy.wait_recv()
-    out_rows[...] = (middle[...] + out_across[...].astype(F32)).astype(BF16)
-    y_finish()
-    grad = parts[:ROWS, :].astype(F32)
-    for i in range(2):
-        grad += y_got[i * ROWS : (i + 1) * ROWS, :].astype(F32)
-    rows_back, gain_sum = rms_back(grad, tokens[...].astype(F32), attn_gain[...])
-    tokens_grad[...] = (middle_grad[...] + rows_back).astype(BF16)
-    for i in range(16):
-        g_out[0, i : i + 1, :] = gain_sum[:, i * HD : (i + 1) * HD]
-        g_out[0, 16 + i : 17 + i, :] = mlp_gain_grad[:, i * HD : (i + 1) * HD]
 
     def gain_stage(stage, places):
         copies = []
@@ -1204,33 +1273,45 @@
         return total
 
     copies = gain_stage(0, [(along_y(k), 3 - k) for k in (1, 2, 3)])
-
-    z_copies = qkv_z(x_finish)
-    value = o_finish(o_z_copies)
-    for i in range(2):
-        o_wgrad[i * HD : (i + 1) * HD, :] = value[:, i * HD : (i + 1) * HD].T
+    x_pass, x_finish = qkv_x(core_copy)
     g_out[1] = gain_sum_of(0, copies)
     copies = gain_stage(1, [(along_x(k), 3 - k) for k in (1, 2, 3)])
+    y_pass()
+    x_pass()
     g_out[2] = gain_sum_of(1, copies)
     copies = gain_stage(2, [(zs[d], d - 1) for d in (1, 2, 3)])
-    value = qkv_finish(z_copies)
-    q_wgrad[...] = value[:, : 2 * HD]
-    k_wgrad[...] = value[:, 2 * HD : 3 * HD]
-    v_wgrad[...] = value[:, 3 * HD :]
+    o_z_copies = o_z(o_x_finish)
+    across_copy.wait_recv()
+    out_rows[...] = (middle[...] + out_across[...].astype(F32)).astype(BF16)
     g_out[3] = gain_sum_of(2, copies)
     copies = gain_stage(3, [(other_core, 0)])
+    z_copies = qkv_z(x_finish)
     gains = gain_sum_of(3, copies)
     for i in range(16):
         attn_total[:, i * HD : (i + 1) * HD] = gains[i : i + 1, :]
         mlp_total[:, i * HD : (i + 1) * HD] = gains[16 + i : 17 + i, :]
     q_total[...] = gains[32:33, :]
     k_total[...] = gains[33:34, :]
+
+    y_finish()
+    grad = parts[:ROWS, :].astype(F32)
+    for i in range(2):
+        grad += y_got[i * ROWS : (i + 1) * ROWS, :].astype(F32)
+    rows_back, _ = rms_back(grad, tokens[...].astype(F32), attn_gain[...])
+    tokens_grad[...] = (middle_grad[...] + rows_back).astype(BF16)
+    value = qkv_finish(z_copies)
+    q_wgrad[...] = value[:, : 2 * HD]
+    k_wgrad[...] = value[:, 2 * HD : 3 * HD]
+    v_wgrad[...] = value[:, 3 * HD :]
+    value = o_finish(o_z_copies)
+    for i in range(2):
+        o_wgrad[i * HD : (i + 1) * HD, :] = value[:, i * HD : (i + 1) * HD].T
     for copy in waits:
         copy.wait_send()
 
 
-def back(q_grad, keep, send, raw, cos, sin, q_gain, k_gain, tokens, middle_grad, attn_gain, mlp_gain_grad,
-         middle, normed, w_own, w_par, branch_all, att, part):
+def back(place, stored, doc_lengths, log_total, cos, sin, q_gain, k_gain, attn_gain, mlp_gain_grad, grad_in, q_pos, k_pos,
+         v_pos, part, branch, att, raw, normed, w_own, w_par, middle, tokens, middle_grad):
     rows, model = tokens.shape
     wide = raw.shape[1]
     anywhere = pl.BlockSpec(memory_space=pl.ANY)
@@ -1250,9 +1331,19 @@
             jax.ShapeDtypeStruct((1, HD), F32),
             jax.ShapeDtypeStruct((1, HD), F32),
         ),
-        in_specs=[vmem] * 13 + [anywhere] * 6,
+        in_specs=[pl.BlockSpec(memory_space=pltpu.SMEM)] * 3 + [vmem] * 7 + [anywhere] * 14,
         out_specs=(vmem,) * 10,
-        scratch_shapes=[
+        scratch_shapes=[pltpu.VMEM((16 * rows // BLK, BLK, HD), BF16)]
+        + [pltpu.VMEM((16 * rows, HD), BF16)] * 4
+        + [pltpu.VMEM((16 * rows // BLK, BLK, HD), BF16)]
+        + [pltpu.VMEM((16 * rows, HD), BF16)] * 2
+        + [pltpu.VMEM((16 * rows // BLK, BLK, HD), F32)] * 2
+        + [pltpu.VMEM((16 * rows, HD), F32)]
+        + [
+            pltpu.VMEM((4 * rows, wide), F32),
+            pltpu.VMEM((rows, model), F32),
+            pltpu.VMEM((rows, model), BF16),
+            pltpu.VMEM((rows, model), F32),
             pltpu.VMEM((4 * rows, model), BF16),
             pltpu.VMEM((model, wide // 2), BF16),
             pltpu.VMEM((model, wide // 2), BF16),
@@ -1287,7 +1378,8 @@
             pltpu.VMEM((3, rows, 2 * HD), BF16),
             pltpu.VMEM((4, 40, HD), F32),
             pltpu.VMEM((4, 3, 40, HD), F32),
-            dma((6,)),
+            pltpu.VMEM((1, model), F32),
+            dma((14,)),
             dma((2,)),
             dma((2,)),
             dma((16,)),
@@ -1298,6 +1390,8 @@
             dma((6,)),
             dma((6,)),
             dma((6,)),
+            dma((4,)),
+            dma((4,)),
             dma((2,)),
             dma((2,)),
             dma((2, 6)),
@@ -1308,15 +1402,15 @@
             dma((12,)),
         ],
         compiler_params=pltpu.CompilerParams(
-            collective_id=2, has_side_effects=True, vmem_limit_bytes=58 * 2**20
+            collective_id=2, has_side_effects=True, vmem_limit_bytes=62 * 2**20
         ),
         cost_estimate=pl.CostEstimate(
             flops=4 * 4 * rows * model * wide, bytes_accessed=24 * 2**20, transcendentals=0
         ),
         name="back",
     )(
-        q_grad, keep, send, raw, cos, sin, q_gain, k_gain, tokens, middle_grad, attn_gain, mlp_gain_grad,
-        middle, normed, w_own, w_par, branch_all, att, part,
+        place, stored, doc_lengths, log_total, cos, sin, q_gain, k_gain, attn_gain, mlp_gain_grad,
+        grad_in.reshape(-1, BLK, HD), q_pos, k_pos, v_pos, part, branch, att, raw, normed, w_own, w_par, middle, tokens, middle_grad,
     )
 
 
@@ -1339,12 +1433,9 @@
 ):
     rows = tokens.shape[1]
     zl, x, core = (lax.axis_index(a) for a in CTX)
-    zh, y = (lax.axis_index(a) for a in FSDP)
     ctx_place = zl * 8 + x * 2 + core
-    sequence = zh * 4 + lax.rem(y + ctx_place // 4, 4)
-    ends = jnp.cumsum(lax.dynamic_index_in_dim(doc_lengths, sequence, 0, keepdims=False))
-    ends = ends.astype(jnp.int32)
-    core_flag = core.astype(jnp.int32).reshape(1)
+    numbers = jnp.arange(block_place.shape[0], dtype=jnp.int32)
+    stored = jnp.sum(jnp.where(block_place[None, :] == numbers[:, None], numbers[None, :], 0), axis=1, dtype=jnp.int32)
     own_blocks = lax.dynamic_slice_in_dim(block_place, ctx_place * (rows // BLK), rows // BLK)
     own_positions = (own_blocks[:, None] * BLK + jnp.arange(BLK, dtype=jnp.int32)[None, :]).reshape(-1)
     cos_rows, sin_rows = tables(own_positions, HD)
@@ -1352,21 +1443,18 @@
     attn_gain, mlp_gain = attn_gain.reshape(1, -1), mlp_gain.reshape(1, -1)
     cot = cotangent[0]
 
-    q_in, mine, other, raw, normed, w_own, w_par, o_par, cot_half = pre(
-        tokens[0], cos_rows, sin_rows, attn_gain, q_gain, k_gain, cot, q_weight, k_weight, v_weight, o_weight
+    log_total, out, q_pos, k_pos, v_pos, raw, normed, w_own, w_par, o_par, cot_half = pre(
+        block_place, stored, doc_lengths, tokens[0], cos_rows, sin_rows, attn_gain, q_gain, k_gain, cot, q_weight, k_weight,
+        v_weight, o_weight,
     )
-    out, q_pos, k_pos, v_pos, log_total = attend(block_place, ends, core_flag, q_in, mine, other)
     (
-        middle, middle_grad, mlp_gain_grad, gate_wgrad, up_wgrad, down_wgrad, grad_in, att, branch_all, part,
+        middle, middle_grad, mlp_gain_grad, gate_wgrad, up_wgrad, down_wgrad, grad_in, att, branch, part, _,
     ) = middle_part(tokens[0], cot, mlp_gain, out, o_weight, o_par, cot_half, gate_weight, up_weight, down_weight)
-    q_grad, keep_grad, send_grad = attend_back(
-        block_place, ends, core_flag, grad_in, q_pos, k_pos, v_pos, log_total
-    )
     (
         tokens_grad, out_rows, q_wgrad, k_wgrad, v_wgrad, o_wgrad, attn_gain_grad, mlp_gain_grad, q_gain_grad, k_gain_grad,
     ) = back(
-        q_grad, keep_grad, send_grad, raw, cos_rows, sin_rows, q_gain, k_gain, tokens[0], middle_grad, attn_gain,
-        mlp_gain_grad, middle, normed, w_own, w_par, branch_all, att, part,
+        block_place, stored, doc_lengths, log_total, cos_rows, sin_rows, q_gain, k_gain, attn_gain, mlp_gain_grad, grad_in,
+        q_pos, k_pos, v_pos, part, branch, att, raw, normed, w_own, w_par, middle, tokens[0], middle_grad,
     )
     return (
         out_rows[None],

time: 349 us -> 334 us (0.957)
  the two profiles are of different devices: /device:TPU:1 before, /device:TPU:0 now
where the time goes in v5:
time: 334 us; the launch traced here: 328 us
  Pallas kernels  311 us (93%)
  local copies, waits for them, and re-layouts  12.4 us (4%)
    pallas_call x1, Pallas kernels, middle_part(): pl.pallas_call(middle_kernel, out_shape=(jax.ShapeDtypeStruct((rows, mode...  173 us
    pallas_call x1, Pallas kernels, back(): pl.pallas_call(back_kernel, out_shape=(jax.ShapeDtypeStruct((rows, model)...  80.4 us
    pallas_call x1, Pallas kernels, pre(): pl.pallas_call(pre_kernel, out_shape=(jax.ShapeDtypeStruct((16 * rows, 1)...  57.9 us
    unnamed x36, local copies, waits for them, and re-layouts  12.3 us

profile of v5, /device:TPU:0, one launch (start us, length us, event | category | flops | bytes accessed | tf_op | source)
XLA Modules:
  0.0 327.6 jit_solution(9693835516339781751)
XLA Ops:
  0.7 0.7 dynamic-slice_multiply_fusion
  1.4 1.3 select_reduce_fusion.stored
  2.7 0.1 add_convert_fusion
  2.7 0.1 convert_element_type.18
  2.8 1.4 copy.31.doc_lengths
  4.2 0.1 broadcast_multiply_fusion
  4.3 1.0 fusion
  5.2 57.9 %pre.1 = (f32[2048,1]{1,0:T(8,128)}, bf16[2048,128]{1,0:T(8,128)(2,1)}, bf16[2048,128]{1,0:T(8,128)(2,1)}, bf16[2048,128]{1,0:T(8,128)(2,1)}, bf16[2048,128]{1,0...) custom-call(s32[32]{0:T(128)} %place.3, ...), custom_call_target="tpu_custom_call" | custom-call | flops 2147483648 | bytes 25165824 | tf_op jit(solution)/shard_map/pre/pallas_call | solution.py:414
  63.2 172.7 %middle.1 = (f32[128,2048]{1,0:T(8,128)}, f32[128,2048]{1,0:T(8,128)}, f32[1,2048]{1,0:T(1,128)}, f32[128,768]{1,0:T(8,128)}, f32[128,768]{1,0:T(8,128)}, /*inde...) custom-call(bf16[128,2048]{1,0:T(8,128)(2,1)} %bitcast.14, ...), custom_call_target="tpu_custom_call" | custom-call | flops 28991029248 | bytes 41943040 | tf_op jit(solution)/shard_map/middle/pallas_call | solution.py:922
  235.9 80.4 %back.1 = (bf16[128,2048]{1,0:T(8,128)(2,1)}, bf16[128,2048]{1,0:T(8,128)(2,1)}, f32[128,256]{1,0:T(8,128)}, f32[128,128]{1,0:T(8,128)}, f32[128,128]{1,0:T(8,12...) custom-call(s32[32]{0:T(128)} %place.3, ...), custom_call_target="tpu_custom_call" | custom-call | flops 4294967296 | bytes 25165824 | tf_op jit(solution)/shard_map/back/pallas_call | solution.py:1320
  316.4 2.0 copy.45
  318.4 1.9 copy.46
  320.3 0.6 copy.47
  320.9 0.0 copy-done.4
  320.9 0.7 copy.48
  321.6 0.6 copy.49
  322.2 0.6 copy.50
  322.8 0.5 copy.51
  323.4 0.5 copy.52
  323.9 0.7 copy.53
  324.5 0.6 copy.54
  325.1 0.7 copy.55
  325.9 0.7 copy.56
  326.6 0.7 copy.57
  (22 shorter events, 0.1 us)
Async XLA Ops:
  316.3 4.0 %copy-start.8 = (f32[1,2048]{1,0:T(1,128)S(1)}, f32[1,2048]{1,0:T(1,128)}, u32[]{:S(2)}) copy-start(f32[1,2048]{1,0:T(1,128)} %get-tuple-element.64) | copy-start | bytes 24580
  316.3 4.6 %copy-start.4 = (f32[128,256]{1,0:T(8,128)S(1)}, f32[128,256]{1,0:T(8,128)}, u32[]{:S(2)}) copy-start(f32[128,256]{1,0:T(8,128)} %get-tuple-element.93) | copy-start | bytes 393220
  316.3 5.3 %copy-start.6 = (f32[128,128]{1,0:T(8,128)S(1)}, f32[128,128]{1,0:T(8,128)}, u32[]{:S(2)}) copy-start(f32[128,128]{1,0:T(8,128)} %get-tuple-element.94) | copy-start | bytes 196612
  316.3 5.9 %copy-start.5 = (f32[128,128]{1,0:T(8,128)S(1)}, f32[128,128]{1,0:T(8,128)}, u32[]{:S(2)}) copy-start(f32[128,128]{1,0:T(8,128)} %get-tuple-element.95) | copy-start | bytes 196612
  316.3 6.5 %copy-start.10 = (f32[1,128]{1,0:T(1,128)S(1)}, f32[1,128]{1,0:T(1,128)}, u32[]{:S(2)}) copy-start(f32[1,128]{1,0:T(1,128)} %get-tuple-element.68) | copy-start | bytes 1540
  316.3 7.0 %copy-start.9 = (f32[1,128]{1,0:T(1,128)S(1)}, f32[1,128]{1,0:T(1,128)}, u32[]{:S(2)}) copy-start(f32[1,128]{1,0:T(1,128)} %get-tuple-element.69) | copy-start | bytes 1540
  316.3 7.5 %copy-start.3 = (f32[256,128]{1,0:T(8,128)S(1)}, f32[256,128]{1,0:T(8,128)}, u32[]{:S(2)}) copy-start(f32[256,128]{1,0:T(8,128)} %get-tuple-element.98) | copy-start | bytes 393220
  316.4 8.2 %copy-start.7 = (f32[1,2048]{1,0:T(1,128)S(1)}, f32[1,2048]{1,0:T(1,128)}, u32[]{:S(2)}) copy-start(f32[1,2048]{1,0:T(1,128)} %get-tuple-element.71) | copy-start | bytes 24580
  316.4 8.8 %copy-start.2 = (f32[128,768]{1,0:T(8,128)S(1)}, f32[128,768]{1,0:T(8,128)}, u32[]{:S(2)}) copy-start(f32[128,768]{1,0:T(8,128)} %get-tuple-element.100) | copy-start | bytes 1179652
  316.4 9.5 %copy-start.1 = (f32[128,768]{1,0:T(8,128)S(1)}, f32[128,768]{1,0:T(8,128)}, u32[]{:S(2)}) copy-start(f32[128,768]{1,0:T(8,128)} %get-tuple-element.101) | copy-start | bytes 1179652
  316.4 10.2 %copy-start = (f32[768,128]{1,0:T(8,128)S(1)}, f32[768,128]{1,0:T(8,128)}, u32[]{:S(2)}) copy-start(f32[768,128]{1,0:T(8,128)} %get-tuple-element.102) | copy-start | bytes 1179652

commit v6 on v5

--- a/solution.py
+++ b/solution.py
@@ -1015,8 +1015,8 @@
     middle_hbm, tokens_hbm, middle_grad_hbm,
     tokens_grad, out_rows, q_wgrad, k_wgrad, v_wgrad, o_wgrad, attn_total, mlp_total, q_total, k_total,
     grad_in, q_pos, k_pos, v_pos, grad_pos, q_acc, q_grad, send, k_acc, v_acc, keep, raw, middle, tokens, middle_grad,
-    normed, w_own, w_par, branch_all, att, part, out_got, relay, out_across, swap_got, kv_out, q_got, kv_got, low, parts, y_got,
-    core_out, core_got, red, x_relay, x_got, z_out, z_low, z_got, o_core_out, o_core_got, o_red, o_x_relay, o_x_got, o_z_out, o_z_low, o_z_got,
+    normed, w_own, w_par, branch_all, att, part, out_got, relay, out_across, swap_got, kv_out, q_got, kv_got, low_q, low_kv, parts, y_got,
+    q_bufs, kv_bufs, o_bufs,
     g_out, g_got, by_gain,
     load_sem, swap_sem, across_sem, q_sent, q_land, kv_sent, kv_land, y_sent, y_land, out_sent, out_land, branch_sent, branch_land,
     core_sent, core_land, x_sent, x_land, z_sent, z_land, g_sent, g_land,
@@ -1131,12 +1131,9 @@
 
         return tile
 
-    qkv_cores, qkv_x, qkv_z, qkv_finish = grad_stages(
-        0, tile_of(normed, low), core_out, core_got, red, x_relay, x_got, z_out, z_low, z_got
-    )
-    o_cores, o_x, o_z, o_finish = grad_stages(
-        1, tile_of(branch_all, att), o_core_out, o_core_got, o_red, o_x_relay, o_x_got, o_z_out, o_z_low, o_z_got
-    )
+    q_cores, q_x, q_z, q_finish = grad_stages(0, tile_of(normed, low_q), *q_bufs)
+    kv_cores, kv_x, kv_z, kv_finish = grad_stages(1, tile_of(normed, low_kv), *kv_bufs)
+    o_cores, o_x, o_z, o_finish = grad_stages(2, tile_of(branch_all, att), *o_bufs)
     for load in loads[:5] + loads[6:7]:
         load.wait()
 
@@ -1183,15 +1180,10 @@
     kv_copies = to_rows(kv_out, kv_got, kv_sent, kv_land)
     kv_got[:ROWS, :] = kv_out[mine, :]
 
-    branch_finish()
-    o_x_pass, o_x_finish = o_x(o_cores())
     for load in loads[7:]:
         load.wait()
     for copy in q_copies:
         copy.wait_recv()
-    for copy in kv_copies:
-        copy.wait_recv()
-    out_pass()
 
     g_out[0] = jnp.zeros_like(g_out[0])
 
@@ -1209,42 +1201,44 @@
         rows = pl.ds(pl.multiple_of(s * ROWS, ROWS), ROWS)
         for h in range(4):
             at = (h // 2) * half + (h % 2) * HD
-            cols = slice(at, at + HD)
             grad = from_unit(q_got, s * 4 + h).astype(F32)
-            back, gain_sum = head_back(grad, raw[rows, cols], q_gain[...])
-            low[rows, cols] = back
+            back, gain_sum = head_back(grad, raw[rows, at : at + HD], q_gain[...])
+            low_q[rows, h * HD : (h + 1) * HD] = back
             g_out[0, 32:33, :] += gain_sum
+
+    q_core_copy = q_cores()
+    branch_finish()
+    o_core_copy = o_cores()
+    for copy in kv_copies:
+        copy.wait_recv()
+
+    @pl.loop(0, 4)
+    def _(s):
+        rows = pl.ds(pl.multiple_of(s * ROWS, ROWS), ROWS)
         for kv in range(2):
             at = kv * half + 2 * HD
-            cols = slice(at, at + HD)
             grad = from_unit(kv_got, s * 4 + kv * 2).astype(F32)
-            back, gain_sum = head_back(grad, raw[rows, cols], k_gain[...])
-            low[rows, cols] = back
+            back, gain_sum = head_back(grad, raw[rows, at : at + HD], k_gain[...])
+            low_kv[rows, kv * 2 * HD : (kv * 2 + 1) * HD] = back
             g_out[0, 33:34, :] += gain_sum
-            low[rows, at + HD : at + 2 * HD] = from_unit(kv_got, s * 4 + kv * 2 + 1)
-
-    core_copy = qkv_cores()
-    out_finish()
-    value = part[:ROWS, :].astype(F32)
-    for i in range(2):
-        value += out_got[i * ROWS : (i + 1) * ROWS, :].astype(F32)
-    part[:ROWS, :] = value.astype(BF16)
-    across_copy = remote(part.at[pl.ds(0, ROWS), :], out_across, across_sem.at[0], across_sem.at[1], zs[2])
-    across_copy.start()
-    waits.append(across_copy)
-
+            low_kv[rows, (kv * 2 + 1) * HD : (kv * 2 + 2) * HD] = from_unit(kv_got, s * 4 + kv * 2 + 1)
+
+    kv_core_copy = kv_cores()
+    out_pass()
+    q_x_pass, q_x_finish = q_x(q_core_copy)
     @pl.loop(0, parts.shape[1] // WIDE)
     def _(n):
         cols = pl.ds(pl.multiple_of(n * WIDE, WIDE), WIDE)
-        total = dot(low[:, :half], w_own[cols, :], ((1,), (1,)))
-        total += dot(low[:, half:], w_par[cols, :], ((1,), (1,)))
+        total = dot(low_q[:, : half // 2], w_own[cols, : half // 2], ((1,), (1,)))
+        total += dot(low_q[:, half // 2 :], w_par[cols, : half // 2], ((1,), (1,)))
+        total += dot(low_kv[:, : half // 2], w_own[cols, half // 2 :], ((1,), (1,)))
+        total += dot(low_kv[:, half // 2 :], w_par[cols, half // 2 :], ((1,), (1,)))
         parts[:, cols] = total.astype(BF16)
         by_gain[:, cols] = jnp.sum(total * normed[:, cols].astype(F32), axis=0, keepdims=True) / attn_gain[:, cols]
 
     for i in range(16):
         g_out[0, i : i + 1, :] = by_gain[:, i * HD : (i + 1) * HD]
         g_out[0, 16 + i : 17 + i, :] = mlp_gain_grad[:, i * HD : (i + 1) * HD]
-    o_x_pass()
     y_pass, y_finish = scatter_ring(
         row_slots(parts),
         lambda h: relay.at[pl.ds(ROWS + h * (ROWS // 2), ROWS // 2), :],
@@ -1273,41 +1267,68 @@
         return total
 
     copies = gain_stage(0, [(along_y(k), 3 - k) for k in (1, 2, 3)])
-    x_pass, x_finish = qkv_x(core_copy)
+    kv_x_pass, kv_x_finish = kv_x(kv_core_copy)
+    q_x_pass()
+    o_x_pass, o_x_finish = o_x(o_core_copy)
+    out_finish()
+    value = part[:ROWS, :].astype(F32)
+    for i in range(2):
+        value += out_got[i * ROWS : (i + 1) * ROWS, :].astype(F32)
+    part[:ROWS, :] = value.astype(BF16)
+    across_copy = remote(part.at[pl.ds(0, ROWS), :], out_across, across_sem.at[0], across_sem.at[1], zs[2])
+    across_copy.start()
+    waits.append(across_copy)
+    y_pass()
+    kv_x_pass()
     g_out[1] = gain_sum_of(0, copies)
     copies = gain_stage(1, [(along_x(k), 3 - k) for k in (1, 2, 3)])
-    y_pass()
-    x_pass()
+    o_x_pass()
+    q_z_copies = q_z(q_x_finish)
     g_out[2] = gain_sum_of(1, copies)
     copies = gain_stage(2, [(zs[d], d - 1) for d in (1, 2, 3)])
-    o_z_copies = o_z(o_x_finish)
     across_copy.wait_recv()
     out_rows[...] = (middle[...] + out_across[...].astype(F32)).astype(BF16)
+    kv_z_copies = kv_z(kv_x_finish)
+
+    y_finish()
+    grad = parts[:ROWS, :].astype(F32)
+    for i in range(2):
+        grad += y_got[i * ROWS : (i + 1) * ROWS, :].astype(F32)
+    rows_back, _ = rms_back(grad, tokens[...].astype(F32), attn_gain[...])
+    tokens_grad[...] = (middle_grad[...] + rows_back).astype(BF16)
     g_out[3] = gain_sum_of(2, copies)
     copies = gain_stage(3, [(other_core, 0)])
-    z_copies = qkv_z(x_finish)
+    o_z_copies = o_z(o_x_finish)
+    q_wgrad[...] = q_finish(q_z_copies)
+    value = kv_finish(kv_z_copies)
+    k_wgrad[...] = value[:, :HD]
+    v_wgrad[...] = value[:, HD:]
+    value = o_finish(o_z_copies)
+    for i in range(2):
+        o_wgrad[i * HD : (i + 1) * HD, :] = value[:, i * HD : (i + 1) * HD].T
     gains = gain_sum_of(3, copies)
     for i in range(16):
         attn_total[:, i * HD : (i + 1) * HD] = gains[i : i + 1, :]
         mlp_total[:, i * HD : (i + 1) * HD] = gains[16 + i : 17 + i, :]
     q_total[...] = gains[32:33, :]
     k_total[...] = gains[33:34, :]
-
-    y_finish()
-    grad = parts[:ROWS, :].astype(F32)
-    for i in range(2):
-        grad += y_got[i * ROWS : (i + 1) * ROWS, :].astype(F32)
-    rows_back, _ = rms_back(grad, tokens[...].astype(F32), attn_gain[...])
-    tokens_grad[...] = (middle_grad[...] + rows_back).astype(BF16)
-    value = qkv_finish(z_copies)
-    q_wgrad[...] = value[:, : 2 * HD]
-    k_wgrad[...] = value[:, 2 * HD : 3 * HD]
-    v_wgrad[...] = value[:, 3 * HD :]
-    value = o_finish(o_z_copies)
-    for i in range(2):
-        o_wgrad[i * HD : (i + 1) * HD, :] = value[:, i * HD : (i + 1) * HD].T
     for copy in waits:
         copy.wait_send()
+
+
+def stage_buffers(rows):
+    wide = 4 * HD
+    low = functools.partial(pltpu.VMEM, dtype=BF16)
+    return (
+        low((8, rows, wide)),
+        low((8, rows, wide)),
+        low((8, rows, wide)),
+        low((2, rows, wide)),
+        low((2, 2, rows, wide)),
+        pltpu.VMEM((2, rows, wide), F32),
+        low((2, rows, wide)),
+        low((3, rows, wide // 2)),
+    )
 
 
 def back(place, stored, doc_lengths, log_total, cos, sin, q_gain, k_gain, attn_gain, mlp_gain_grad, grad_in, q_pos, k_pos,
@@ -1357,25 +1378,13 @@
             pltpu.VMEM((16 * rows, HD), BF16),
             pltpu.VMEM((16 * rows, HD), BF16),
             pltpu.VMEM((16 * rows, HD), BF16),
-            pltpu.VMEM((4 * rows, wide), BF16),
+            pltpu.VMEM((4 * rows, wide // 2), BF16),
+            pltpu.VMEM((4 * rows, wide // 2), BF16),
             pltpu.VMEM((4 * rows, model), BF16),
             pltpu.VMEM((2 * rows, model), BF16),
-            pltpu.VMEM((8, rows, wide), BF16),
-            pltpu.VMEM((8, rows, wide), BF16),
-            pltpu.VMEM((8, rows, wide), BF16),
-            pltpu.VMEM((2, rows, wide), BF16),
-            pltpu.VMEM((2, 2, rows, wide), BF16),
-            pltpu.VMEM((2, rows, wide), F32),
-            pltpu.VMEM((2, rows, wide), BF16),
-            pltpu.VMEM((3, rows, wide // 2), BF16),
-            pltpu.VMEM((8, rows, 4 * HD), BF16),
-            pltpu.VMEM((8, rows, 4 * HD), BF16),
-            pltpu.VMEM((8, rows, 4 * HD), BF16),
-            pltpu.VMEM((2, rows, 4 * HD), BF16),
-            pltpu.VMEM((2, 2, rows, 4 * HD), BF16),
-            pltpu.VMEM((2, rows, 4 * HD), F32),
-            pltpu.VMEM((2, rows, 4 * HD), BF16),
-            pltpu.VMEM((3, rows, 2 * HD), BF16),
+            stage_buffers(rows),
+            stage_buffers(rows),
+            stage_buffers(rows),
             pltpu.VMEM((4, 40, HD), F32),
             pltpu.VMEM((4, 3, 40, HD), F32),
             pltpu.VMEM((1, model), F32),
@@ -1392,12 +1401,12 @@
             dma((6,)),
             dma((4,)),
             dma((4,)),
-            dma((2,)),
-            dma((2,)),
-            dma((2, 6)),
-            dma((2, 6)),
-            dma((6,)),
-            dma((6,)),
+            dma((3,)),
+            dma((3,)),
+            dma((3, 6)),
+            dma((3, 6)),
+            dma((9,)),
+            dma((9,)),
             dma((12,)),
             dma((12,)),
         ],
@@ -1412,6 +1421,33 @@
         place, stored, doc_lengths, log_total, cos, sin, q_gain, k_gain, attn_gain, mlp_gain_grad,
         grad_in.reshape(-1, BLK, HD), q_pos, k_pos, v_pos, part, branch, att, raw, normed, w_own, w_par, middle, tokens, middle_grad,
     )
+
+
+def results_kernel(*refs):
+    count = (len(refs) - 2) // 3
+    arrays, outs, held, (in_sem, out_sem) = refs[:count], refs[count : 2 * count], refs[2 * count : 3 * count], refs[-2:]
+    copies = [pltpu.make_async_copy(arrays[i], held[i], in_sem.at[i]) for i in range(count)]
+    for copy in copies:
+        copy.start()
+    for i in range(count):
+        copies[i].wait()
+        copies[i] = pltpu.make_async_copy(held[i], outs[i], out_sem.at[i])
+        copies[i].start()
+    for copy in copies:
+        copy.wait()
+
+
+def results(arrays):
+    anywhere = pl.BlockSpec(memory_space=pl.ANY)
+    return pl.pallas_call(
+        results_kernel,
+        out_shape=tuple(jax.ShapeDtypeStruct(a.shape, a.dtype) for a in arrays),
+        in_specs=[anywhere] * len(arrays),
+        out_specs=(anywhere,) * len(arrays),
+        scratch_shapes=[pltpu.VMEM(a.shape, a.dtype) for a in arrays] + [pltpu.SemaphoreType.DMA((len(arrays),))] * 2,
+        compiler_params=pltpu.CompilerParams(vmem_limit_bytes=62 * 2**20),
+        name="results",
+    )(*arrays)
 
 
 def per_device(
@@ -1455,6 +1491,15 @@
     ) = back(
         block_place, stored, doc_lengths, log_total, cos_rows, sin_rows, q_gain, k_gain, attn_gain, mlp_gain_grad, grad_in,
         q_pos, k_pos, v_pos, part, branch, att, raw, normed, w_own, w_par, middle, tokens[0], middle_grad,
+    )
+    (
+        out_rows, tokens_grad, attn_gain_grad, q_wgrad, k_wgrad, v_wgrad, q_gain_grad, k_gain_grad, o_wgrad, mlp_gain_grad,
+        gate_wgrad, up_wgrad, down_wgrad,
+    ) = results(
+        (
+            out_rows, tokens_grad, attn_gain_grad, q_wgrad, k_wgrad, v_wgrad, q_gain_grad, k_gain_grad, o_wgrad,
+            mlp_gain_grad, gate_wgrad, up_wgrad, down_wgrad,
+        )
     )
     return (
         out_rows[None],

time: 334 us -> 320 us (0.958)
  local copies, waits for them, and re-layouts: 12.4 us -> 1.44 us
    unnamed x36 -> x1, local copies, waits for them, and re-layouts: 12.3 us -> 1.35 us
    pallas_call x1, Pallas kernels: 80.4 us -> 75.9 us  [back(): pl.pallas_call(back_kernel, out_shape=(jax.ShapeDtypeStruct((rows, model)...]
where the time goes in v6:
time: 320 us; the launch traced here: 315 us
  Pallas kernels  309 us (97%)
    pallas_call x1, Pallas kernels, middle_part(): pl.pallas_call(middle_kernel, out_shape=(jax.ShapeDtypeStruct((rows, mode...  173 us
    pallas_call x1, Pallas kernels, back(): pl.pallas_call(back_kernel, out_shape=(jax.ShapeDtypeStruct((rows, model)...  75.9 us
    pallas_call x1, Pallas kernels, pre(): pl.pallas_call(pre_kernel, out_shape=(jax.ShapeDtypeStruct((16 * rows, 1)...  57.9 us

profile of v6, /device:TPU:0, one launch (start us, length us, event | category | flops | bytes accessed | tf_op | source)
XLA Modules:
  0.0 314.7 jit_solution(6922844263684466903)
XLA Ops:
  0.7 0.7 dynamic-slice_multiply_fusion
  1.4 1.3 select_reduce_fusion.stored
  2.7 0.1 add_convert_fusion
  2.7 0.1 convert_element_type.18
  2.8 1.4 copy.31.doc_lengths
  4.2 0.1 broadcast_multiply_fusion
  4.3 1.0 fusion
  5.2 57.9 %pre.1 = (f32[2048,1]{1,0:T(8,128)}, bf16[2048,128]{1,0:T(8,128)(2,1)}, bf16[2048,128]{1,0:T(8,128)(2,1)}, bf16[2048,128]{1,0:T(8,128)(2,1)}, bf16[2048,128]{1,0...) custom-call(s32[32]{0:T(128)} %place.3, ...), custom_call_target="tpu_custom_call" | custom-call | flops 2147483648 | bytes 25165824 | tf_op jit(solution)/shard_map/pre/pallas_call | solution.py:414
  63.2 172.6 %middle.1 = (f32[128,2048]{1,0:T(8,128)}, f32[128,2048]{1,0:T(8,128)}, f32[1,2048]{1,0:T(1,128)}, f32[128,768]{1,0:T(8,128)}, f32[128,768]{1,0:T(8,128)}, /*inde...) custom-call(bf16[128,2048]{1,0:T(8,128)(2,1)} %bitcast.14, ...), custom_call_target="tpu_custom_call" | custom-call | flops 28991029248 | bytes 41943040 | tf_op jit(solution)/shard_map/middle/pallas_call | solution.py:922
  235.8 75.9 %back.1 = (bf16[128,2048]{1,0:T(8,128)(2,1)}, bf16[128,2048]{1,0:T(8,128)(2,1)}, f32[128,256]{1,0:T(8,128)}, f32[128,128]{1,0:T(8,128)}, f32[128,128]{1,0:T(8,12...) custom-call(s32[32]{0:T(128)} %place.3, ...), custom_call_target="tpu_custom_call" | custom-call | flops 4294967296 | bytes 25165824 | tf_op jit(solution)/shard_map/back/pallas_call | solution.py:1341
  311.6 2.8 results.1
  (1 shorter events, 0.0 us)
